TPU v7x, 32 devices: a whole 2x2x4 slice. The times are simulated.
32 devices in a mesh: dp: 8 (over z, y), bn: 4 (over x, core).
Axes of the slice: x: 2, y: 2, z: 4, core: 2. Of those that a mesh axis runs over, the one named last changes fastest.
Arguments:
- key_feats: bfloat16 [256, 12, 16, 2048], P(('dp', 'bn')), may hold values from -22 to 22
- clip_starts: int32 [256], P(('dp', 'bn')), may hold values from 0 to 4
- shuffle: int32 [4, 8], P('bn'), may hold values from 0 to 7, each once within a row
- query_feats: bfloat16 [256, 2048], P(('dp', 'bn')), may hold values from -6 to 6
- conv_time: bfloat16 [3, 2048, 512], replicated, may hold values from -0.078125 to 0.078125
- conv_space: bfloat16 [9, 512, 512], replicated, may hold values from -0.09375 to 0.09375
- conv_expand: bfloat16 [512, 2048], replicated, may hold values from -0.25 to 0.25
- gain_one: float32 [512], replicated, may hold values from 0.25 to 1.75
- shift_one: float32 [512], replicated, may hold values from -3 to 3
- gain_two: float32 [512], replicated, may hold values from 0.25 to 1.75
- shift_two: float32 [512], replicated, may hold values from -3 to 3
- gain_three: float32 [2048], replicated, may hold values from 0.25 to 1.75
- shift_three: float32 [2048], replicated, may hold values from -3 to 3
- w_key: bfloat16 [2048, 128], replicated, may hold values from -0.125 to 0.125
- w_query: bfloat16 [2048, 128], replicated, may hold values from -0.125 to 0.125
- queue: bfloat16 [16384, 128], replicated, may hold values from -6 to 6
Outputs:
- keys: bfloat16 [256, 128], P(('dp', 'bn'))
- query_grad: float32 [2048, 128], replicated
Inputs may be any that keep to these rules, and one draw needn't show every extreme that they name: `shuffle`: each row is a permutation of 0 to 7.
All inputs are finite; a program needn't handle non-finite values.
Results may differ from a plain program's by a relative error of at most 0.0061.
Values may be sent and summed in bfloat16 or wider, within the bound.
No kernel may reach another device: no remote copies, remote signals or barrier semaphores. Data moves between devices by JAX's collectives and lax.ppermute only.
A program may use at most 128 MiB of HBM per device.

v0:
```python
import jax
import jax.numpy as jnp
from jax import lax
from jax.sharding import PartitionSpec as P

FRAMES = 8
SIDE = 4


SHARPNESS_DIVISOR = 0.2
EPSILON = 1e-05


def pick_frames(features, starts):

    def single(clip_feats, first_frame):
        return lax.dynamic_slice_in_dim(clip_feats, first_frame, FRAMES, 0)

    return jax.vmap(single)(features, starts)


def time_conv(values, weights):
    padded = jnp.pad(values, ((0, 0), (1, 1), (0, 0), (0, 0)))
    length = values.shape[1]
    summed = jnp.zeros(values.shape[:3] + (weights.shape[2],), jnp.float32)
    for offset in range(3):
        summed = summed + jnp.einsum(
            "afsc,cd->afsd",
            padded[:, offset : offset + length],
            weights[offset],
            preferred_element_type=jnp.float32,
        )
    return summed


def space_conv(values, weights):
    square_grid = values.reshape(values.shape[0], values.shape[1], SIDE, SIDE, values.shape[3])
    padded = jnp.pad(square_grid, ((0, 0), (0, 0), (1, 1), (1, 1), (0, 0)))
    summed = jnp.zeros(
        (values.shape[0], values.shape[1], SIDE, SIDE, weights.shape[2]), jnp.float32
    )
    for row_shift in range(3):
        for col_shift in range(3):
            window = padded[:, :, row_shift : row_shift + SIDE, col_shift : col_shift + SIDE]
            summed = summed + jnp.einsum(
                "afhwc,cd->afhwd",
                window,
                weights[3 * row_shift + col_shift],
                preferred_element_type=jnp.float32,
            )
    return summed.reshape(values.shape[0], values.shape[1], SIDE * SIDE, weights.shape[2])


def batch_norm(values, total_sum, squares, row_count, gain_row, shift_row):
    center = total_sum / row_count
    spread = squares / row_count - center * center
    return (values - center) * (gain_row * lax.rsqrt(spread + EPSILON)) + shift_row


def encode(values, params, moments, row_count):
    (
        conv_time,
        conv_space,
        conv_expand,
        gain_one,
        shift_one,
        gain_two,
        shift_two,
        gain_three,
        shift_three,
        w_key,
    ) = params
    first_out = time_conv(values, conv_time)
    total_sum, squares = moments(first_out)
    act_one = jnp.maximum(
        batch_norm(first_out, total_sum, squares, row_count, gain_one, shift_one), 0.0
    ).astype(jnp.bfloat16)
    second = space_conv(act_one, conv_space)
    total_sum, squares = moments(second)
    act_two = jnp.maximum(
        batch_norm(second, total_sum, squares, row_count, gain_two, shift_two), 0.0
    ).astype(jnp.bfloat16)
    third_out = jnp.einsum(
        "afsc,cd->afsd", act_two, conv_expand, preferred_element_type=jnp.float32
    )
    total_sum, squares = moments(third_out)
    merged = jnp.maximum(
        batch_norm(third_out, total_sum, squares, row_count, gain_three, shift_three)
        + values.astype(jnp.float32),
        0.0,
    )
    pooled = jnp.mean(merged, axis=(1, 2)).astype(jnp.bfloat16)
    projected = jnp.dot(pooled, w_key, preferred_element_type=jnp.float32)
    return (
        projected * lax.rsqrt(jnp.sum(projected * projected, axis=-1, keepdims=True) + 1e-06)
    ).astype(jnp.bfloat16)


def query_terms(query_feats, own_keys, w_query, queue):
    projected = jnp.dot(query_feats, w_query, preferred_element_type=jnp.float32)
    length = jnp.sqrt(jnp.sum(projected * projected, axis=-1, keepdims=True) + 1e-06)
    anchor_direction = projected / length
    queue_wide = queue.astype(jnp.float32)
    memory_bank_directions = (
        queue_wide * lax.rsqrt(jnp.sum(queue_wide * queue_wide, axis=-1, keepdims=True) + 1e-06)
    ).astype(jnp.bfloat16)
    collected_encodings = own_keys.astype(jnp.float32)
    matching_scores = jnp.sum(anchor_direction * collected_encodings, axis=-1) / SHARPNESS_DIVISOR
    distractor_scores = (
        jnp.einsum(
            "nf,ef->ne",
            anchor_direction.astype(jnp.bfloat16),
            memory_bank_directions,
            preferred_element_type=jnp.float32,
        )
        / SHARPNESS_DIVISOR
    )
    partition = jnp.exp(matching_scores) + jnp.sum(jnp.exp(distractor_scores), axis=-1)
    log_total = jnp.log(partition)
    weight_pos = jnp.exp(matching_scores - log_total)
    weight_neg = jnp.exp(distractor_scores - log_total[:, None]).astype(jnp.bfloat16)
    retrieved_samples = (
        jnp.dot(weight_neg, memory_bank_directions, preferred_element_type=jnp.float32)
        + (weight_pos - 1.0)[:, None] * collected_encodings
    )
    anchor_loss_derivative = retrieved_samples / SHARPNESS_DIVISOR
    radial = jnp.sum(anchor_direction * anchor_loss_derivative, axis=-1, keepdims=True)
    return ((anchor_loss_derivative - radial * anchor_direction) / length).astype(jnp.bfloat16)


def local(
    key_feats,
    clip_starts,
    shuffle,
    query_feats,
    conv_time,
    conv_space,
    conv_expand,
    gain_one,
    shift_one,
    gain_two,
    shift_two,
    gain_three,
    shift_three,
    w_key,
    w_query,
    queue,
):
    params = (
        conv_time,
        conv_space,
        conv_expand,
        gain_one,
        shift_one,
        gain_two,
        shift_two,
        gain_three,
        shift_three,
        w_key,
    )
    chosen = pick_frames(key_feats, clip_starts)
    peer_count = lax.axis_size("dp")
    groups = lax.axis_size("bn")
    target = shuffle[0, lax.axis_index("dp")]
    row_count = groups * chosen.shape[0] * chosen.shape[1] * chosen.shape[2]
    places = (jnp.arange(peer_count, dtype=jnp.int32) == target).astype(jnp.float32)[:, None]

    def table_moments(values):
        sum_table, square_table = lax.psum(
            (
                places * jnp.sum(values, axis=(0, 1, 2))[None, :],
                places * jnp.sum(values * values, axis=(0, 1, 2))[None, :],
            ),
            ("dp", "bn"),
        )
        return (
            lax.dynamic_index_in_dim(sum_table, target, 0, keepdims=False),
            lax.dynamic_index_in_dim(square_table, target, 0, keepdims=False),
        )

    own_keys = encode(chosen, params, table_moments, row_count)
    grad_proj = query_terms(query_feats, own_keys, w_query, queue)
    grad_part = jnp.einsum("nc,ne->ce", query_feats, grad_proj, preferred_element_type=jnp.float32)
    query_grad = lax.psum(grad_part, ("dp", "bn"))
    return (own_keys, query_grad)


def solution(mesh):
    placed = (
        P(("dp", "bn"), None, None, None),
        P(("dp", "bn")),
        P("bn", None),
        P(("dp", "bn"), None),
        P(),
        P(),
        P(),
        P(),
        P(),
        P(),
        P(),
        P(),
        P(),
        P(),
        P(),
        P(),
    )
    return jax.shard_map(
        local, mesh=mesh, in_specs=placed, out_specs=(P(("dp", "bn"), None), P()), check_vma=False
    )
```

profile of v0, /device:TPU:0, one launch (start us, length us, event | category | flops | bytes accessed | tf_op | source)
XLA Modules:
  0.0 422.5 jit_solution(13021821343237458632)
XLA Ops:
  7.2 0.0 copy-start
  7.2 0.0 copy-start.14
  7.2 0.0 all-reduce.11.cloned.1.call-start
  7.2 6.7 %copy.18 = bf16[8,12,16,2048]{3,2,0,1:T(8,128)(2,1)} copy(bf16[8,12,16,2048]{3,2,1,0:T(8,128)(2,1)} %param.16) | data formatting | bytes 12582912 | tf_op args[0]
  13.9 0.0 copy-done.14
  14.0 5.6 %gather_fusion = bf16[8,8,16,2048]{3,2,1,0:T(8,128)(2,1)} fusion(bf16[8,12,16,2048]{3,2,0,1:T(8,128)(2,1)} %copy.18, s32[8]{0:T(128)S(1)} %fusion.70), kind=kCustom, calls=%fused_computation | custom fusion | bytes 8388736 | tf_op jit(solution)/shard_map/vmap()/gather | solution.py:17
  19.5 6.7 %fusion.6 = f32[8,8,16,512]{3,2,1,0:T(8,128)} fusion(bf16[8,8,16,2048]{3,2,1,0:T(8,128)(2,1)} %gather_fusion, bf16[3,2048,512]{2,1,0:T(8,128)(2,1)} %param.20), kind=kOutput, calls=%fused_computation.13 | convolution fusion | flops 2147483648 | bytes 8388608 | tf_op jit(solution)/shard_map/afsc,cd->afsd/dot_general | solution.py:27
  26.2 5.2 %fusion.8 = f32[8,8,16,512]{3,2,1,0:T(8,128)} fusion(bf16[8,8,16,2048]{3,2,1,0:T(8,128)(2,1)S(1)} %copy-done.3, bf16[3,2048,512]{2,1,0:T(8,128)(2,1)} %param.20), kind=kOutput, calls=%fused_computation.15 | convolution fusion | flops 1879048192 | bytes 8388608 | tf_op jit(solution)/shard_map/afsc,cd->afsd/dot_general | solution.py:27
  31.4 0.0 copy-done.15
  31.5 0.6 constant_dynamic-slice_fusion
  32.0 0.6 compare_convert_fusion
  34.0 0.0 copy-start.9
  34.0 0.0 copy-start.12
  34.0 7.7 %fusion.75 = (f32[512]{0:T(512)S(1)}, f32[512]{0:T(512)S(1)}, f32[8,8,16,512]{3,2,1,0:T(8,128)}) fusion(bf16[8,8,16,2048]{3,2,1,0:T(8,128)(2,1)} %gather_fusion, bf16[3,2048,512]{2,1,0:T(8,128)(2,1)} %param.20, f32[8,8,16,512]{3,2,1,0:T(8,128)} %fusion.8, f32[8,8,16,512]{3,2,1,0:T(8,128)} %fusion.6), kind=kOutput, calls=%fused_computation.113 | convolution fusion | flops 1881668608 | bytes 12587008 | tf_op jit(solution)/shard_map/afsc,cd->afsd/dot_general | solution.py:27
  41.7 0.1 broadcast_multiply_fusion.5
  41.8 42.4 %all-reduce.4 = (f32[8,512]{1,0:T(8,128)S(1)}, f32[8,512]{1,0:T(8,128)S(1)}) all-reduce(f32[8,512]{1,0:T(8,128)S(1)} %get-tuple-element.25, f32[8,512]{1,0:T(8,128)S(1)} %get-tuple-element.24), channel_id=1, replica_groups=mesh['dp'=8,'bn'=4] {'dp','bn'}, use_global_device_ids=true, to_apply=%region_3.4 | all-reduce | flops 8192 | bytes 65536 | tf_op jit(solution)/shard_map/psum | solution.py:169
  84.8 0.0 copy-done.9
  84.8 0.0 copy-done.12
  84.8 0.0 slice-start
  84.8 2.1 maximum_convert_fusion
  86.9 0.6 copy.37
  87.6 0.0 slice-start.1
  87.6 1.8 fusion.34
  89.4 1.7 fusion.36
  91.1 1.7 fusion.38
  92.9 0.7 fusion.40
  93.6 0.7 fusion.42
  94.4 0.7 fusion.44
  95.1 0.7 fusion.46
  95.8 0.7 fusion.48
  96.5 0.0 copy-start.10
  96.5 0.0 copy-start.13
  96.5 2.6 fusion.74
  99.1 0.1 broadcast_multiply_fusion.3
  99.2 40.2 %all-reduce.3 = (f32[8,512]{1,0:T(8,128)S(1)}, f32[8,512]{1,0:T(8,128)S(1)}) all-reduce(f32[8,512]{1,0:T(8,128)S(1)} %get-tuple-element.23, f32[8,512]{1,0:T(8,128)S(1)} %get-tuple-element.22), channel_id=1, replica_groups=mesh['dp'=8,'bn'=4] {'dp','bn'}, use_global_device_ids=true, to_apply=%region_7.8 | all-reduce | flops 8192 | bytes 65536 | tf_op jit(solution)/shard_map/psum | solution.py:169
  139.6 0.0 copy-start.4
  139.6 0.0 copy-start.6
  139.6 8.0 %fusion.73 = (f32[2048]{0:T(1024)S(1)}, f32[2048]{0:T(1024)S(1)}, f32[8,8,16,2048]{3,2,1,0:T(8,128)}) fusion(bf16[512,2048]{1,0:T(8,128)(2,1)S(1)} %copy-done, f32[8,8,16,512]{3,1,2,0:T(8,128)} %bitcast.143, f32[512]{0:T(512)S(1)} %copy-done.13, f32[512]{0:T(512)S(1)} %rsqrt_multiply_fusion.1, f32[512]{0:T(512)S(1)} %bitcast.151), kind=kOutput, calls=%fused_computation.111 | convolution fusion | flops 2156392448 | bytes 12605440 | tf_op jit(solution)/shard_map/afsc,cd->afsd/dot_general | solution.py:83
  147.6 0.7 broadcast_multiply_fusion.1
  148.3 0.0 all-reduce.11.cloned.1.call-update
  148.3 0.3 all-reduce.9.cloned.1.call-start
  148.6 0.3 multiply_reduce_fusion.4
  148.9 0.0 copy-start.1
  148.9 4.2 fusion
  153.2 0.0 copy-done.1
  153.2 0.0 copy-start.7
  153.2 0.0 copy-start.8
  153.2 2.5 exponential_reduce_fusion
  155.7 116.3 %all-reduce.11.cloned.1.call-done = (f32[8,2048]{1,0:T(8,128)}, f32[8,2048]{1,0:T(8,128)}) async-done(((f32[8,2048]{1,0:T(8,128)}, f32[8,2048]{1,0:T(8,128)}), (f32[8,2048]{1,0:T(8,128)}, f32[8,2048]{1,0:T(8,128)})) %all-reduce.11.cloned.1.call-update) | async-done | bytes 131088 | tf_op jit(solution)/shard_map/psum | solution.py:169
  272.0 0.8 dynamic-slice_multiply_fusion.1
  272.8 0.9 dynamic-slice_multiply_fusion
  273.7 0.0 copy-done.7
  273.7 0.0 copy-done.8
  273.7 0.0 copy-start.5
  273.8 0.0 copy-start.2
  273.8 5.8 %maximum_reduce_fusion = f32[8,2048]{1,0:T(8,128)S(1)} fusion(bf16[8,8,16,2048]{3,2,1,0:T(8,128)(2,1)} %gather_fusion, f32[8,8,16,2048]{3,2,1,0:T(8,128)} %get-tuple-element.30, f32[2048]{0:T(1024)S(1)} %copy-done.8, f32[2048]{0:T(1024)S(1)} %rsqrt_multiply_fusion, f32[2048]{0:T(1024)S(1)} %bitcast.145), kind=kLoop, calls=%fused_computation.6 | loop fusion | flops 14663680 | bytes 12673024 | tf_op jit(solution)/shard_map/reduce_sum | solution.py:92
  279.6 0.3 multiply_reduce_fusion.5
  279.9 0.2 fusion.62
  280.1 0.0 copy-start.11
  280.1 2.5 multiply_reduce_fusion.3
  282.6 1.4 convolution_bitcast_fusion
  284.0 0.0 all-reduce.9.cloned.1.call-update
  284.0 129.1 %all-reduce.9.cloned.1.call-done = f32[2048,128]{0,1:T(8,128)} async-done(((f32[2048,128]{0,1:T(8,128)}), f32[2048,128]{0,1:T(8,128)}) %all-reduce.9.cloned.1.call-update) | async-done | bytes 1048592 | tf_op jit(solution)/shard_map/psum | solution.py:184
  413.1 2.5 copy.22
  (25 shorter events, 0.1 us)
Async XLA Ops:
  7.2 132.4 %copy-start = (bf16[512,2048]{1,0:T(8,128)(2,1)S(1)}, bf16[512,2048]{1,0:T(8,128)(2,1)}, u32[]{:S(2)}) copy-start(bf16[512,2048]{1,0:T(8,128)(2,1)} %param.22) | copy-start | bytes 6291460
  7.2 6.8 %copy-start.14 = (s32[8]{0:T(128)S(1)}, s32[8]{0:T(128)}, u32[]{:S(2)}) copy-start(s32[8]{0:T(128)} %param.17) | copy-start | bytes 100
  7.2 264.8 %all-reduce.11.cloned.1.call-start = ((), (), s32[]{:S(2)}) async-start(), calls=%async_computation.1 | async-start | bytes 262144 | tf_op jit(solution)/shard_map/psum | solution.py:169
  19.5 6.7 %copy-start.3 = (bf16[8,8,16,2048]{3,2,1,0:T(8,128)(2,1)S(1)}, bf16[8,8,16,2048]{3,2,1,0:T(8,128)(2,1)}, u32[]{:S(2)}) copy-start(bf16[8,8,16,2048]{3,2,1,0:T(8,128)(2,1)} %gather_fusion) | copy-start | bytes 12582916
  26.2 5.2 %copy-start.15 = (s32[1,8]{1,0:T(1,128)S(1)}, s32[1,8]{1,0:T(1,128)}, u32[]{:S(2)}) copy-start(s32[1,8]{1,0:T(1,128)} %param.18) | copy-start | bytes 100
  34.0 50.8 %copy-start.9 = (f32[512]{0:T(512)S(1)}, f32[512]{0:T(512)}, u32[]{:S(2)}) copy-start(f32[512]{0:T(512)} %param.23) | copy-start | bytes 6148
  34.0 50.8 %copy-start.12 = (f32[512]{0:T(512)S(1)}, f32[512]{0:T(512)}, u32[]{:S(2)}) copy-start(f32[512]{0:T(512)} %param.24) | copy-start | bytes 6148
  84.8 8.1 %slice-start = ((s8[4718592]{0:T(1024)(128)(4,1)}), s8[4194304]{0:T(1024)(128)(4,1)S(1)}, s32[]{:S(2)}) async-start(s8[4718592]{0:T(1024)(128)(4,1)} %bitcast.141), calls=%async_computation.2 | async-start | bytes 8388608
  87.6 5.3 %slice-start.1 = ((s8[4718592]{0:T(1024)(128)(4,1)}), s8[524288]{0:T(1024)(128)(4,1)S(1)}, s32[]{:S(2)}) async-start(s8[4718592]{0:T(1024)(128)(4,1)} %bitcast.141), calls=%async_computation.3 | async-start | bytes 1048576
  96.5 43.0 %copy-start.10 = (f32[512]{0:T(512)S(1)}, f32[512]{0:T(512)}, u32[]{:S(2)}) copy-start(f32[512]{0:T(512)} %param.25) | copy-start | bytes 6148
  96.5 43.1 %copy-start.13 = (f32[512]{0:T(512)S(1)}, f32[512]{0:T(512)}, u32[]{:S(2)}) copy-start(f32[512]{0:T(512)} %param.26) | copy-start | bytes 6148
  139.6 9.0 %copy-start.4 = (bf16[2048,128]{1,0:T(8,128)(2,1)S(1)}, bf16[2048,128]{1,0:T(8,128)(2,1)}, u32[]{:S(2)}) copy-start(bf16[2048,128]{1,0:T(8,128)(2,1)} %param.30) | copy-start | bytes 1572868
  139.6 9.0 %copy-start.6 = (bf16[8,2048]{1,0:T(8,128)(2,1)S(1)}, bf16[8,2048]{1,0:T(8,128)(2,1)}, u32[]{:S(2)}) copy-start(bf16[8,2048]{1,0:T(8,128)(2,1)} %param.19) | copy-start | bytes 98308
  148.3 264.8 %all-reduce.9.cloned.1.call-start = ((), (), s32[]{:S(2)}) async-start(), calls=%async_computation | async-start | bytes 2097152 | tf_op jit(solution)/shard_map/psum | solution.py:184
  148.9 4.3 %copy-start.1 = (bf16[16384,128]{1,0:T(8,128)(2,1)S(1)}, bf16[16384,128]{1,0:T(8,128)(2,1)}, u32[]{:S(2)}) copy-start(bf16[16384,128]{1,0:T(8,128)(2,1)} %param.31) | copy-start | bytes 12582916
  153.2 120.5 %copy-start.7 = (f32[2048]{0:T(1024)S(1)}, f32[2048]{0:T(1024)}, u32[]{:S(2)}) copy-start(f32[2048]{0:T(1024)} %param.27) | copy-start | bytes 24580
  153.2 120.5 %copy-start.8 = (f32[2048]{0:T(1024)S(1)}, f32[2048]{0:T(1024)}, u32[]{:S(2)}) copy-start(f32[2048]{0:T(1024)} %param.28) | copy-start | bytes 24580
  273.7 5.9 %copy-start.5 = (bf16[2048,128]{1,0:T(8,128)(2,1)S(1)}, bf16[2048,128]{1,0:T(8,128)(2,1)}, u32[]{:S(2)}) copy-start(bf16[2048,128]{1,0:T(8,128)(2,1)} %param.29) | copy-start | bytes 1572868
  273.8 6.4 %copy-start.2 = (bf16[16384,128]{1,0:T(8,128)(2,1)S(1)}, bf16[16384,128]{1,0:T(8,128)(2,1)}, u32[]{:S(2)}) copy-start(bf16[16384,128]{1,0:T(8,128)(2,1)} %param.31) | copy-start | bytes 12582916
  280.1 2.5 copy-start.11
Sparse Core Ops, SparseCore 0:
  148.4 123.4 all-reduce.10
  284.1 128.8 all-reduce.8
where the time goes:
time: 423 us; the launch traced here: 422 us
  waiting for transfers between devices  245 us (58%)
  blocking collectives  82.6 us (20%)
  matrix products  46 us (11%)
  between operations  16.4 us (4%)
  local copies, waits for them, and re-layouts  16.1 us (4%)
  other arithmetic  15.7 us (4%)
    psum x1, waiting for transfers between devices, local(): query_grad = lax.psum(grad_part, ('dp', 'bn'))  129 us
    psum x1, waiting for transfers between devices, table_moments(): lax.psum((places * jnp.sum(values, axis=(0, 1, 2))[None, :], places * jnp...  116 us
    psum x2, blocking collectives, table_moments(): lax.psum((places * jnp.sum(values, axis=(0, 1, 2))[None, :], places * jnp...  82.6 us
    dot_general x3, matrix products, time_conv(): jnp.einsum('afsc,cd->afsd', padded[:, offset:offset + length], weights[of...  19.6 us
    dot_general x9, matrix products, space_conv(): jnp.einsum('afhwc,cd->afhwd', window, weights[3 * row_shift + col_shift],...  11.5 us
    unnamed x38, local copies, waits for them, and re-layouts  9.35 us
  transfers between devices with their start and end apart: 2, of which 2 were waited for; matrix products, arithmetic and copies ran while one was open for 2% of the time, Pallas kernels for 0%

commit v1 on v0

--- a/solution.py
+++ b/solution.py
@@ -126,6 +126,12 @@
     anchor_loss_derivative = retrieved_samples / SHARPNESS_DIVISOR
     radial = jnp.sum(anchor_direction * anchor_loss_derivative, axis=-1, keepdims=True)
     return ((anchor_loss_derivative - radial * anchor_direction) / length).astype(jnp.bfloat16)
+
+
+def spread_to_all(own):
+    device_count = lax.axis_size("dp") * lax.axis_size("bn")
+    copies = jnp.broadcast_to(own[None], (device_count,) + own.shape)
+    return lax.all_to_all(copies, ("dp", "bn"), 0, 0)
 
 
 def local(
@@ -163,25 +169,25 @@
     groups = lax.axis_size("bn")
     target = shuffle[0, lax.axis_index("dp")]
     row_count = groups * chosen.shape[0] * chosen.shape[1] * chosen.shape[2]
-    places = (jnp.arange(peer_count, dtype=jnp.int32) == target).astype(jnp.float32)[:, None]
+    tables = lax.all_gather(shuffle[0], "bn")
+    same = (tables.T == target).astype(jnp.float32).reshape(peer_count * groups, 1)
+    all_queries = lax.all_gather(query_feats, ("dp", "bn"))
 
     def table_moments(values):
-        sum_table, square_table = lax.psum(
-            (
-                places * jnp.sum(values, axis=(0, 1, 2))[None, :],
-                places * jnp.sum(values * values, axis=(0, 1, 2))[None, :],
-            ),
-            ("dp", "bn"),
+        width = values.shape[-1]
+        own = jnp.concatenate(
+            [jnp.sum(values, axis=(0, 1, 2)), jnp.sum(values * values, axis=(0, 1, 2))]
         )
-        return (
-            lax.dynamic_index_in_dim(sum_table, target, 0, keepdims=False),
-            lax.dynamic_index_in_dim(square_table, target, 0, keepdims=False),
-        )
+        every = spread_to_all(own.reshape(-1, 128)).reshape(peer_count * groups, 2 * width)
+        total = jnp.sum(every * same, axis=0)
+        return total[:width], total[width:]
 
     own_keys = encode(chosen, params, table_moments, row_count)
     grad_proj = query_terms(query_feats, own_keys, w_query, queue)
-    grad_part = jnp.einsum("nc,ne->ce", query_feats, grad_proj, preferred_element_type=jnp.float32)
-    query_grad = lax.psum(grad_part, ("dp", "bn"))
+    all_grads = spread_to_all(grad_proj)
+    query_grad = jnp.einsum(
+        "dnc,dne->ce", all_queries, all_grads, preferred_element_type=jnp.float32
+    )
     return (own_keys, query_grad)
 
 

time: 423 us -> 139 us (0.33)
  waiting for transfers between devices: 245 us -> 22.4 us
  blocking collectives: 82.6 us -> 15.7 us
  starting transfers between devices: 0.3 us -> 14.2 us
  matrix products: 46 us -> 41.3 us
    psum x2 -> x0, waiting for transfers between devices: 245 us -> none  [the longest x1 129 us: local(): query_grad = lax.psum(grad_part, ('dp', 'bn'))]
    psum x2 -> x0, blocking collectives: 82.6 us -> none  [table_moments(): lax.psum((places * jnp.sum(values, axis=(0, 1, 2))[None, :], places * jnp...]
    all_to_all x0 -> x3, waiting for transfers between devices: none -> 20.7 us  [spread_to_all(): return lax.all_to_all(copies, ('dp', 'bn'), 0, 0)]
    all_to_all x0 -> x3, starting transfers between devices: none -> 14.2 us  [spread_to_all(): return lax.all_to_all(copies, ('dp', 'bn'), 0, 0)]
    all_to_all x0 -> x1, blocking collectives: none -> 10.7 us  [spread_to_all(): return lax.all_to_all(copies, ('dp', 'bn'), 0, 0)]
    all_gather x0 -> x1, blocking collectives: none -> 5.04 us  [local(): tables = lax.all_gather(shuffle[0], 'bn')]
    dot_general x3, matrix products: 19.6 us -> 14.7 us  [time_conv(): jnp.einsum('afsc,cd->afsd', padded[:, offset:offset + length], weights[of...]
    unnamed x38 -> x36, local copies, waits for them, and re-layouts: 9.35 us -> 8.14 us
  transfers between devices with their start and end apart: 2 -> 4, of which waited for: 2 -> 4; matrix products, arithmetic and copies ran while one was open for 2% -> 19% of each run, Pallas kernels for 0% -> 0%
where the time goes in v1:
time: 139 us
  matrix products  41.3 us (30%)
  waiting for transfers between devices  22.4 us (16%)
  local copies, waits for them, and re-layouts  17.3 us (12%)
  blocking collectives  15.7 us (11%)
  between operations  14.5 us (10%)
  starting transfers between devices  14.2 us (10%)
  other arithmetic  13.2 us (9%)
    all_to_all x3, waiting for transfers between devices, spread_to_all(): return lax.all_to_all(copies, ('dp', 'bn'), 0, 0)  20.7 us
    dot_general x3, matrix products, time_conv(): jnp.einsum('afsc,cd->afsd', padded[:, offset:offset + length], weights[of...  14.7 us
    all_to_all x3, starting transfers between devices, spread_to_all(): return lax.all_to_all(copies, ('dp', 'bn'), 0, 0)  14.2 us
    dot_general x9, matrix products, space_conv(): jnp.einsum('afhwc,cd->afhwd', window, weights[3 * row_shift + col_shift],...  11.5 us
    all_to_all x1, blocking collectives, spread_to_all(): return lax.all_to_all(copies, ('dp', 'bn'), 0, 0)  10.7 us
    unnamed x36, local copies, waits for them, and re-layouts  8.14 us
    dot_general x1, matrix products, encode(): jnp.einsum('afsc,cd->afsd', act_two, conv_expand, preferred_element_type=...  8.01 us
    reduce_sum x1, other arithmetic, encode(): pooled = jnp.mean(merged, axis=(1, 2)).astype(jnp.bfloat16)  5.84 us
  transfers between devices with their start and end apart: 4, of which 4 were waited for; matrix products, arithmetic and copies ran while one was open for 19% of the time, Pallas kernels for 0%

profile of v1, /device:TPU:0, one launch (start us, length us, event | category | flops | bytes accessed | tf_op | source)
XLA Modules:
  0.0 138.6 jit_solution(13425015365731980411)
XLA Ops:
  7.2 0.0 copy-start
  7.2 6.7 %copy.39 = bf16[8,12,16,2048]{3,2,0,1:T(8,128)(2,1)} copy(bf16[8,12,16,2048]{3,2,1,0:T(8,128)(2,1)} %param.16) | data formatting | bytes 12582912 | tf_op args[0]
  13.9 0.0 copy-done.14
  13.9 5.6 %gather_fusion = bf16[8,8,16,2048]{3,2,1,0:T(8,128)(2,1)} fusion(bf16[8,12,16,2048]{3,2,0,1:T(8,128)(2,1)} %copy.39, s32[8]{0:T(128)S(1)} %fusion.81), kind=kCustom, calls=%fused_computation | custom fusion | bytes 8388736 | tf_op jit(solution)/shard_map/vmap()/gather | solution.py:17
  19.5 5.3 %fusion.6 = f32[8,8,16,512]{3,2,1,0:T(8,128)S(1)} fusion(bf16[8,8,16,2048]{3,2,1,0:T(8,128)(2,1)} %gather_fusion, bf16[3,2048,512]{2,1,0:T(8,128)(2,1)} %param.20), kind=kOutput, calls=%fused_computation.13 | convolution fusion | flops 2147483648 | bytes 8388608 | tf_op jit(solution)/shard_map/afsc,cd->afsd/dot_general | solution.py:27
  24.8 0.0 copy-done.2
  24.8 3.9 %fusion.8 = f32[8,8,16,512]{3,2,1,0:T(8,128)S(1)} fusion(bf16[8,8,16,2048]{3,2,1,0:T(8,128)(2,1)S(1)} %copy-done.2, bf16[3,2048,512]{2,1,0:T(8,128)(2,1)} %param.20), kind=kOutput, calls=%fused_computation.15 | convolution fusion | flops 1879048192 | bytes 8388608 | tf_op jit(solution)/shard_map/afsc,cd->afsd/dot_general | solution.py:27
  28.8 0.0 copy-start.12
  28.8 0.0 copy-start.8
  28.8 0.0 copy-start.11
  28.8 5.4 %fusion.86 = (f32[512]{0:T(512)S(1)}, f32[512]{0:T(512)S(1)}, f32[8,8,16,512]{3,2,1,0:T(8,128)}) fusion(bf16[8,8,16,2048]{3,2,1,0:T(8,128)(2,1)S(1)} %copy-done.2, bf16[3,2048,512]{2,1,0:T(8,128)(2,1)} %param.20, f32[8,8,16,512]{3,2,1,0:T(8,128)S(1)} %fusion.8, f32[8,8,16,512]{3,2,1,0:T(8,128)S(1)} %fusion.6), kind=kOutput, calls=%fused_computation.121 | convolution fusion | flops 1881668608 | bytes 12587008 | tf_op jit(solution)/shard_map/afsc,cd->afsd/dot_general | solution.py:27
  34.3 0.7 broadcast_in_dim.11
  34.9 7.3 %all-to-all-start = ((f32[32,8,128]{2,1,0:T(8,128)}), f32[32,8,128]{2,1,0:T(8,128)S(1)}, u32[]{:S(2)}, u32[]{:S(2)}) async-start(f32[32,8,128]{2,1,0:T(8,128)} %broadcast_in_dim.11), calls=%async_computation | async-start | bytes 262144 | tf_op jit(solution)/shard_map/all_to_all | solution.py:134
  42.2 5.0 %all-gather.1 = s32[4,1,8]{2,1,0:T(1,128)S(1)} all-gather(s32[1,1,8]{2,1,0:T(1,128)S(1)} %bitcast.198), channel_id=1, replica_groups=mesh['dp'=8,'bn'=4] {'bn'}, dimensions={0}, use_global_device_ids=true | all-gather | bytes 160 | tf_op jit(solution)/shard_map/all_gather | solution.py:172
  47.3 0.6 constant_dynamic-slice_fusion
  47.9 0.6 compare_convert_fusion
  48.5 0.1 copy.40
  48.6 0.1 reshape.107
  48.7 1.8 %all-to-all-done = f32[32,8,128]{2,1,0:T(8,128)S(1)} async-done(((f32[32,8,128]{2,1,0:T(8,128)}), f32[32,8,128]{2,1,0:T(8,128)S(1)}, u32[]{:S(2)}, u32[]{:S(2)}) %all-to-all-start) | async-done | bytes 131104 | tf_op jit(solution)/shard_map/all_to_all | solution.py:134
  50.5 0.1 multiply_reduce_fusion.5
  50.6 0.0 slice-start
  50.6 2.1 %maximum_convert_fusion = bf16[8,8,16,512]{3,2,1,0:T(8,128)(2,1)S(1)} fusion(f32[8,8,16,512]{3,2,1,0:T(8,128)} %get-tuple-element.22, f32[512]{0:T(512)S(1)} %copy-done.11, f32[512]{0:T(512)S(1)} %fusion.75, f32[512]{0:T(512)S(1)} %multiply_bitcast_fusion.1), kind=kLoop, calls=%fused_computation.24 | loop fusion | flops 2621440 | bytes 3151872 | tf_op jit(solution)/shard_map/convert_element_type | solution.py:77
  52.7 0.6 copy.59
  53.3 0.0 slice-start.1
  53.4 1.8 %fusion.35 = f32[8,8,4,4,512]{4,1,3,2,0:T(8,128)S(1)} fusion(bf16[8,8,4,4,512]{4,1,3,2,0:T(8,128)(2,1)S(1)} %bitcast.179, bf16[9,512,512]{2,1,0:T(8,128)(2,1)} %param.21), kind=kOutput, calls=%fused_computation.39 | convolution fusion | flops 402653184 | bytes 3670016 | tf_op jit(solution)/shard_map/afhwc,cd->afhwd/dot_general | solution.py:45
  55.2 1.7 %fusion.37 = f32[8,8,4,4,512]{4,1,3,2,0:T(8,128)S(1)} fusion(bf16[8,8,4,4,512]{4,1,3,2,0:T(8,128)(2,1)S(1)} %bitcast.180, bf16[9,512,512]{2,1,0:T(8,128)(2,1)} %param.21), kind=kOutput, calls=%fused_computation.41 | convolution fusion | flops 301989888 | bytes 3670016 | tf_op jit(solution)/shard_map/afhwc,cd->afhwd/dot_general | solution.py:45
  56.9 1.7 %fusion.39 = f32[8,8,4,4,512]{4,1,3,2,0:T(8,128)S(1)} fusion(bf16[8,8,4,4,512]{4,1,3,2,0:T(8,128)(2,1)S(1)} %bitcast.181, bf16[9,512,512]{2,1,0:T(8,128)(2,1)} %param.21), kind=kOutput, calls=%fused_computation.43 | convolution fusion | flops 402653184 | bytes 3670016 | tf_op jit(solution)/shard_map/afhwc,cd->afhwd/dot_general | solution.py:45
  58.7 0.7 fusion.41
  59.4 0.7 fusion.43
  60.1 0.7 fusion.45
  60.8 0.7 fusion.47
  61.6 0.7 fusion.49
  62.3 0.0 copy-start.9
  62.3 0.0 copy-start.13
  62.3 2.6 %fusion.85 = (f32[512]{0:T(512)S(1)}, f32[512]{0:T(512)S(1)}, f32[8,8,4,4,512]{4,1,3,2,0:T(8,128)}) fusion(bf16[8,8,4,4,512]{4,1,3,2,0:T(8,128)(2,1)S(1)} %bitcast.187, bf16[9,512,512]{2,1,0:T(8,128)(2,1)S(1)} %bitcast.189, f32[8,8,4,4,512]{4,1,3,2,0:T(8,128)S(1)} %fusion.35, f32[8,8,4,4,512]{4,1,3,2,0:T(8,128)S(1)} %fusion.37, ...), kind=kOutput, calls=%fused_computation.120 | convolution fusion | flops 307756032 | bytes 20451328 | tf_op jit(solution)/shard_map/afhwc,cd->afhwd/dot_general | solution.py:45
  64.9 0.7 broadcast_in_dim.12
  65.6 4.2 %all-to-all-start.1 = ((f32[32,8,128]{2,1,0:T(8,128)}), f32[32,8,128]{2,1,0:T(8,128)S(1)}, u32[]{:S(2)}, u32[]{:S(2)}) async-start(f32[32,8,128]{2,1,0:T(8,128)} %broadcast_in_dim.12), calls=%async_computation.1 | async-start | bytes 262144 | tf_op jit(solution)/shard_map/all_to_all | solution.py:134
  69.9 0.0 all-gather.4.cloned.1.call-start
  69.9 0.7 all-gather.4.cloned.1.call-update
  70.6 7.3 %all-to-all-done.1 = f32[32,8,128]{2,1,0:T(8,128)S(1)} async-done(((f32[32,8,128]{2,1,0:T(8,128)}), f32[32,8,128]{2,1,0:T(8,128)S(1)}, u32[]{:S(2)}, u32[]{:S(2)}) %all-to-all-start.1) | async-done | bytes 131104 | tf_op jit(solution)/shard_map/all_to_all | solution.py:134
  77.9 0.1 multiply_reduce_fusion.4
  78.1 0.0 copy-start.3
  78.1 0.0 copy-start.5
  78.1 8.0 %fusion.84 = (f32[2048]{0:T(1024)S(1)}, f32[2048]{0:T(1024)S(1)}, f32[8,8,16,2048]{3,2,1,0:T(8,128)}) fusion(bf16[512,2048]{1,0:T(8,128)(2,1)S(1)} %copy-done, f32[8,8,16,512]{3,1,2,0:T(8,128)} %bitcast.190, f32[512]{0:T(512)S(1)} %copy-done.13, f32[512]{0:T(512)S(1)} %fusion.72, f32[512]{0:T(512)S(1)} %multiply_bitcast_fusion), kind=kOutput, calls=%fused_computation.119 | convolution fusion | flops 2156392448 | bytes 12605440 | tf_op jit(solution)/shard_map/afsc,cd->afsd/dot_general | solution.py:83
  86.1 0.9 broadcast_in_dim.13
  87.0 2.6 %all-to-all-start.2 = ((f32[32,32,128]{2,1,0:T(8,128)}), f32[32,32,128]{2,1,0:T(8,128)S(1)}, u32[]{:S(2)}, u32[]{:S(2)}) async-start(f32[32,32,128]{2,1,0:T(8,128)} %broadcast_in_dim.13), calls=%async_computation.2 | async-start | bytes 1048576 | tf_op jit(solution)/shard_map/all_to_all | solution.py:134
  89.6 0.3 multiply_reduce_fusion.7
  89.9 0.0 copy-start.7
  89.9 3.9 %fusion = f32[16384]{0:T(1024)S(1)} fusion(bf16[16384,128]{1,0:T(8,128)(2,1)} %param.31), kind=kLoop, calls=%fused_computation.4 | loop fusion | flops 6275072 | bytes 4259840 | tf_op jit(solution)/shard_map/reduce_sum | solution.py:105
  93.9 11.6 %all-to-all-done.2 = f32[32,32,128]{2,1,0:T(8,128)S(1)} async-done(((f32[32,32,128]{2,1,0:T(8,128)}), f32[32,32,128]{2,1,0:T(8,128)S(1)}, u32[]{:S(2)}, u32[]{:S(2)}) %all-to-all-start.2) | async-done | bytes 524320 | tf_op jit(solution)/shard_map/all_to_all | solution.py:134
  105.5 0.1 multiply_reduce_fusion.3
  105.6 0.0 copy-start.4
  105.6 0.0 copy-start.1
  105.6 5.8 %maximum_reduce_fusion = f32[8,2048]{1,0:T(8,128)S(1)} fusion(bf16[8,8,16,2048]{3,2,1,0:T(8,128)(2,1)} %gather_fusion, f32[8,8,16,2048]{3,2,1,0:T(8,128)} %get-tuple-element.24, f32[2048]{0:T(1024)S(1)} %copy-done.7, f32[2048]{0:T(1024)S(1)} %fusion.67, f32[2048]{0:T(1024)S(1)} %fusion.68), kind=kLoop, calls=%fused_computation.6 | loop fusion | flops 14663680 | bytes 12673024 | tf_op jit(solution)/shard_map/reduce_sum | solution.py:92
  111.5 0.3 multiply_reduce_fusion.8
  111.8 0.2 fusion.69
  112.0 0.0 copy-start.10
  112.0 2.5 %exponential_reduce_fusion = (f32[8]{0:T(128)S(1)}, f32[8,16384]{1,0:T(8,128)S(1)}) fusion(bf16[16384,128]{1,0:T(8,128)(2,1)S(1)} %copy-done.1, f32[16384]{0:T(1024)S(1)} %add_rsqrt_fusion, f32[8,128]{1,0:T(8,128)S(1)} %get-tuple-element.21, f32[8]{0:T(128)S(1)} %get-tuple-element.31), kind=kOutput, calls=%fused_computation.56 | convolution fusion | flops 40110072 | bytes 4788288 | tf_op jit(solution)/shard_map/nf,ef->ne/dot_general | solution.py:110
  114.5 2.5 %multiply_reduce_fusion.6 = (f32[8]{0:T(128)S(1)}, f32[8,128]{1,0:T(8,128)S(1)}) fusion(f32[8,128]{1,0:T(8,128)S(1)} %get-tuple-element.21, f32[8]{0:T(128)S(1)} %get-tuple-element.31, bf16[8,128]{1,0:T(8,128)(2,1)S(1)} %get-tuple-element.17, f32[8]{0:T(128)S(1)} %get-tuple-element.18, bf16[16384,128]{1,0:T(8,128)(2,1)S(1)} %copy-done.1, ...), kind=kOutput, calls=%fused_computation.90 | convolution fusion | flops 40115192 | bytes 4794496 | tf_op jit(solution)/shard_map/dot_general | solution.py:123
  117.0 0.1 divide_convert_fusion
  117.1 10.7 %all_to_all.20 = bf16[32,8,128]{2,1,0:T(8,128)(2,1)S(1)} all-to-all(bf16[32,8,128]{2,1,0:T(8,128)(2,1)S(1)} %broadcast_in_dim.14), channel_id=1, replica_groups=mesh['dp'=8,'bn'=4] {'dp','bn'}, dimensions={0} | all-to-all | bytes 131072 | tf_op jit(solution)/shard_map/all_to_all | solution.py:134
  127.8 1.1 all-gather.4.cloned.1.call-done
  128.9 1.6 %convolution_bitcast_fusion = f32[2048,128]{0,1:T(8,128)S(1)} fusion(bf16[32,8,128]{2,1,0:T(8,128)(2,1)S(1)} %all_to_all.20, bf16[256,2048]{1,0:T(8,128)(2,1)} %all-gather.4.cloned.1.call-done), kind=kOutput, calls=%fused_computation.8 | convolution fusion | flops 134217728 | bytes 2162688 | tf_op jit(solution)/shard_map/dnc,dne->ce/dot_general | solution.py:188
  130.4 1.3 copy.44
  (33 shorter events, 0.2 us)
Async XLA Ops:
  7.2 70.9 %copy-start = (bf16[512,2048]{1,0:T(8,128)(2,1)S(1)}, bf16[512,2048]{1,0:T(8,128)(2,1)}, u32[]{:S(2)}) copy-start(bf16[512,2048]{1,0:T(8,128)(2,1)} %param.22) | copy-start | bytes 6291460
  7.2 6.7 %copy-start.14 = (s32[8]{0:T(128)S(1)}, s32[8]{0:T(128)}, u32[]{:S(2)}) copy-start(s32[8]{0:T(128)} %param.17) | copy-start | bytes 100
  19.5 5.3 %copy-start.2 = (bf16[8,8,16,2048]{3,2,1,0:T(8,128)(2,1)S(1)}, bf16[8,8,16,2048]{3,2,1,0:T(8,128)(2,1)}, u32[]{:S(2)}) copy-start(bf16[8,8,16,2048]{3,2,1,0:T(8,128)(2,1)} %gather_fusion) | copy-start | bytes 12582916
  28.8 13.5 %copy-start.12 = (s32[1,8]{1,0:T(1,128)S(1)}, s32[1,8]{1,0:T(1,128)}, u32[]{:S(2)}) copy-start(s32[1,8]{1,0:T(1,128)} %param.18) | copy-start | bytes 100
  28.8 21.8 %copy-start.8 = (f32[512]{0:T(512)S(1)}, f32[512]{0:T(512)}, u32[]{:S(2)}) copy-start(f32[512]{0:T(512)} %param.23) | copy-start | bytes 6148
  28.8 21.8 %copy-start.11 = (f32[512]{0:T(512)S(1)}, f32[512]{0:T(512)}, u32[]{:S(2)}) copy-start(f32[512]{0:T(512)} %param.24) | copy-start | bytes 6148
  34.9 15.5 %all-to-all-start = ((f32[32,8,128]{2,1,0:T(8,128)}), f32[32,8,128]{2,1,0:T(8,128)S(1)}, u32[]{:S(2)}, u32[]{:S(2)}) async-start(f32[32,8,128]{2,1,0:T(8,128)} %broadcast_in_dim.11), calls=%async_computation | async-start | bytes 262144 | tf_op jit(solution)/shard_map/all_to_all | solution.py:134
  50.6 8.1 %slice-start = ((s8[4718592]{0:T(1024)(128)(4,1)}), s8[4194304]{0:T(1024)(128)(4,1)S(1)}, s32[]{:S(2)}) async-start(s8[4718592]{0:T(1024)(128)(4,1)} %bitcast.188), calls=%async_computation.5 | async-start | bytes 8388608
  53.3 5.3 %slice-start.1 = ((s8[4718592]{0:T(1024)(128)(4,1)}), s8[524288]{0:T(1024)(128)(4,1)S(1)}, s32[]{:S(2)}) async-start(s8[4718592]{0:T(1024)(128)(4,1)} %bitcast.188), calls=%async_computation.6 | async-start | bytes 1048576
  62.3 15.8 %copy-start.9 = (f32[512]{0:T(512)S(1)}, f32[512]{0:T(512)}, u32[]{:S(2)}) copy-start(f32[512]{0:T(512)} %param.25) | copy-start | bytes 6148
  62.3 15.8 %copy-start.13 = (f32[512]{0:T(512)S(1)}, f32[512]{0:T(512)}, u32[]{:S(2)}) copy-start(f32[512]{0:T(512)} %param.26) | copy-start | bytes 6148
  65.6 12.3 %all-to-all-start.1 = ((f32[32,8,128]{2,1,0:T(8,128)}), f32[32,8,128]{2,1,0:T(8,128)S(1)}, u32[]{:S(2)}, u32[]{:S(2)}) async-start(f32[32,8,128]{2,1,0:T(8,128)} %broadcast_in_dim.12), calls=%async_computation.1 | async-start | bytes 262144 | tf_op jit(solution)/shard_map/all_to_all | solution.py:134
  69.9 59.0 %all-gather.4.cloned.1.call-start = ((), (), s32[]{:S(2)}) async-start(), calls=%async_computation.4 | async-start | bytes 1081344 | tf_op jit(solution)/shard_map/all_gather | solution.py:174
  78.1 11.5 %copy-start.3 = (bf16[2048,128]{1,0:T(8,128)(2,1)S(1)}, bf16[2048,128]{1,0:T(8,128)(2,1)}, u32[]{:S(2)}) copy-start(bf16[2048,128]{1,0:T(8,128)(2,1)} %param.30) | copy-start | bytes 1572868
  78.1 11.5 %copy-start.5 = (bf16[8,2048]{1,0:T(8,128)(2,1)S(1)}, bf16[8,2048]{1,0:T(8,128)(2,1)}, u32[]{:S(2)}) copy-start(bf16[8,2048]{1,0:T(8,128)(2,1)} %param.19) | copy-start | bytes 98308
  87.0 18.5 %all-to-all-start.2 = ((f32[32,32,128]{2,1,0:T(8,128)}), f32[32,32,128]{2,1,0:T(8,128)S(1)}, u32[]{:S(2)}, u32[]{:S(2)}) async-start(f32[32,32,128]{2,1,0:T(8,128)} %broadcast_in_dim.13), calls=%async_computation.2 | async-start | bytes 1048576 | tf_op jit(solution)/shard_map/all_to_all | solution.py:134
  89.9 15.7 %copy-start.6 = (f32[2048]{0:T(1024)S(1)}, f32[2048]{0:T(1024)}, u32[]{:S(2)}) copy-start(f32[2048]{0:T(1024)} %param.27) | copy-start | bytes 24580
  89.9 15.7 %copy-start.7 = (f32[2048]{0:T(1024)S(1)}, f32[2048]{0:T(1024)}, u32[]{:S(2)}) copy-start(f32[2048]{0:T(1024)} %param.28) | copy-start | bytes 24580
  105.6 5.9 %copy-start.4 = (bf16[2048,128]{1,0:T(8,128)(2,1)S(1)}, bf16[2048,128]{1,0:T(8,128)(2,1)}, u32[]{:S(2)}) copy-start(bf16[2048,128]{1,0:T(8,128)(2,1)} %param.29) | copy-start | bytes 1572868
  105.6 6.4 %copy-start.1 = (bf16[16384,128]{1,0:T(8,128)(2,1)S(1)}, bf16[16384,128]{1,0:T(8,128)(2,1)}, u32[]{:S(2)}) copy-start(bf16[16384,128]{1,0:T(8,128)(2,1)} %param.31) | copy-start | bytes 12582916
  112.0 2.5 %copy-start.10 = (bf16[8,128]{1,0:T(8,128)(2,1)}, bf16[8,128]{1,0:T(8,128)(2,1)S(1)}, u32[]{:S(2)}) copy-start(bf16[8,128]{1,0:T(8,128)(2,1)S(1)} %get-tuple-element.17) | copy-start | bytes 6148
Sparse Core Ops, SparseCore 0:
  73.6 55.2 all-gather.3

commit v2 on v0

v2 whole, which is shorter than its diff:
```python
import functools

import jax
import jax.numpy as jnp
from jax import lax
from jax.experimental import pallas as pl
from jax.experimental.pallas import tpu as pltpu
from jax.sharding import PartitionSpec as P

FRAMES = 8
SIDE = 4
SPOTS = SIDE * SIDE
LANES = 128
SHARPNESS_DIVISOR = 0.2
EPSILON = 1e-05
MIB = 1 << 20

VMEM = pl.BlockSpec(memory_space=pltpu.VMEM)
ANY = pl.BlockSpec(memory_space=pl.ANY)


def in_hbm(array):
    return pltpu.with_memory_space_constraint(array, pltpu.HBM)


def as_row(block):
    return jnp.concatenate([block[i : i + 1] for i in range(block.shape[0])], axis=1)


def as_block(row):
    return jnp.concatenate(
        [row[:, i : i + LANES] for i in range(0, row.shape[1], LANES)], axis=0
    )


def two_halves(values):
    high = values.astype(jnp.bfloat16).astype(jnp.float32)
    return high, values - high


def mean_and_var(total, squares, count):
    mean = total / count
    return mean, jnp.maximum(squares / count - mean * mean, 0.0)


def write_moments(message, mean, var, group):
    high, low = two_halves(mean)
    part = [as_block(high), as_block(low), as_block(var)]
    rest = message.shape[1] - sum(p.shape[0] for p in part)
    part.append(jnp.broadcast_to(group, (rest, LANES)))
    block = jnp.concatenate(part, axis=0).astype(jnp.bfloat16)
    message[...] = jnp.broadcast_to(block[None], message.shape)


def group_row(message, part):
    return message[0, 3 * part : 3 * part + 1, :].astype(jnp.float32)


def members(message, group, part):
    sender = message[:, 3 * part : 3 * part + 1, :].astype(jnp.float32)
    return (sender == group[None]).astype(jnp.float32)


def group_scale_and_bias(message, group, gain, shift):
    part = gain.shape[1] // LANES
    same = members(message, group, part)
    every = message[...].astype(jnp.float32)
    block_mean = every[:, :part] + every[:, part : 2 * part]
    block_var = every[:, 2 * part : 3 * part]
    blocks = jnp.sum(same, axis=0)
    mean = jnp.sum(block_mean * same, axis=0) / blocks
    apart = block_mean - mean[None]
    var = jnp.sum((block_var + apart * apart) * same, axis=0) / blocks
    scale = gain[...] * lax.rsqrt(as_row(var) + EPSILON)
    return scale, shift[...] - as_row(mean) * scale


def time_conv_kernel(
    cuts,
    starts_hbm,
    shuffle_hbm,
    feats,
    weights,
    first,
    frames,
    message,
    starts,
    shuffle,
    taps,
    small_sem,
    frames_sem,
    taps_sem,
):
    clips, _, spots, _ = feats.shape
    inner = weights.shape[2]
    pieces = len(cuts) - 1
    rows = clips * FRAMES * spots
    span = [pl.ds(cuts[k], cuts[k + 1] - cuts[k]) for k in range(pieces)]

    def copy_clip(k, n):
        return pltpu.make_async_copy(
            feats.at[n, pl.ds(starts[n], FRAMES), :, span[k]],
            frames.at[n, pl.ds(1, FRAMES), :, span[k]],
            frames_sem.at[k, n],
        )

    def copy_taps(k):
        return pltpu.make_async_copy(
            weights.at[:, span[k], :], taps.at[:, span[k], :], taps_sem.at[k]
        )

    copy_starts = pltpu.make_async_copy(starts_hbm, starts, small_sem.at[0])
    copy_shuffle = pltpu.make_async_copy(shuffle_hbm, shuffle, small_sem.at[1])
    copy_starts.start()
    copy_shuffle.start()
    copy_taps(0).start()
    copy_starts.wait()
    for k in range(pieces):
        for n in range(clips):
            copy_clip(k, n).start()
        if k + 1 < pieces:
            copy_taps(k + 1).start()
    blank = jnp.zeros((clips, 1) + frames.shape[2:], jnp.bfloat16)
    frames[:, 0:1] = blank
    frames[:, FRAMES + 1 : FRAMES + 2] = blank
    for k in range(pieces):
        depth = cuts[k + 1] - cuts[k]
        copy_taps(k).wait()
        for n in range(clips):
            copy_clip(k, n).wait()
        stacked = jnp.concatenate(
            [
                frames[:, o : o + FRAMES, :, cuts[k] : cuts[k + 1]].reshape(rows, depth)
                for o in range(3)
            ],
            axis=1,
        )
        product = jnp.dot(
            stacked,
            taps[:, cuts[k] : cuts[k + 1], :].reshape(3 * depth, inner),
            preferred_element_type=jnp.float32,
        )
        for j in range(inner // LANES):
            piece = product[:, j * LANES : (j + 1) * LANES]
            if k == 0:
                first[j] = piece
            else:
                first[j] += piece
    total, squares = [], []
    for j in range(inner // LANES):
        values = first[j]
        total.append(jnp.sum(values, axis=0, keepdims=True))
        squares.append(jnp.sum(values * values, axis=0, keepdims=True))
    mean, var = mean_and_var(
        jnp.concatenate(total, axis=1), jnp.concatenate(squares, axis=1), rows
    )
    copy_shuffle.wait()
    group = shuffle[0, lax.axis_index("dp")].astype(jnp.float32)
    write_moments(message, mean, var, jnp.full((1, LANES), group, jnp.float32))


def space_conv_kernel(own, got, gain, shift, first, weights, second, message, act, taken):
    inner = weights.shape[1]
    part = inner // LANES
    rows = first.shape[1] // SPOTS
    number = group_row(own, part)
    scale, bias = group_scale_and_bias(got, number, gain, shift)
    for r in range(SIDE):
        for c in range(SIDE):
            values = jnp.concatenate(
                [first[j, pl.ds(r * SIDE + c, rows, stride=SPOTS), :] for j in range(part)],
                axis=1,
            )
            act[r, c] = jnp.maximum(values * scale + bias, 0.0).astype(jnp.bfloat16)
    for k in (4, 0, 1, 2, 3, 5, 6, 7, 8):
        down, right = k // 3 - 1, k % 3 - 1
        r0, r1 = max(0, -down), min(SIDE, SIDE - down)
        c0, c1 = max(0, -right), min(SIDE, SIDE - right)
        source = act[r0 + down : r1 + down, c0 + right : c1 + right]
        product = jnp.dot(
            source.reshape((r1 - r0) * (c1 - c0) * rows, inner),
            weights[k],
            preferred_element_type=jnp.float32,
        ).reshape(r1 - r0, c1 - c0, rows, inner)
        if k == 4:
            taken[...] = product
        else:
            taken[r0:r1, c0:c1] += product
    total = jnp.zeros((1, inner), jnp.float32)
    squares = jnp.zeros((1, inner), jnp.float32)
    for r in range(SIDE):
        for c in range(SIDE):
            values = taken[r, c]
            for j in range(part):
                second[j, r * SIDE + c, 0:rows] = values[:, j * LANES : (j + 1) * LANES]
            total = total + jnp.sum(values, axis=0, keepdims=True)
            squares = squares + jnp.sum(values * values, axis=0, keepdims=True)
    mean, var = mean_and_var(total, squares, rows * SPOTS)
    write_moments(message, mean, var, number)


def expand_kernel(own, got, gain, shift, second, weights, third, message, act):
    inner, channels = weights.shape
    rows = act.shape[0]
    part = inner // LANES
    scale, bias = group_scale_and_bias(got, group_row(own, part), gain, shift)
    pitch = second.shape[1] // SPOTS
    total = jnp.zeros((SPOTS, inner), jnp.float32)
    for i in range(rows // SPOTS):
        values = jnp.concatenate(
            [second[j, pl.ds(i, SPOTS, stride=pitch), :] for j in range(part)], axis=1
        )
        act_two = jnp.maximum(values * scale + bias, 0.0).astype(jnp.bfloat16)
        act[i * SPOTS : (i + 1) * SPOTS] = act_two
        total = total + act_two.astype(jnp.float32)
    act_mean = jnp.sum(total, axis=0, keepdims=True) / rows
    high, low = two_halves(act_mean)
    found = []
    width = 4 * LANES
    for start in range(0, channels, width):
        product = jnp.dot(
            act[...], weights[:, start : start + width], preferred_element_type=jnp.float32
        )
        for j in range(width // LANES):
            third[start // LANES + j] = product[:, j * LANES : (j + 1) * LANES]
        total = jnp.sum(product, axis=0, keepdims=True)
        squares = jnp.sum(product * product, axis=0, keepdims=True)
        found.append(mean_and_var(total, squares, rows)[1])
    var = jnp.concatenate(found, axis=1)
    block = jnp.concatenate([as_block(high), as_block(low), as_block(var)], axis=0)
    message[...] = jnp.broadcast_to(block.astype(jnp.bfloat16)[None], message.shape)


def keys_kernel(
    own_numbers,
    numbers,
    got,
    gain,
    shift,
    weights,
    third,
    w_key,
    unit,
    length,
    negatives,
    pulled,
    frames,
    keys,
    message,
    pooled,
):
    clips = frames.shape[0]
    inner, channels = weights.shape
    part, wide = inner // LANES, channels // LANES
    same = members(numbers, group_row(own_numbers, part), part)
    act_mean = jnp.concatenate(
        [
            jnp.concatenate([got[:, h * part + j, :] for j in range(part)], axis=1)
            for h in range(2)
        ],
        axis=0,
    )
    parts = jnp.dot(act_mean, weights[...], preferred_element_type=jnp.float32)
    devices = got.shape[0]
    block_mean = parts[:devices] + parts[devices:]
    chosen = same[:, 0, 0:1]
    blocks = jnp.sum(same, axis=0)
    mean = jnp.sum(block_mean * chosen, axis=0, keepdims=True) / blocks[:, 0:1]
    apart = block_mean - mean
    between = jnp.sum(apart * apart * chosen, axis=0, keepdims=True) / blocks[:, 0:1]
    block_var = got[:, 2 * part : 2 * part + wide, :].astype(jnp.float32)
    within = as_row(jnp.sum(block_var * same, axis=0) / blocks)
    scale = gain[...] * lax.rsqrt(within + between + EPSILON)
    bias = shift[...] - mean * scale

    def one_clip(n, _):
        total = jnp.zeros((SPOTS, channels), jnp.float32)
        for t in range(FRAMES):
            values = jnp.concatenate(
                [
                    third[j, pl.ds((n * FRAMES + t) * SPOTS, SPOTS), :]
                    for j in range(wide)
                ],
                axis=1,
            )
            total = total + jnp.maximum(
                values * scale + bias + frames[n, t + 1].astype(jnp.float32), 0.0
            )
        pooled[pl.ds(n, 1), :] = jnp.sum(total, axis=0, keepdims=True) / (FRAMES * SPOTS)
        return 0

    lax.fori_loop(0, clips, one_clip, 0)
    projected = jnp.dot(
        pooled[...].astype(jnp.bfloat16), w_key[...], preferred_element_type=jnp.float32
    )
    own = (
        projected * lax.rsqrt(jnp.sum(projected * projected, axis=-1, keepdims=True) + 1e-06)
    ).astype(jnp.bfloat16)
    keys[...] = own
    own = own.astype(jnp.float32)
    direction = unit[...]
    positive = jnp.exp(jnp.sum(direction * own, axis=-1, keepdims=True) / SHARPNESS_DIVISOR)
    partition = positive + negatives[...]
    grad = (pulled[...] / partition + (positive / partition - 1.0) * own) / SHARPNESS_DIVISOR
    radial = jnp.sum(direction * grad, axis=-1, keepdims=True)
    grad = ((grad - radial * direction) / length[...]).astype(jnp.bfloat16)
    message[...] = jnp.broadcast_to(grad[None], message.shape)


def queue_kernel(query_feats, w_query, queue, unit, length, negatives, pulled):
    projected = jnp.dot(query_feats[...], w_query[...], preferred_element_type=jnp.float32)
    norm = jnp.sqrt(jnp.sum(projected * projected, axis=-1, keepdims=True) + 1e-06)
    direction = projected / norm
    unit[...] = direction
    length[...] = jnp.broadcast_to(norm, length.shape)
    rounded = direction.astype(jnp.bfloat16)
    rows, width = rounded.shape
    ones = jnp.ones((rows, width), jnp.bfloat16)
    across = (((1,), (1,)), ((), ()))
    step = queue.shape[0] // 8

    def one_step(i, carry):
        total, weighted = carry
        entries = queue[pl.ds(i * step, step), :]
        squares = lax.dot_general(
            ones, entries * entries, across, preferred_element_type=jnp.float32
        )
        inverse = lax.rsqrt(squares + 1e-06)
        scores = lax.dot_general(rounded, entries, across, preferred_element_type=jnp.float32)
        weight = jnp.exp(scores * inverse / SHARPNESS_DIVISOR)
        total = total + jnp.sum(weight, axis=-1, keepdims=True)
        weighted = weighted + jnp.dot(
            (weight * inverse).astype(jnp.bfloat16), entries, preferred_element_type=jnp.float32
        )
        return total, weighted

    total, weighted = lax.fori_loop(
        0,
        8,
        one_step,
        (jnp.zeros((rows, 1), jnp.float32), jnp.zeros((rows, width), jnp.float32)),
    )
    negatives[...] = jnp.broadcast_to(total, negatives.shape)
    pulled[...] = weighted


def gradient_kernel(queries_hbm, grads, out_hbm, queries, out, queries_sem, out_sem):
    channels = out.shape[0]
    width = channels // queries_sem.shape[0]

    def fetch(i):
        span = pl.ds(i * width, width)
        return pltpu.make_async_copy(
            queries_hbm.at[:, span], queries.at[:, span], queries_sem.at[i]
        )

    def give(i):
        span = pl.ds(i * width, width)
        return pltpu.make_async_copy(out.at[span], out_hbm.at[span], out_sem.at[i])

    pieces = channels // width
    for i in range(pieces):
        fetch(i).start()
    for i in range(pieces):
        fetch(i).wait()
        out[i * width : (i + 1) * width] = lax.dot_general(
            queries[:, i * width : (i + 1) * width],
            grads[...],
            (((0,), (0,)), ((), ())),
            preferred_element_type=jnp.float32,
        )
        give(i).start()
    for i in range(pieces):
        give(i).wait()


def exchange(message):
    return lax.all_to_all(message, ("dp", "bn"), 0, 0)


def local(
    key_feats,
    clip_starts,
    shuffle,
    query_feats,
    conv_time,
    conv_space,
    conv_expand,
    gain_one,
    shift_one,
    gain_two,
    shift_two,
    gain_three,
    shift_three,
    w_key,
    w_query,
    queue,
):
    devices = lax.axis_size("dp") * lax.axis_size("bn")
    clips, _, spots, channels = key_feats.shape
    inner, emb = conv_space.shape[1], queue.shape[1]
    part, wide = inner // LANES, channels // LANES
    rows = clips * FRAMES * spots
    short = jax.ShapeDtypeStruct((devices, 16, LANES), jnp.bfloat16)
    row = lambda vector: vector.reshape(1, -1)

    all_queries = lax.all_gather(query_feats, ("dp", "bn"), tiled=True)

    cuts = (0, channels // 8, 3 * channels // 8, channels)
    pieces = len(cuts) - 1
    padded = (clips, FRAMES + 2, spots, channels)
    first, frames, sent_one = pl.pallas_call(
        functools.partial(time_conv_kernel, cuts),
        out_shape=(
            jax.ShapeDtypeStruct((part, rows, LANES), jnp.float32),
            jax.ShapeDtypeStruct(padded, jnp.bfloat16),
            short,
        ),
        in_specs=[ANY] * 4,
        out_specs=(VMEM,) * 3,
        scratch_shapes=[
            pltpu.SMEM(clip_starts.shape, jnp.int32),
            pltpu.SMEM(shuffle.shape, jnp.int32),
            pltpu.VMEM(conv_time.shape, jnp.bfloat16),
            pltpu.SemaphoreType.DMA((2,)),
            pltpu.SemaphoreType.DMA((pieces, clips)),
            pltpu.SemaphoreType.DMA((pieces,)),
        ],
        compiler_params=pltpu.CompilerParams(vmem_limit_bytes=20 * MIB),
        name="time_conv",
    )(in_hbm(clip_starts), in_hbm(shuffle), in_hbm(key_feats), in_hbm(conv_time))
    got_one = exchange(sent_one)

    unit, length, negatives, pulled = pl.pallas_call(
        queue_kernel,
        out_shape=(jax.ShapeDtypeStruct((clips, emb), jnp.float32),) * 4,
        in_specs=[VMEM] * 3,
        out_specs=(VMEM,) * 4,
        compiler_params=pltpu.CompilerParams(vmem_limit_bytes=4 * MIB),
        name="queue_terms",
    )(query_feats, w_query, queue)

    grid_rows = rows // spots
    pitch = grid_rows + 8
    second, sent_two = pl.pallas_call(
        space_conv_kernel,
        out_shape=(jax.ShapeDtypeStruct((part, SPOTS, pitch, LANES), jnp.float32), short),
        in_specs=[VMEM] * 6,
        out_specs=(VMEM, VMEM),
        scratch_shapes=[
            pltpu.VMEM((SIDE, SIDE, grid_rows, inner), jnp.bfloat16),
            pltpu.VMEM((SIDE, SIDE, grid_rows, inner), jnp.float32),
        ],
        compiler_params=pltpu.CompilerParams(vmem_limit_bytes=10 * MIB),
        name="space_conv",
    )(sent_one, got_one, row(gain_one), row(shift_one), first, conv_space)
    got_two = exchange(sent_two)
    second = second.reshape(part, SPOTS * pitch, LANES)

    third, sent = pl.pallas_call(
        expand_kernel,
        out_shape=(
            jax.ShapeDtypeStruct((wide, rows, LANES), jnp.float32),
            jax.ShapeDtypeStruct((devices, 2 * part + wide, LANES), jnp.bfloat16),
        ),
        in_specs=[VMEM] * 6,
        out_specs=(VMEM, VMEM),
        scratch_shapes=[pltpu.VMEM((rows, inner), jnp.bfloat16)],
        compiler_params=pltpu.CompilerParams(vmem_limit_bytes=8 * MIB),
        name="expand",
    )(sent_two, got_two, row(gain_two), row(shift_two), second, conv_expand)
    got_three = exchange(sent)

    own_keys, sent = pl.pallas_call(
        keys_kernel,
        out_shape=(
            jax.ShapeDtypeStruct((clips, emb), jnp.bfloat16),
            jax.ShapeDtypeStruct((devices, clips, emb), jnp.bfloat16),
        ),
        in_specs=[VMEM] * 13,
        out_specs=(VMEM, VMEM),
        scratch_shapes=[pltpu.VMEM((clips, channels), jnp.float32)],
        compiler_params=pltpu.CompilerParams(vmem_limit_bytes=8 * MIB),
        name="keys",
    )(
        sent_one,
        got_one,
        got_three,
        row(gain_three),
        row(shift_three),
        conv_expand,
        third,
        w_key,
        unit,
        length,
        negatives,
        pulled,
        frames,
    )
    all_grads = exchange(sent).reshape(devices * clips, emb)
    query_grad = pl.pallas_call(
        gradient_kernel,
        out_shape=jax.ShapeDtypeStruct((channels, emb), jnp.float32),
        in_specs=[ANY, VMEM],
        out_specs=ANY,
        scratch_shapes=[
            pltpu.VMEM(all_queries.shape, jnp.bfloat16),
            pltpu.VMEM((channels, emb), jnp.float32),
            pltpu.SemaphoreType.DMA((4,)),
            pltpu.SemaphoreType.DMA((4,)),
        ],
        compiler_params=pltpu.CompilerParams(vmem_limit_bytes=12 * MIB),
        name="query_grad",
    )(in_hbm(all_queries), all_grads)
    return (own_keys, query_grad)


def solution(mesh):
    both = ("dp", "bn")
    placed = (
        P(both, None, None, None),
        P(both),
        P("bn", None),
        P(both, None),
    ) + (P(),) * 12
    return jax.shard_map(
        local, mesh=mesh, in_specs=placed, out_specs=(P(both, None), P()), check_vma=False
    )
```

time: 423 us -> 98 us (0.23)
  waiting for transfers between devices: 245 us -> 4.56 us
  blocking collectives: 82.6 us -> 35.6 us
  matrix products: 46 us -> 0 us
  Pallas kernels: 0 us -> 28.2 us
  other arithmetic: 15.7 us -> 0 us
    psum x2 -> x0, waiting for transfers between devices: 245 us -> none  [the longest x1 129 us: local(): query_grad = lax.psum(grad_part, ('dp', 'bn'))]
    psum x2 -> x0, blocking collectives: 82.6 us -> none  [table_moments(): lax.psum((places * jnp.sum(values, axis=(0, 1, 2))[None, :], places * jnp...]
    dot_general x18 -> x0, matrix products: 46 us -> none  [the longest x3 19.6 us: time_conv(): jnp.einsum('afsc,cd->afsd', padded[:, offset:offset + length], weights[of...]
    all_to_all x0 -> x3, blocking collectives: none -> 35.6 us  [exchange(): return lax.all_to_all(message, ('dp', 'bn'), 0, 0)]
    pallas_call x0 -> x6, Pallas kernels: none -> 28.2 us  [the longest x1 10 us: local(): pl.pallas_call(functools.partial(time_conv_kernel, cuts), out_shape=(jax....]
    reduce_sum x3 -> x0, other arithmetic: 10.2 us -> none  [the longest x1 5.82 us: encode(): pooled = jnp.mean(merged, axis=(1, 2)).astype(jnp.bfloat16)]
    gather x1 -> x0, local copies, waits for them, and re-layouts: 5.58 us -> none  [single(): return lax.dynamic_slice_in_dim(clip_feats, first_frame, FRAMES, 0)]
    unnamed x38 -> x32, local copies, waits for them, and re-layouts: 9.35 us -> 12.4 us
  transfers between devices with their start and end apart: 2 -> 2, of which waited for: 2 -> 1; matrix products, arithmetic and copies ran while one was open for 2% -> 0% of each run, Pallas kernels for 0% -> 26%
where the time goes in v2:
time: 98 us; the launch traced here: 97.6 us
  blocking collectives  35.6 us (36%)
  Pallas kernels  28.2 us (29%)
  between operations  14.2 us (14%)
  local copies, waits for them, and re-layouts  12.4 us (13%)
  waiting for transfers between devices  4.56 us (5%)
  starting transfers between devices  2.62 us (3%)
    all_to_all x3, blocking collectives, exchange(): return lax.all_to_all(message, ('dp', 'bn'), 0, 0)  35.6 us
    unnamed x32, local copies, waits for them, and re-layouts  12.4 us
    pallas_call x1, Pallas kernels, local(): pl.pallas_call(functools.partial(time_conv_kernel, cuts), out_shape=(jax....  10 us
    pallas_call x1, Pallas kernels, local(): pl.pallas_call(queue_kernel, out_shape=(jax.ShapeDtypeStruct((clips, emb)...  4.43 us
    pallas_call x1, Pallas kernels, local(): pl.pallas_call(space_conv_kernel, out_shape=(jax.ShapeDtypeStruct((part,...  4.18 us
    all_to_all x1, waiting for transfers between devices, exchange(): return lax.all_to_all(message, ('dp', 'bn'), 0, 0)  3.88 us
    pallas_call x1, Pallas kernels, local(): pl.pallas_call(keys_kernel, out_shape=(jax.ShapeDtypeStruct((clips, emb),...  3.31 us
    pallas_call x1, Pallas kernels, local(): pl.pallas_call(expand_kernel, out_shape=(jax.ShapeDtypeStruct((wide, rows...  3.24 us
  transfers between devices with their start and end apart: 2, of which 1 were waited for; matrix products, arithmetic and copies ran while one was open for 0% of the time, Pallas kernels for 26%

profile of v2, /device:TPU:0, one launch (start us, length us, event | category | flops | bytes accessed | tf_op | source)
XLA Modules:
  0.0 97.6 jit_solution(14186578205462617968)
XLA Ops:
  7.2 0.0 all-gather.2.cloned.1.call-start
  7.2 0.7 all-gather.2.cloned.1.call-update
  7.9 0.0 copy-start.5
  7.9 0.0 copy-start.12
  7.9 0.0 copy-start.13
  7.9 10.0 %time_conv.1 = (f32[4,1024,128]{2,1,0:T(8,128)S(1)}, bf16[8,10,16,2048]{3,2,1,0:T(8,128)(2,1)S(1)}, bf16[32,16,128]{2,1,0:T(8,128)(2,1)S(1)}) custom-call(s32[8]{0:T(128)} %starts_hbm.1, s32[1,8]{1,0:T(1,128)} %shuffle_hbm.1, bf16[8,12,16,2048]{3,2,1,0:T(8,128)(2,1)} %feats.1, bf16[3,2048,512]{2,1,0:T(8,128)(2,1)} %weights.4), custom_call_target="tpu_custom_call" | custom-call | tf_op jit(solution)/shard_map/time_conv/pallas_call | solution.py:412
  18.0 0.0 copy-start.3
  18.0 0.0 copy-start.2
  18.0 0.0 copy-start.14
  18.0 0.0 copy-start.15
  18.0 15.4 %all_to_all.20.got.numbers = bf16[32,16,128]{2,1,0:T(8,128)(2,1)S(1)} all-to-all(bf16[32,16,128]{2,1,0:T(8,128)(2,1)S(1)} %get-tuple-element.15.own.own_numbers), channel_id=1, replica_groups=mesh['dp'=8,'bn'=4] {'dp','bn'}, dimensions={0} | all-to-all | bytes 262144 | tf_op jit(solution)/shard_map/all_to_all | solution.py:378
  33.4 0.0 copy-done.5
  33.4 0.0 copy-done.12
  33.4 0.0 copy-done.13
  33.4 0.0 copy-start.7
  33.4 0.0 copy-start.9
  33.4 4.2 %space_conv.1 = (f32[4,16,72,128]{3,2,1,0:T(8,128)S(1)}, bf16[32,16,128]{2,1,0:T(8,128)(2,1)S(1)}) custom-call(bf16[32,16,128]{2,1,0:T(8,128)(2,1)S(1)} %get-tuple-element.15.own.own_numbers, bf16[32,16,128]{2,1,0:T(8,128)(2,1)S(1)} %all_to_all.20.got.numbers, f32[1,512]{1,0:T(1,128)S(1)} %bitcast.12, f32[1,512]{1,0:T(1,128)S(1)} %bitcast.13, ...), custom_call_target="tpu_custom_call" | custom-call | tf_op jit(solution)/shard_map/space_conv/pallas_call | solution.py:445
  37.6 10.6 %all_to_all.21.got = bf16[32,16,128]{2,1,0:T(8,128)(2,1)S(1)} all-to-all(bf16[32,16,128]{2,1,0:T(8,128)(2,1)S(1)} %get-tuple-element.17.own), channel_id=1, replica_groups=mesh['dp'=8,'bn'=4] {'dp','bn'}, dimensions={0} | all-to-all | bytes 262144 | tf_op jit(solution)/shard_map/all_to_all | solution.py:378
  48.2 0.0 copy-done.2
  48.2 0.0 copy-done.14
  48.2 0.0 copy-done.15
  48.2 0.0 copy-start.10
  48.2 0.0 copy-start.11
  48.2 3.2 %expand.1 = (f32[16,1024,128]{2,1,0:T(8,128)S(1)}, bf16[32,24,128]{2,1,0:T(8,128)(2,1)}) custom-call(bf16[32,16,128]{2,1,0:T(8,128)(2,1)S(1)} %get-tuple-element.17.own, bf16[32,16,128]{2,1,0:T(8,128)(2,1)S(1)} %all_to_all.21.got, f32[1,512]{1,0:T(1,128)S(1)} %bitcast.14, f32[1,512]{1,0:T(1,128)S(1)} %bitcast.15, f32[4,1152,128]{2,1,0:T(8,128)S(1)} %bitcast.8, ...), custom_call_target="tpu_custom_call" | custom-call | tf_op jit(solution)/shard_map/expand/pallas_call | solution.py:460
  51.5 0.0 copy-done.3
  51.5 0.0 copy-start
  51.5 3.3 %copy-done = f32[16,1024,128]{2,1,0:T(8,128)} copy-done((f32[16,1024,128]{2,1,0:T(8,128)}, f32[16,1024,128]{2,1,0:T(8,128)S(1)}, u32[]{:S(2)}) %copy-start) | copy-done | bytes 8388632
  54.7 2.6 %all-to-all-start.2 = ((bf16[32,24,128]{2,1,0:T(8,128)(2,1)}), bf16[32,24,128]{2,1,0:T(8,128)(2,1)S(1)}, u32[]{:S(2)}, u32[]{:S(2)}) async-start(bf16[32,24,128]{2,1,0:T(8,128)(2,1)} %get-tuple-element.19), calls=%async_computation.2 | async-start | bytes 393216 | tf_op jit(solution)/shard_map/all_to_all | solution.py:378
  57.3 0.0 copy-done.7
  57.3 0.0 copy-done.9
  57.3 0.0 copy-start.6
  57.3 2.2 %copy-done.6 = bf16[16384,128]{1,0:T(8,128)(2,1)S(1)} copy-done((bf16[16384,128]{1,0:T(8,128)(2,1)S(1)}, bf16[16384,128]{1,0:T(8,128)(2,1)}, u32[]{:S(2)}) %copy-start.6) | copy-done | bytes 4194328
  59.5 4.4 %queue_terms.1 = (f32[8,128]{1,0:T(8,128)S(1)}, f32[8,128]{1,0:T(8,128)S(1)}, f32[8,128]{1,0:T(8,128)S(1)}, f32[8,128]{1,0:T(8,128)S(1)}) custom-call(bf16[8,2048]{1,0:T(8,128)(2,1)S(1)} %copy-done.9, bf16[2048,128]{1,0:T(8,128)(2,1)S(1)} %copy-done.7, bf16[16384,128]{1,0:T(8,128)(2,1)S(1)} %copy-done.6), custom_call_target="tpu_custom_call" | custom-call | tf_op jit(solution)/shard_map/queue_terms/pallas_call | solution.py:434
  64.0 3.9 %all-to-all-done.2.got = bf16[32,24,128]{2,1,0:T(8,128)(2,1)S(1)} async-done(((bf16[32,24,128]{2,1,0:T(8,128)(2,1)}), bf16[32,24,128]{2,1,0:T(8,128)(2,1)S(1)}, u32[]{:S(2)}, u32[]{:S(2)}) %all-to-all-start.2) | async-done | bytes 196640 | tf_op jit(solution)/shard_map/all_to_all | solution.py:378
  67.9 0.0 copy-done.10
  67.9 0.0 copy-done.11
  67.9 0.0 copy-start.1
  67.9 3.4 %copy-done.1 = f32[16,1024,128]{2,1,0:T(8,128)S(1)} copy-done((f32[16,1024,128]{2,1,0:T(8,128)S(1)}, f32[16,1024,128]{2,1,0:T(8,128)}, u32[]{:S(2)}) %copy-start.1) | copy-done | bytes 8388632
  71.2 0.0 copy-start.4
  71.2 2.5 %copy-done.4 = bf16[8,10,16,2048]{3,2,1,0:T(8,128)(2,1)S(1)} copy-done((bf16[8,10,16,2048]{3,2,1,0:T(8,128)(2,1)S(1)}, bf16[8,10,16,2048]{3,2,1,0:T(8,128)(2,1)}, u32[]{:S(2)}) %copy-start.4) | copy-done | bytes 5242904
  73.7 0.0 copy-start.8
  73.7 1.0 %copy-done.8 = bf16[2048,128]{1,0:T(8,128)(2,1)S(1)} copy-done((bf16[2048,128]{1,0:T(8,128)(2,1)S(1)}, bf16[2048,128]{1,0:T(8,128)(2,1)}, u32[]{:S(2)}) %copy-start.8) | copy-done | bytes 524312
  74.8 3.3 %keys.1 = (bf16[8,128]{1,0:T(8,128)(2,1)}, bf16[32,8,128]{2,1,0:T(8,128)(2,1)S(1)}) custom-call(bf16[32,16,128]{2,1,0:T(8,128)(2,1)S(1)} %get-tuple-element.15.own.own_numbers, bf16[32,16,128]{2,1,0:T(8,128)(2,1)S(1)} %all_to_all.20.got.numbers, bf16[32,24,128]{2,1,0:T(8,128)(2,1)S(1)} %all-to-all-done.2.got, f32[1,2048]{1,0:T(1,128)S(1)} %bitcast.10, ...), custom_call_target="tpu_custom_call" | custom-call | tf_op jit(solution)/shard_map/keys/pallas_call | solution.py:474
  78.1 9.6 %all_to_all.22 = bf16[32,8,128]{2,1,0:T(8,128)(2,1)S(1)} all-to-all(bf16[32,8,128]{2,1,0:T(8,128)(2,1)S(1)} %get-tuple-element.27), channel_id=1, replica_groups=mesh['dp'=8,'bn'=4] {'dp','bn'}, dimensions={0} | all-to-all | bytes 131072 | tf_op jit(solution)/shard_map/all_to_all | solution.py:378
  87.7 0.0 all-gather.2.cloned.1.call-done.queries_hbm
  87.7 3.0 %query_grad.1 = f32[2048,128]{1,0:T(8,128)} custom-call(bf16[256,2048]{1,0:T(8,128)(2,1)} %all-gather.2.cloned.1.call-done.queries_hbm, bf16[256,128]{1,0:T(8,128)(2,1)S(1)} %bitcast.9), custom_call_target="tpu_custom_call" | custom-call | tf_op jit(solution)/shard_map/query_grad/pallas_call | solution.py:501
Async XLA Ops:
  7.2 80.6 %all-gather.2.cloned.1.call-start = ((), (), s32[]{:S(2)}) async-start(), calls=%async_computation.4 | async-start | bytes 1081344 | tf_op jit(solution)/shard_map/all_gather | solution.py:407
  7.9 25.5 %copy-start.5 = (bf16[9,512,512]{2,1,0:T(8,128)(2,1)S(1)}, bf16[9,512,512]{2,1,0:T(8,128)(2,1)}, u32[]{:S(2)}) copy-start(bf16[9,512,512]{2,1,0:T(8,128)(2,1)} %weights.5) | copy-start | bytes 14155780
  7.9 25.5 %copy-start.12 = (f32[512]{0:T(512)S(1)}, f32[512]{0:T(512)}, u32[]{:S(2)}) copy-start(f32[512]{0:T(512)} %param.23) | copy-start | bytes 6148
  7.9 25.5 %copy-start.13 = (f32[512]{0:T(512)S(1)}, f32[512]{0:T(512)}, u32[]{:S(2)}) copy-start(f32[512]{0:T(512)} %param.24) | copy-start | bytes 6148
  18.0 33.5 %copy-start.3 = (bf16[8,10,16,2048]{3,2,1,0:T(8,128)(2,1)}, bf16[8,10,16,2048]{3,2,1,0:T(8,128)(2,1)S(1)}, u32[]{:S(2)}) copy-start(bf16[8,10,16,2048]{3,2,1,0:T(8,128)(2,1)S(1)} %get-tuple-element.25.frames) | copy-start | bytes 15728644
  18.0 30.2 %copy-start.2 = (bf16[512,2048]{1,0:T(8,128)(2,1)S(1)}, bf16[512,2048]{1,0:T(8,128)(2,1)}, u32[]{:S(2)}) copy-start(bf16[512,2048]{1,0:T(8,128)(2,1)} %weights.7) | copy-start | bytes 6291460
  18.0 30.2 %copy-start.14 = (f32[512]{0:T(512)S(1)}, f32[512]{0:T(512)}, u32[]{:S(2)}) copy-start(f32[512]{0:T(512)} %param.25) | copy-start | bytes 6148
  18.0 30.2 %copy-start.15 = (f32[512]{0:T(512)S(1)}, f32[512]{0:T(512)}, u32[]{:S(2)}) copy-start(f32[512]{0:T(512)} %param.26) | copy-start | bytes 6148
  33.4 23.9 %copy-start.7 = (bf16[2048,128]{1,0:T(8,128)(2,1)S(1)}, bf16[2048,128]{1,0:T(8,128)(2,1)}, u32[]{:S(2)}) copy-start(bf16[2048,128]{1,0:T(8,128)(2,1)} %w_query.1) | copy-start | bytes 1572868
  33.4 23.9 %copy-start.9 = (bf16[8,2048]{1,0:T(8,128)(2,1)S(1)}, bf16[8,2048]{1,0:T(8,128)(2,1)}, u32[]{:S(2)}) copy-start(bf16[8,2048]{1,0:T(8,128)(2,1)} %query_feats.1) | copy-start | bytes 98308
  48.2 19.7 %copy-start.10 = (f32[2048]{0:T(1024)S(1)}, f32[2048]{0:T(1024)}, u32[]{:S(2)}) copy-start(f32[2048]{0:T(1024)} %param.27) | copy-start | bytes 24580
  48.2 19.7 %copy-start.11 = (f32[2048]{0:T(1024)S(1)}, f32[2048]{0:T(1024)}, u32[]{:S(2)}) copy-start(f32[2048]{0:T(1024)} %param.28) | copy-start | bytes 24580
  51.5 3.3 %copy-start = (f32[16,1024,128]{2,1,0:T(8,128)}, f32[16,1024,128]{2,1,0:T(8,128)S(1)}, u32[]{:S(2)}) copy-start(f32[16,1024,128]{2,1,0:T(8,128)S(1)} %get-tuple-element.20.third) | copy-start | bytes 25165828
  54.7 13.1 %all-to-all-start.2 = ((bf16[32,24,128]{2,1,0:T(8,128)(2,1)}), bf16[32,24,128]{2,1,0:T(8,128)(2,1)S(1)}, u32[]{:S(2)}, u32[]{:S(2)}) async-start(bf16[32,24,128]{2,1,0:T(8,128)(2,1)} %get-tuple-element.19), calls=%async_computation.2 | async-start | bytes 393216 | tf_op jit(solution)/shard_map/all_to_all | solution.py:378
  57.3 2.2 %copy-start.6 = (bf16[16384,128]{1,0:T(8,128)(2,1)S(1)}, bf16[16384,128]{1,0:T(8,128)(2,1)}, u32[]{:S(2)}) copy-start(bf16[16384,128]{1,0:T(8,128)(2,1)} %queue.1) | copy-start | bytes 12582916
  67.9 3.4 %copy-start.1 = (f32[16,1024,128]{2,1,0:T(8,128)S(1)}, f32[16,1024,128]{2,1,0:T(8,128)}, u32[]{:S(2)}) copy-start(f32[16,1024,128]{2,1,0:T(8,128)} %copy-done) | copy-start | bytes 25165828
  71.2 2.5 %copy-start.4 = (bf16[8,10,16,2048]{3,2,1,0:T(8,128)(2,1)S(1)}, bf16[8,10,16,2048]{3,2,1,0:T(8,128)(2,1)}, u32[]{:S(2)}) copy-start(bf16[8,10,16,2048]{3,2,1,0:T(8,128)(2,1)} %copy-done.3) | copy-start | bytes 15728644
  73.7 1.0 %copy-start.8 = (bf16[2048,128]{1,0:T(8,128)(2,1)S(1)}, bf16[2048,128]{1,0:T(8,128)(2,1)}, u32[]{:S(2)}) copy-start(bf16[2048,128]{1,0:T(8,128)(2,1)} %w_key.1) | copy-start | bytes 1572868
Sparse Core Ops, SparseCore 0:
  10.9 57.2 all-gather.1

commit v3 on v2

--- a/solution.py
+++ b/solution.py
@@ -14,6 +14,8 @@
 SHARPNESS_DIVISOR = 0.2
 EPSILON = 1e-05
 MIB = 1 << 20
+MOMENT_ROWS = 16
+QUERY_ROWS = 16
 
 VMEM = pl.BlockSpec(memory_space=pltpu.VMEM)
 ANY = pl.BlockSpec(memory_space=pl.ANY)
@@ -33,6 +35,23 @@
     )
 
 
+def write_queries(message, query_feats, piece):
+    half = query_feats.shape[1] // 2
+    parts = []
+    for side in range(2):
+        at = side * half + piece * 2 * LANES
+        parts.append(
+            jnp.concatenate(
+                [query_feats[:, at : at + LANES], query_feats[:, at + LANES : at + 2 * LANES]],
+                axis=0,
+            )
+        )
+    pair = jnp.stack(parts)
+    devices, length, _ = message.shape
+    every = jnp.broadcast_to(pair[None], (devices // 2,) + pair.shape)
+    message[:, length - pair.shape[1] :, :] = every.reshape((devices,) + pair.shape[1:])
+
+
 def two_halves(values):
     high = values.astype(jnp.bfloat16).astype(jnp.float32)
     return high, values - high
@@ -46,10 +65,10 @@
 def write_moments(message, mean, var, group):
     high, low = two_halves(mean)
     part = [as_block(high), as_block(low), as_block(var)]
-    rest = message.shape[1] - sum(p.shape[0] for p in part)
+    rest = MOMENT_ROWS - sum(p.shape[0] for p in part)
     part.append(jnp.broadcast_to(group, (rest, LANES)))
     block = jnp.concatenate(part, axis=0).astype(jnp.bfloat16)
-    message[...] = jnp.broadcast_to(block[None], message.shape)
+    message[:, :MOMENT_ROWS, :] = jnp.broadcast_to(block[None], (message.shape[0],) + block.shape)
 
 
 def group_row(message, part):
@@ -64,7 +83,7 @@
 def group_scale_and_bias(message, group, gain, shift):
     part = gain.shape[1] // LANES
     same = members(message, group, part)
-    every = message[...].astype(jnp.float32)
+    every = message[:, :MOMENT_ROWS, :].astype(jnp.float32)
     block_mean = every[:, :part] + every[:, part : 2 * part]
     block_var = every[:, 2 * part : 3 * part]
     blocks = jnp.sum(same, axis=0)
@@ -81,11 +100,13 @@
     shuffle_hbm,
     feats,
     weights,
+    queries_hbm,
     first,
     frames,
     message,
     starts,
     shuffle,
+    query_feats,
     taps,
     small_sem,
     frames_sem,
@@ -111,6 +132,7 @@
 
     copy_starts = pltpu.make_async_copy(starts_hbm, starts, small_sem.at[0])
     copy_shuffle = pltpu.make_async_copy(shuffle_hbm, shuffle, small_sem.at[1])
+    copy_queries = pltpu.make_async_copy(queries_hbm, query_feats, small_sem.at[2])
     copy_starts.start()
     copy_shuffle.start()
     copy_taps(0).start()
@@ -120,6 +142,7 @@
             copy_clip(k, n).start()
         if k + 1 < pieces:
             copy_taps(k + 1).start()
+    copy_queries.start()
     blank = jnp.zeros((clips, 1) + frames.shape[2:], jnp.bfloat16)
     frames[:, 0:1] = blank
     frames[:, FRAMES + 1 : FRAMES + 2] = blank
@@ -157,9 +180,13 @@
     copy_shuffle.wait()
     group = shuffle[0, lax.axis_index("dp")].astype(jnp.float32)
     write_moments(message, mean, var, jnp.full((1, LANES), group, jnp.float32))
-
-
-def space_conv_kernel(own, got, gain, shift, first, weights, second, message, act, taken):
+    copy_queries.wait()
+    write_queries(message, query_feats, 0)
+
+
+def space_conv_kernel(
+    own, got, gain, shift, first, weights, query_feats, second, message, act, taken
+):
     inner = weights.shape[1]
     part = inner // LANES
     rows = first.shape[1] // SPOTS
@@ -197,9 +224,10 @@
             squares = squares + jnp.sum(values * values, axis=0, keepdims=True)
     mean, var = mean_and_var(total, squares, rows * SPOTS)
     write_moments(message, mean, var, number)
-
-
-def expand_kernel(own, got, gain, shift, second, weights, third, message, act):
+    write_queries(message, query_feats, 1)
+
+
+def expand_kernel(own, got, gain, shift, second, weights, query_feats, third, message, act):
     inner, channels = weights.shape
     rows = act.shape[0]
     part = inner // LANES
@@ -228,7 +256,11 @@
         found.append(mean_and_var(total, squares, rows)[1])
     var = jnp.concatenate(found, axis=1)
     block = jnp.concatenate([as_block(high), as_block(low), as_block(var)], axis=0)
-    message[...] = jnp.broadcast_to(block.astype(jnp.bfloat16)[None], message.shape)
+    block = block.astype(jnp.bfloat16)
+    message[:, : block.shape[0], :] = jnp.broadcast_to(
+        block[None], (message.shape[0],) + block.shape
+    )
+    write_queries(message, query_feats, 2)
 
 
 def keys_kernel(
@@ -245,6 +277,7 @@
     negatives,
     pulled,
     frames,
+    query_feats,
     keys,
     message,
     pooled,
@@ -304,7 +337,8 @@
     grad = (pulled[...] / partition + (positive / partition - 1.0) * own) / SHARPNESS_DIVISOR
     radial = jnp.sum(direction * grad, axis=-1, keepdims=True)
     grad = ((grad - radial * direction) / length[...]).astype(jnp.bfloat16)
-    message[...] = jnp.broadcast_to(grad[None], message.shape)
+    message[:, :clips, :] = jnp.broadcast_to(grad[None], (message.shape[0],) + grad.shape)
+    write_queries(message, query_feats, 3)
 
 
 def queue_kernel(query_feats, w_query, queue, unit, length, negatives, pulled):
@@ -315,63 +349,44 @@
     length[...] = jnp.broadcast_to(norm, length.shape)
     rounded = direction.astype(jnp.bfloat16)
     rows, width = rounded.shape
-    ones = jnp.ones((rows, width), jnp.bfloat16)
-    across = (((1,), (1,)), ((), ()))
-    step = queue.shape[0] // 8
-
-    def one_step(i, carry):
-        total, weighted = carry
-        entries = queue[pl.ds(i * step, step), :]
-        squares = lax.dot_general(
-            ones, entries * entries, across, preferred_element_type=jnp.float32
-        )
-        inverse = lax.rsqrt(squares + 1e-06)
-        scores = lax.dot_general(rounded, entries, across, preferred_element_type=jnp.float32)
-        weight = jnp.exp(scores * inverse / SHARPNESS_DIVISOR)
+    none, ones = jnp.zeros((rows, width), jnp.bfloat16), jnp.ones((rows, width), jnp.bfloat16)
+    both = jnp.concatenate(
+        [jnp.concatenate([rounded, none], axis=1), jnp.concatenate([none, ones], axis=1)], axis=0
+    )
+    pieces = 8
+    step = queue.shape[0] // pieces
+    total = jnp.zeros((rows, 1), jnp.float32)
+    weighted = jnp.zeros((rows, width), jnp.float32)
+    for i in range(pieces):
+        entries = queue[i * step : (i + 1) * step, :]
+        products = lax.dot_general(
+            both,
+            jnp.concatenate([entries, entries * entries], axis=1),
+            (((1,), (1,)), ((), ())),
+            preferred_element_type=jnp.float32,
+        )
+        inverse = lax.rsqrt(products[rows:] + 1e-06)
+        weight = jnp.exp(products[:rows] * inverse / SHARPNESS_DIVISOR)
         total = total + jnp.sum(weight, axis=-1, keepdims=True)
         weighted = weighted + jnp.dot(
             (weight * inverse).astype(jnp.bfloat16), entries, preferred_element_type=jnp.float32
         )
-        return total, weighted
-
-    total, weighted = lax.fori_loop(
-        0,
-        8,
-        one_step,
-        (jnp.zeros((rows, 1), jnp.float32), jnp.zeros((rows, width), jnp.float32)),
-    )
     negatives[...] = jnp.broadcast_to(total, negatives.shape)
     pulled[...] = weighted
 
 
-def gradient_kernel(queries_hbm, grads, out_hbm, queries, out, queries_sem, out_sem):
-    channels = out.shape[0]
-    width = channels // queries_sem.shape[0]
-
-    def fetch(i):
-        span = pl.ds(i * width, width)
-        return pltpu.make_async_copy(
-            queries_hbm.at[:, span], queries.at[:, span], queries_sem.at[i]
-        )
-
-    def give(i):
-        span = pl.ds(i * width, width)
-        return pltpu.make_async_copy(out.at[span], out_hbm.at[span], out_sem.at[i])
-
-    pieces = channels // width
-    for i in range(pieces):
-        fetch(i).start()
-    for i in range(pieces):
-        fetch(i).wait()
-        out[i * width : (i + 1) * width] = lax.dot_general(
-            queries[:, i * width : (i + 1) * width],
-            grads[...],
-            (((0,), (0,)), ((), ())),
-            preferred_element_type=jnp.float32,
-        )
-        give(i).start()
-    for i in range(pieces):
-        give(i).wait()
+def gradient_kernel(one, two, three, four, out):
+    devices, _, width = four.shape
+    clips = QUERY_ROWS // 2
+    grads = four[:, :clips, :].reshape(devices * clips, width)
+    for i, message in enumerate((one, two, three, four)):
+        for j in range(2):
+            at = message.shape[1] - QUERY_ROWS + j * clips
+            queries = message[:, at : at + clips, :].reshape(devices * clips, LANES)
+            start = (2 * i + j) * LANES
+            out[start : start + LANES] = lax.dot_general(
+                queries, grads, (((0,), (0,)), ((), ())), preferred_element_type=jnp.float32
+            )
 
 
 def exchange(message):
@@ -401,10 +416,8 @@
     inner, emb = conv_space.shape[1], queue.shape[1]
     part, wide = inner // LANES, channels // LANES
     rows = clips * FRAMES * spots
-    short = jax.ShapeDtypeStruct((devices, 16, LANES), jnp.bfloat16)
+    short = jax.ShapeDtypeStruct((devices, MOMENT_ROWS + QUERY_ROWS, LANES), jnp.bfloat16)
     row = lambda vector: vector.reshape(1, -1)
-
-    all_queries = lax.all_gather(query_feats, ("dp", "bn"), tiled=True)
 
     cuts = (0, channels // 8, 3 * channels // 8, channels)
     pieces = len(cuts) - 1
@@ -416,21 +429,27 @@
             jax.ShapeDtypeStruct(padded, jnp.bfloat16),
             short,
         ),
-        in_specs=[ANY] * 4,
+        in_specs=[ANY] * 5,
         out_specs=(VMEM,) * 3,
         scratch_shapes=[
             pltpu.SMEM(clip_starts.shape, jnp.int32),
             pltpu.SMEM(shuffle.shape, jnp.int32),
+            pltpu.VMEM(query_feats.shape, jnp.bfloat16),
             pltpu.VMEM(conv_time.shape, jnp.bfloat16),
-            pltpu.SemaphoreType.DMA((2,)),
+            pltpu.SemaphoreType.DMA((3,)),
             pltpu.SemaphoreType.DMA((pieces, clips)),
             pltpu.SemaphoreType.DMA((pieces,)),
         ],
         compiler_params=pltpu.CompilerParams(vmem_limit_bytes=20 * MIB),
         name="time_conv",
-    )(in_hbm(clip_starts), in_hbm(shuffle), in_hbm(key_feats), in_hbm(conv_time))
-    got_one = exchange(sent_one)
-
+    )(
+        in_hbm(clip_starts),
+        in_hbm(shuffle),
+        in_hbm(key_feats),
+        in_hbm(conv_time),
+        in_hbm(query_feats),
+    )
+    late_queries, sent_one = lax.optimization_barrier((query_feats, sent_one))
     unit, length, negatives, pulled = pl.pallas_call(
         queue_kernel,
         out_shape=(jax.ShapeDtypeStruct((clips, emb), jnp.float32),) * 4,
@@ -438,14 +457,18 @@
         out_specs=(VMEM,) * 4,
         compiler_params=pltpu.CompilerParams(vmem_limit_bytes=4 * MIB),
         name="queue_terms",
-    )(query_feats, w_query, queue)
+    )(late_queries, w_query, queue)
+    sent_one, unit, length, negatives, pulled = lax.optimization_barrier(
+        (sent_one, unit, length, negatives, pulled)
+    )
+    got_one = exchange(sent_one)
 
     grid_rows = rows // spots
     pitch = grid_rows + 8
     second, sent_two = pl.pallas_call(
         space_conv_kernel,
         out_shape=(jax.ShapeDtypeStruct((part, SPOTS, pitch, LANES), jnp.float32), short),
-        in_specs=[VMEM] * 6,
+        in_specs=[VMEM] * 7,
         out_specs=(VMEM, VMEM),
         scratch_shapes=[
             pltpu.VMEM((SIDE, SIDE, grid_rows, inner), jnp.bfloat16),
@@ -453,7 +476,7 @@
         ],
         compiler_params=pltpu.CompilerParams(vmem_limit_bytes=10 * MIB),
         name="space_conv",
-    )(sent_one, got_one, row(gain_one), row(shift_one), first, conv_space)
+    )(sent_one, got_one, row(gain_one), row(shift_one), first, conv_space, query_feats)
     got_two = exchange(sent_two)
     second = second.reshape(part, SPOTS * pitch, LANES)
 
@@ -461,23 +484,23 @@
         expand_kernel,
         out_shape=(
             jax.ShapeDtypeStruct((wide, rows, LANES), jnp.float32),
-            jax.ShapeDtypeStruct((devices, 2 * part + wide, LANES), jnp.bfloat16),
+            jax.ShapeDtypeStruct((devices, 2 * part + wide + QUERY_ROWS, LANES), jnp.bfloat16),
         ),
-        in_specs=[VMEM] * 6,
+        in_specs=[VMEM] * 7,
         out_specs=(VMEM, VMEM),
         scratch_shapes=[pltpu.VMEM((rows, inner), jnp.bfloat16)],
         compiler_params=pltpu.CompilerParams(vmem_limit_bytes=8 * MIB),
         name="expand",
-    )(sent_two, got_two, row(gain_two), row(shift_two), second, conv_expand)
+    )(sent_two, got_two, row(gain_two), row(shift_two), second, conv_expand, query_feats)
     got_three = exchange(sent)
 
     own_keys, sent = pl.pallas_call(
         keys_kernel,
         out_shape=(
             jax.ShapeDtypeStruct((clips, emb), jnp.bfloat16),
-            jax.ShapeDtypeStruct((devices, clips, emb), jnp.bfloat16),
+            jax.ShapeDtypeStruct((devices, clips + QUERY_ROWS, emb), jnp.bfloat16),
         ),
-        in_specs=[VMEM] * 13,
+        in_specs=[VMEM] * 14,
         out_specs=(VMEM, VMEM),
         scratch_shapes=[pltpu.VMEM((clips, channels), jnp.float32)],
         compiler_params=pltpu.CompilerParams(vmem_limit_bytes=8 * MIB),
@@ -496,22 +519,23 @@
         negatives,
         pulled,
         frames,
-    )
-    all_grads = exchange(sent).reshape(devices * clips, emb)
-    query_grad = pl.pallas_call(
+        query_feats,
+    )
+    got_four = exchange(sent)
+    own_half = pl.pallas_call(
         gradient_kernel,
-        out_shape=jax.ShapeDtypeStruct((channels, emb), jnp.float32),
-        in_specs=[ANY, VMEM],
-        out_specs=ANY,
-        scratch_shapes=[
-            pltpu.VMEM(all_queries.shape, jnp.bfloat16),
-            pltpu.VMEM((channels, emb), jnp.float32),
-            pltpu.SemaphoreType.DMA((4,)),
-            pltpu.SemaphoreType.DMA((4,)),
-        ],
-        compiler_params=pltpu.CompilerParams(vmem_limit_bytes=12 * MIB),
+        out_shape=jax.ShapeDtypeStruct((channels // 2, emb), jnp.float32),
+        in_specs=[VMEM] * 4,
+        out_specs=VMEM,
+        compiler_params=pltpu.CompilerParams(vmem_limit_bytes=6 * MIB),
         name="query_grad",
-    )(in_hbm(all_queries), all_grads)
+    )(got_one, got_two, got_three, got_four)
+    members_bn = lax.axis_size("bn")
+    other_half = lax.ppermute(own_half, "bn", [(i, i ^ 1) for i in range(members_bn)])
+    odd = lax.axis_index("bn") % 2 == 1
+    query_grad = jnp.concatenate(
+        [jnp.where(odd, other_half, own_half), jnp.where(odd, own_half, other_half)], axis=0
+    )
     return (own_keys, query_grad)
 
 

time: 98 us -> 84.5 us (0.86)
  blocking collectives: 35.6 us -> 55.8 us
  between operations: 14.2 us -> 0.79 us
  local copies, waits for them, and re-layouts: 12.4 us -> 0.07 us
  Pallas kernels: 28.2 us -> 24.3 us
  waiting for transfers between devices: 4.56 us -> 1.54 us
  starting transfers between devices: 2.62 us -> 0.66 us
  other arithmetic: 0 us -> 1.11 us
    all_to_all x3 -> x4, blocking collectives: 35.6 us -> 55.8 us  [exchange(): return lax.all_to_all(message, ('dp', 'bn'), 0, 0)]
    unnamed x32 -> x24, local copies, waits for them, and re-layouts: 12.4 us -> 0.07 us
    all_to_all x1 -> x0, waiting for transfers between devices: 3.88 us -> none  [exchange(): return lax.all_to_all(message, ('dp', 'bn'), 0, 0)]
    pallas_call x1, Pallas kernels: 2.95 us -> 0.35 us  [local(): pl.pallas_call(gradient_kernel, out_shape=jax.ShapeDtypeStruct((channels...]
    all_to_all x1 -> x0, starting transfers between devices: 2.58 us -> none  [exchange(): return lax.all_to_all(message, ('dp', 'bn'), 0, 0)]
    ppermute x0 -> x1, waiting for transfers between devices: none -> 1.54 us  [local(): lax.ppermute(own_half, 'bn', [(i, i ^ 1) for i in range(members_bn)])]
    concatenate x0 -> x1, other arithmetic: none -> 1.04 us  [local(): jnp.concatenate([jnp.where(odd, other_half, own_half), jnp.where(odd, own...]
  transfers between devices with their start and end apart: 2 -> 1, of which waited for: 1 -> 1; matrix products, arithmetic and copies ran while one was open for 0% -> 0% of each run, Pallas kernels for 26% -> 0%
where the time goes in v3:
time: 84.5 us; the launch traced here: 84.3 us
  blocking collectives  55.8 us (66%)
  Pallas kernels  24.3 us (29%)
  waiting for transfers between devices  1.54 us (2%)
  other arithmetic  1.11 us (1%)
    all_to_all x4, blocking collectives, exchange(): return lax.all_to_all(message, ('dp', 'bn'), 0, 0)  55.8 us
    pallas_call x1, Pallas kernels, local(): pl.pallas_call(functools.partial(time_conv_kernel, cuts), out_shape=(jax....  10.3 us
    pallas_call x1, Pallas kernels, local(): pl.pallas_call(space_conv_kernel, out_shape=(jax.ShapeDtypeStruct((part,...  4.19 us
    pallas_call x1, Pallas kernels, local(): pl.pallas_call(queue_kernel, out_shape=(jax.ShapeDtypeStruct((clips, emb)...  3.51 us
    pallas_call x1, Pallas kernels, local(): pl.pallas_call(keys_kernel, out_shape=(jax.ShapeDtypeStruct((clips, emb),...  3.34 us
    pallas_call x1, Pallas kernels, local(): pl.pallas_call(expand_kernel, out_shape=(jax.ShapeDtypeStruct((wide, rows...  2.58 us
  transfers between devices with their start and end apart: 1, of which 1 were waited for; matrix products, arithmetic and copies ran while one was open for 0% of the time, Pallas kernels for 0%

profile of v3, /device:TPU:0, one launch (start us, length us, event | category | flops | bytes accessed | tf_op | source)
XLA Modules:
  0.0 84.3 jit_solution(11238522685340794818)
XLA Ops:
  0.6 0.0 copy-start.3
  0.6 0.0 copy-start.4
  0.7 0.0 copy-start.2
  0.7 10.3 %time_conv.1 = (f32[4,1024,128]{2,1,0:T(8,128)S(1)}, bf16[8,10,16,2048]{3,2,1,0:T(8,128)(2,1)S(1)}, bf16[32,32,128]{2,1,0:T(8,128)(2,1)S(1)}) custom-call(s32[8]{0:T(128)} %starts_hbm.1, s32[1,8]{1,0:T(1,128)} %shuffle_hbm.1, bf16[8,12,16,2048]{3,2,1,0:T(8,128)(2,1)} %feats.1, bf16[3,2048,512]{2,1,0:T(8,128)(2,1)} %weights.4, bf16[8,2048]{1,0:T(8,128)(2,1)} %query_feats.6), custom_call_target="tpu_custom_call" | custom-call | tf_op jit(solution)/shard_map/time_conv/pallas_call | solution.py:425
  11.0 0.0 copy-start.1
  11.0 0.0 copy-start.8
  11.0 0.0 copy-start.9
  11.0 0.0 copy-done.3
  11.0 0.0 copy-done.4
  11.0 0.0 copy-done.2
  11.1 3.5 %queue_terms.1 = (f32[8,128]{1,0:T(8,128)S(1)}, f32[8,128]{1,0:T(8,128)S(1)}, f32[8,128]{1,0:T(8,128)S(1)}, f32[8,128]{1,0:T(8,128)S(1)}) custom-call(bf16[8,2048]{1,0:T(8,128)(2,1)S(1)} %copy-done.3, bf16[2048,128]{1,0:T(8,128)(2,1)S(1)} %copy-done.4, bf16[16384,128]{1,0:T(8,128)(2,1)S(1)} %copy-done.2), custom_call_target="tpu_custom_call" | custom-call | tf_op jit(solution)/shard_map/queue_terms/pallas_call | solution.py:453
  14.6 0.0 copy-start
  14.6 0.0 copy-start.10
  14.6 0.0 copy-start.11
  14.6 17.7 %all_to_all.20.got.numbers.one = bf16[32,32,128]{2,1,0:T(8,128)(2,1)S(1)} all-to-all(bf16[32,32,128]{2,1,0:T(8,128)(2,1)S(1)} %get-tuple-element.29.own.own_numbers), channel_id=1, replica_groups=mesh['dp'=8,'bn'=4] {'dp','bn'}, dimensions={0} | all-to-all | bytes 524288 | tf_op jit(solution)/shard_map/all_to_all | solution.py:393
  32.3 0.0 copy-done.1
  32.3 0.0 copy-done.8
  32.3 0.0 copy-done.9
  32.3 4.2 %space_conv.1 = (f32[4,16,72,128]{3,2,1,0:T(8,128)S(1)}, bf16[32,32,128]{2,1,0:T(8,128)(2,1)S(1)}) custom-call(bf16[32,32,128]{2,1,0:T(8,128)(2,1)S(1)} %get-tuple-element.29.own.own_numbers, bf16[32,32,128]{2,1,0:T(8,128)(2,1)S(1)} %all_to_all.20.got.numbers.one, f32[1,512]{1,0:T(1,128)S(1)} %bitcast.10, f32[1,512]{1,0:T(1,128)S(1)} %bitcast.11, ...), custom_call_target="tpu_custom_call" | custom-call | tf_op jit(solution)/shard_map/space_conv/pallas_call | solution.py:468
  36.5 0.0 copy-start.5
  36.5 0.0 copy-start.6
  36.5 0.0 copy-start.7
  36.5 12.8 %all_to_all.21.got.two = bf16[32,32,128]{2,1,0:T(8,128)(2,1)S(1)} all-to-all(bf16[32,32,128]{2,1,0:T(8,128)(2,1)S(1)} %get-tuple-element.31.own), channel_id=1, replica_groups=mesh['dp'=8,'bn'=4] {'dp','bn'}, dimensions={0} | all-to-all | bytes 524288 | tf_op jit(solution)/shard_map/all_to_all | solution.py:393
  49.3 0.0 copy-done
  49.3 0.0 copy-done.10
  49.3 0.0 copy-done.11
  49.4 2.6 %expand.1 = (f32[16,1024,128]{2,1,0:T(8,128)S(1)}, bf16[32,40,128]{2,1,0:T(8,128)(2,1)S(1)}) custom-call(bf16[32,32,128]{2,1,0:T(8,128)(2,1)S(1)} %get-tuple-element.31.own, bf16[32,32,128]{2,1,0:T(8,128)(2,1)S(1)} %all_to_all.21.got.two, f32[1,512]{1,0:T(1,128)S(1)} %bitcast.12, f32[1,512]{1,0:T(1,128)S(1)} %bitcast.13, f32[4,1152,128]{2,1,0:T(8,128)S(1)} %bitcast.7, ...), custom_call_target="tpu_custom_call" | custom-call | tf_op jit(solution)/shard_map/expand/pallas_call | solution.py:483
  51.9 14.2 %all_to_all.22.got.three = bf16[32,40,128]{2,1,0:T(8,128)(2,1)S(1)} all-to-all(bf16[32,40,128]{2,1,0:T(8,128)(2,1)S(1)} %get-tuple-element.33), channel_id=1, replica_groups=mesh['dp'=8,'bn'=4] {'dp','bn'}, dimensions={0} | all-to-all | bytes 655360 | tf_op jit(solution)/shard_map/all_to_all | solution.py:393
  66.1 0.0 copy-done.5
  66.1 0.0 copy-done.6
  66.2 0.0 copy-done.7
  66.2 3.3 %keys.1 = (bf16[8,128]{1,0:T(8,128)(2,1)}, bf16[32,24,128]{2,1,0:T(8,128)(2,1)S(1)}) custom-call(bf16[32,32,128]{2,1,0:T(8,128)(2,1)S(1)} %get-tuple-element.29.own.own_numbers, bf16[32,32,128]{2,1,0:T(8,128)(2,1)S(1)} %all_to_all.20.got.numbers.one, bf16[32,40,128]{2,1,0:T(8,128)(2,1)S(1)} %all_to_all.22.got.three, f32[1,2048]{1,0:T(1,128)S(1)} %bitcast.8, ...), custom_call_target="tpu_custom_call" | custom-call | tf_op jit(solution)/shard_map/keys/pallas_call | solution.py:497
  69.5 11.1 %all_to_all.23.four = bf16[32,24,128]{2,1,0:T(8,128)(2,1)S(1)} all-to-all(bf16[32,24,128]{2,1,0:T(8,128)(2,1)S(1)} %get-tuple-element.41), channel_id=1, replica_groups=mesh['dp'=8,'bn'=4] {'dp','bn'}, dimensions={0} | all-to-all | bytes 393216 | tf_op jit(solution)/shard_map/all_to_all | solution.py:393
  80.6 0.3 query_grad.1
  81.0 0.7 collective-permute-start
  81.6 1.5 %collective-permute-done = f32[1024,128]{1,0:T(8,128)S(1)} collective-permute-done((f32[1024,128]{1,0:T(8,128)S(1)}, f32[1024,128]{1,0:T(8,128)S(1)}, u32[]{:S(2)}, u32[]{:S(2)}) %collective-permute-start) | collective-permute-done | bytes 524320 | tf_op jit(solution)/shard_map/ppermute | solution.py:534
  83.2 0.1 broadcast_select_fusion.1
  83.2 1.0 %pad_maximum_fusion = f32[2048,128]{1,0:T(8,128)} fusion(f32[1024,128]{1,0:T(8,128)S(1)} %get-tuple-element.43, f32[1024,128]{1,0:T(8,128)S(1)} %get-tuple-element.42), kind=kLoop, calls=%fused_computation | loop fusion | flops 262144 | bytes 2097152 | tf_op jit(solution)/shard_map/concatenate | solution.py:536
Async XLA Ops:
  0.6 10.4 %copy-start.3 = (bf16[8,2048]{1,0:T(8,128)(2,1)S(1)}, bf16[8,2048]{1,0:T(8,128)(2,1)}, u32[]{:S(2)}) copy-start(bf16[8,2048]{1,0:T(8,128)(2,1)} %query_feats.6) | copy-start | bytes 98308
  0.6 10.4 %copy-start.4 = (bf16[2048,128]{1,0:T(8,128)(2,1)S(1)}, bf16[2048,128]{1,0:T(8,128)(2,1)}, u32[]{:S(2)}) copy-start(bf16[2048,128]{1,0:T(8,128)(2,1)} %w_query.1) | copy-start | bytes 1572868
  0.7 10.4 %copy-start.2 = (bf16[16384,128]{1,0:T(8,128)(2,1)S(1)}, bf16[16384,128]{1,0:T(8,128)(2,1)}, u32[]{:S(2)}) copy-start(bf16[16384,128]{1,0:T(8,128)(2,1)} %queue.1) | copy-start | bytes 12582916
  11.0 21.3 %copy-start.1 = (bf16[9,512,512]{2,1,0:T(8,128)(2,1)S(1)}, bf16[9,512,512]{2,1,0:T(8,128)(2,1)}, u32[]{:S(2)}) copy-start(bf16[9,512,512]{2,1,0:T(8,128)(2,1)} %weights.5) | copy-start | bytes 14155780
  11.0 21.3 %copy-start.8 = (f32[512]{0:T(512)S(1)}, f32[512]{0:T(512)}, u32[]{:S(2)}) copy-start(f32[512]{0:T(512)} %param.23) | copy-start | bytes 6148
  11.0 21.3 %copy-start.9 = (f32[512]{0:T(512)S(1)}, f32[512]{0:T(512)}, u32[]{:S(2)}) copy-start(f32[512]{0:T(512)} %param.24) | copy-start | bytes 6148
  14.6 34.8 %copy-start = (bf16[512,2048]{1,0:T(8,128)(2,1)S(1)}, bf16[512,2048]{1,0:T(8,128)(2,1)}, u32[]{:S(2)}) copy-start(bf16[512,2048]{1,0:T(8,128)(2,1)} %weights.7) | copy-start | bytes 6291460
  14.6 34.8 %copy-start.10 = (f32[512]{0:T(512)S(1)}, f32[512]{0:T(512)}, u32[]{:S(2)}) copy-start(f32[512]{0:T(512)} %param.25) | copy-start | bytes 6148
  14.6 34.8 %copy-start.11 = (f32[512]{0:T(512)S(1)}, f32[512]{0:T(512)}, u32[]{:S(2)}) copy-start(f32[512]{0:T(512)} %param.26) | copy-start | bytes 6148
  36.5 29.7 %copy-start.5 = (bf16[2048,128]{1,0:T(8,128)(2,1)S(1)}, bf16[2048,128]{1,0:T(8,128)(2,1)}, u32[]{:S(2)}) copy-start(bf16[2048,128]{1,0:T(8,128)(2,1)} %w_key.1) | copy-start | bytes 1572868
  36.5 29.6 %copy-start.6 = (f32[2048]{0:T(1024)S(1)}, f32[2048]{0:T(1024)}, u32[]{:S(2)}) copy-start(f32[2048]{0:T(1024)} %param.27) | copy-start | bytes 24580
  36.5 29.6 %copy-start.7 = (f32[2048]{0:T(1024)S(1)}, f32[2048]{0:T(1024)}, u32[]{:S(2)}) copy-start(f32[2048]{0:T(1024)} %param.28) | copy-start | bytes 24580
  81.0 2.2 %collective-permute-start = (f32[1024,128]{1,0:T(8,128)S(1)}, f32[1024,128]{1,0:T(8,128)S(1)}, u32[]{:S(2)}, u32[]{:S(2)}) collective-permute-start(f32[1024,128]{1,0:T(8,128)S(1)} %query_grad.1), channel_id=1, source_target_pairs={{0,1},{1,0},{2,3},{3,2},{4,5},{5,4},{6,7},{7,6},{8,9},{9,8},{10,11... | collective-permute-start | bytes 1572872 | tf_op jit(solution)/shard_map/ppermute | solution.py:534

commit v4 on v3

--- a/solution.py
+++ b/solution.py
@@ -272,17 +272,37 @@
     weights,
     third,
     w_key,
-    unit,
-    length,
-    negatives,
-    pulled,
     frames,
     query_feats,
+    w_query,
+    queue,
     keys,
     message,
     pooled,
+    products,
 ):
     clips = frames.shape[0]
+    emb = queue.shape[1]
+    query = jnp.dot(query_feats[...], w_query[...], preferred_element_type=jnp.float32)
+    length = jnp.sqrt(jnp.sum(query * query, axis=-1, keepdims=True) + 1e-06)
+    direction = query / length
+    rounded = direction.astype(jnp.bfloat16)
+    none, ones = jnp.zeros((clips, emb), jnp.bfloat16), jnp.ones((clips, emb), jnp.bfloat16)
+    both = jnp.concatenate(
+        [jnp.concatenate([rounded, none], axis=1), jnp.concatenate([none, ones], axis=1)], axis=0
+    )
+    step = queue.shape[0] // clips
+
+    def queue_products(i):
+        entries = queue[pl.ds(i * step, step), :]
+        return lax.dot_general(
+            both,
+            jnp.concatenate([entries, entries * entries], axis=1),
+            (((1,), (1,)), ((), ())),
+            preferred_element_type=jnp.float32,
+        )
+
+    products[...] = queue_products(0)
     inner, channels = weights.shape
     part, wide = inner // LANES, channels // LANES
     same = members(numbers, group_row(own_numbers, part), part)
@@ -306,7 +326,17 @@
     scale = gain[...] * lax.rsqrt(within + between + EPSILON)
     bias = shift[...] - mean * scale
 
-    def one_clip(n, _):
+    def one_step(n, carry):
+        negatives, pulled = carry
+        inverse = lax.rsqrt(products[clips:] + 1e-06)
+        weight = jnp.exp(products[:clips] * inverse / SHARPNESS_DIVISOR)
+        negatives = negatives + jnp.sum(weight, axis=-1, keepdims=True)
+        pulled = pulled + jnp.dot(
+            (weight * inverse).astype(jnp.bfloat16),
+            queue[pl.ds(n * step, step), :],
+            preferred_element_type=jnp.float32,
+        )
+        products[...] = queue_products(jnp.minimum(n + 1, clips - 1))
         total = jnp.zeros((SPOTS, channels), jnp.float32)
         for t in range(FRAMES):
             values = jnp.concatenate(
@@ -320,9 +350,15 @@
                 values * scale + bias + frames[n, t + 1].astype(jnp.float32), 0.0
             )
         pooled[pl.ds(n, 1), :] = jnp.sum(total, axis=0, keepdims=True) / (FRAMES * SPOTS)
-        return 0
-
-    lax.fori_loop(0, clips, one_clip, 0)
+        return negatives, pulled
+
+    negatives, pulled = lax.fori_loop(
+        0,
+        clips,
+        one_step,
+        (jnp.zeros((clips, 1), jnp.float32), jnp.zeros((clips, emb), jnp.float32)),
+        unroll=clips,
+    )
     projected = jnp.dot(
         pooled[...].astype(jnp.bfloat16), w_key[...], preferred_element_type=jnp.float32
     )
@@ -331,48 +367,13 @@
     ).astype(jnp.bfloat16)
     keys[...] = own
     own = own.astype(jnp.float32)
-    direction = unit[...]
     positive = jnp.exp(jnp.sum(direction * own, axis=-1, keepdims=True) / SHARPNESS_DIVISOR)
-    partition = positive + negatives[...]
-    grad = (pulled[...] / partition + (positive / partition - 1.0) * own) / SHARPNESS_DIVISOR
+    partition = positive + negatives
+    grad = (pulled / partition + (positive / partition - 1.0) * own) / SHARPNESS_DIVISOR
     radial = jnp.sum(direction * grad, axis=-1, keepdims=True)
-    grad = ((grad - radial * direction) / length[...]).astype(jnp.bfloat16)
+    grad = ((grad - radial * direction) / length).astype(jnp.bfloat16)
     message[:, :clips, :] = jnp.broadcast_to(grad[None], (message.shape[0],) + grad.shape)
     write_queries(message, query_feats, 3)
-
-
-def queue_kernel(query_feats, w_query, queue, unit, length, negatives, pulled):
-    projected = jnp.dot(query_feats[...], w_query[...], preferred_element_type=jnp.float32)
-    norm = jnp.sqrt(jnp.sum(projected * projected, axis=-1, keepdims=True) + 1e-06)
-    direction = projected / norm
-    unit[...] = direction
-    length[...] = jnp.broadcast_to(norm, length.shape)
-    rounded = direction.astype(jnp.bfloat16)
-    rows, width = rounded.shape
-    none, ones = jnp.zeros((rows, width), jnp.bfloat16), jnp.ones((rows, width), jnp.bfloat16)
-    both = jnp.concatenate(
-        [jnp.concatenate([rounded, none], axis=1), jnp.concatenate([none, ones], axis=1)], axis=0
-    )
-    pieces = 8
-    step = queue.shape[0] // pieces
-    total = jnp.zeros((rows, 1), jnp.float32)
-    weighted = jnp.zeros((rows, width), jnp.float32)
-    for i in range(pieces):
-        entries = queue[i * step : (i + 1) * step, :]
-        products = lax.dot_general(
-            both,
-            jnp.concatenate([entries, entries * entries], axis=1),
-            (((1,), (1,)), ((), ())),
-            preferred_element_type=jnp.float32,
-        )
-        inverse = lax.rsqrt(products[rows:] + 1e-06)
-        weight = jnp.exp(products[:rows] * inverse / SHARPNESS_DIVISOR)
-        total = total + jnp.sum(weight, axis=-1, keepdims=True)
-        weighted = weighted + jnp.dot(
-            (weight * inverse).astype(jnp.bfloat16), entries, preferred_element_type=jnp.float32
-        )
-    negatives[...] = jnp.broadcast_to(total, negatives.shape)
-    pulled[...] = weighted
 
 
 def gradient_kernel(one, two, three, four, out):
@@ -449,18 +450,6 @@
         in_hbm(conv_time),
         in_hbm(query_feats),
     )
-    late_queries, sent_one = lax.optimization_barrier((query_feats, sent_one))
-    unit, length, negatives, pulled = pl.pallas_call(
-        queue_kernel,
-        out_shape=(jax.ShapeDtypeStruct((clips, emb), jnp.float32),) * 4,
-        in_specs=[VMEM] * 3,
-        out_specs=(VMEM,) * 4,
-        compiler_params=pltpu.CompilerParams(vmem_limit_bytes=4 * MIB),
-        name="queue_terms",
-    )(late_queries, w_query, queue)
-    sent_one, unit, length, negatives, pulled = lax.optimization_barrier(
-        (sent_one, unit, length, negatives, pulled)
-    )
     got_one = exchange(sent_one)
 
     grid_rows = rows // spots
@@ -500,9 +489,12 @@
             jax.ShapeDtypeStruct((clips, emb), jnp.bfloat16),
             jax.ShapeDtypeStruct((devices, clips + QUERY_ROWS, emb), jnp.bfloat16),
         ),
-        in_specs=[VMEM] * 14,
+        in_specs=[VMEM] * 12,
         out_specs=(VMEM, VMEM),
-        scratch_shapes=[pltpu.VMEM((clips, channels), jnp.float32)],
+        scratch_shapes=[
+            pltpu.VMEM((clips, channels), jnp.float32),
+            pltpu.VMEM((2 * clips, queue.shape[0] // clips), jnp.float32),
+        ],
         compiler_params=pltpu.CompilerParams(vmem_limit_bytes=8 * MIB),
         name="keys",
     )(
@@ -514,12 +506,10 @@
         conv_expand,
         third,
         w_key,
-        unit,
-        length,
-        negatives,
-        pulled,
         frames,
         query_feats,
+        w_query,
+        queue,
     )
     got_four = exchange(sent)
     own_half = pl.pallas_call(

time: 84.5 us -> 82.8 us (0.980)
  Pallas kernels: 24.3 us -> 22.6 us
    pallas_call x1 -> x0, Pallas kernels: 3.51 us -> none  [local(): pl.pallas_call(queue_kernel, out_shape=(jax.ShapeDtypeStruct((clips, emb)...]
    pallas_call x1, Pallas kernels: 3.34 us -> 5.14 us  [local(): pl.pallas_call(keys_kernel, out_shape=(jax.ShapeDtypeStruct((clips, emb),...]
where the time goes in v4:
time: 82.8 us; the launch traced here: 82.6 us
  blocking collectives  55.8 us (67%)
  Pallas kernels  22.6 us (27%)
  waiting for transfers between devices  1.54 us (2%)
  other arithmetic  1.11 us (1%)
    all_to_all x4, blocking collectives, exchange(): return lax.all_to_all(message, ('dp', 'bn'), 0, 0)  55.8 us
    pallas_call x1, Pallas kernels, local(): pl.pallas_call(functools.partial(time_conv_kernel, cuts), out_shape=(jax....  10.3 us
    pallas_call x1, Pallas kernels, local(): pl.pallas_call(keys_kernel, out_shape=(jax.ShapeDtypeStruct((clips, emb),...  5.14 us
    pallas_call x1, Pallas kernels, local(): pl.pallas_call(space_conv_kernel, out_shape=(jax.ShapeDtypeStruct((part,...  4.19 us
    pallas_call x1, Pallas kernels, local(): pl.pallas_call(expand_kernel, out_shape=(jax.ShapeDtypeStruct((wide, rows...  2.55 us
  transfers between devices with their start and end apart: 1, of which 1 were waited for; matrix products, arithmetic and copies ran while one was open for 0% of the time, Pallas kernels for 0%

profile of v4, /device:TPU:0, one launch (start us, length us, event | category | flops | bytes accessed | tf_op | source)
XLA Modules:
  0.0 82.6 jit_solution(7303245119120577904)
XLA Ops:
  0.6 0.0 copy-start.3
  0.6 0.0 copy-start.8
  0.7 0.0 copy-start.9
  0.7 0.0 copy-start.1
  0.7 10.3 %time_conv.1 = (f32[4,1024,128]{2,1,0:T(8,128)S(1)}, bf16[8,10,16,2048]{3,2,1,0:T(8,128)(2,1)S(1)}, bf16[32,32,128]{2,1,0:T(8,128)(2,1)S(1)}) custom-call(s32[8]{0:T(128)} %starts_hbm.1, s32[1,8]{1,0:T(1,128)} %shuffle_hbm.1, bf16[8,12,16,2048]{3,2,1,0:T(8,128)(2,1)} %feats.1, bf16[3,2048,512]{2,1,0:T(8,128)(2,1)} %weights.4, bf16[8,2048]{1,0:T(8,128)(2,1)} %query_feats.5), custom_call_target="tpu_custom_call" | custom-call | tf_op jit(solution)/shard_map/time_conv/pallas_call | solution.py:426
  11.0 0.0 copy-start
  11.0 0.0 copy-start.10
  11.0 0.0 copy-start.11
  11.0 17.7 %all_to_all.20.got.numbers.one = bf16[32,32,128]{2,1,0:T(8,128)(2,1)S(1)} all-to-all(bf16[32,32,128]{2,1,0:T(8,128)(2,1)S(1)} %get-tuple-element.11.own.own_numbers), channel_id=1, replica_groups=mesh['dp'=8,'bn'=4] {'dp','bn'}, dimensions={0} | all-to-all | bytes 524288 | tf_op jit(solution)/shard_map/all_to_all | solution.py:394
  28.7 0.0 copy-done.3
  28.8 0.0 copy-done.8
  28.8 0.0 copy-done.9
  28.8 0.0 copy-done.1
  28.8 4.2 %space_conv.1 = (f32[4,16,72,128]{3,2,1,0:T(8,128)S(1)}, bf16[32,32,128]{2,1,0:T(8,128)(2,1)S(1)}) custom-call(bf16[32,32,128]{2,1,0:T(8,128)(2,1)S(1)} %get-tuple-element.11.own.own_numbers, bf16[32,32,128]{2,1,0:T(8,128)(2,1)S(1)} %all_to_all.20.got.numbers.one, f32[1,512]{1,0:T(1,128)S(1)} %bitcast.10, f32[1,512]{1,0:T(1,128)S(1)} %bitcast.11, ...), custom_call_target="tpu_custom_call" | custom-call | tf_op jit(solution)/shard_map/space_conv/pallas_call | solution.py:457
  33.0 0.0 copy-start.2
  33.0 0.0 copy-start.4
  33.0 0.0 copy-start.5
  33.0 0.0 copy-start.6
  33.0 0.0 copy-start.7
  33.0 12.8 %all_to_all.21.got.two = bf16[32,32,128]{2,1,0:T(8,128)(2,1)S(1)} all-to-all(bf16[32,32,128]{2,1,0:T(8,128)(2,1)S(1)} %get-tuple-element.13.own), channel_id=1, replica_groups=mesh['dp'=8,'bn'=4] {'dp','bn'}, dimensions={0} | all-to-all | bytes 524288 | tf_op jit(solution)/shard_map/all_to_all | solution.py:394
  45.9 0.0 copy-done
  45.9 0.0 copy-done.10
  45.9 0.0 copy-done.11
  45.9 2.6 %expand.1 = (f32[16,1024,128]{2,1,0:T(8,128)S(1)}, bf16[32,40,128]{2,1,0:T(8,128)(2,1)S(1)}) custom-call(bf16[32,32,128]{2,1,0:T(8,128)(2,1)S(1)} %get-tuple-element.13.own, bf16[32,32,128]{2,1,0:T(8,128)(2,1)S(1)} %all_to_all.21.got.two, f32[1,512]{1,0:T(1,128)S(1)} %bitcast.12, f32[1,512]{1,0:T(1,128)S(1)} %bitcast.13, f32[4,1152,128]{2,1,0:T(8,128)S(1)} %bitcast.7, ...), custom_call_target="tpu_custom_call" | custom-call | tf_op jit(solution)/shard_map/expand/pallas_call | solution.py:472
  48.4 14.2 %all_to_all.22.got.three = bf16[32,40,128]{2,1,0:T(8,128)(2,1)S(1)} all-to-all(bf16[32,40,128]{2,1,0:T(8,128)(2,1)S(1)} %get-tuple-element.15), channel_id=1, replica_groups=mesh['dp'=8,'bn'=4] {'dp','bn'}, dimensions={0} | all-to-all | bytes 655360 | tf_op jit(solution)/shard_map/all_to_all | solution.py:394
  62.6 0.0 copy-done.2
  62.6 0.0 copy-done.4
  62.6 0.0 copy-done.5
  62.6 0.0 copy-done.6
  62.7 0.0 copy-done.7
  62.7 5.1 %keys.1 = (bf16[8,128]{1,0:T(8,128)(2,1)}, bf16[32,24,128]{2,1,0:T(8,128)(2,1)S(1)}) custom-call(bf16[32,32,128]{2,1,0:T(8,128)(2,1)S(1)} %get-tuple-element.11.own.own_numbers, bf16[32,32,128]{2,1,0:T(8,128)(2,1)S(1)} %all_to_all.20.got.numbers.one, bf16[32,40,128]{2,1,0:T(8,128)(2,1)S(1)} %all_to_all.22.got.three, f32[1,2048]{1,0:T(1,128)S(1)} %bitcast.8, ...), custom_call_target="tpu_custom_call" | custom-call | tf_op jit(solution)/shard_map/keys/pallas_call | solution.py:486
  67.8 11.1 %all_to_all.23.four = bf16[32,24,128]{2,1,0:T(8,128)(2,1)S(1)} all-to-all(bf16[32,24,128]{2,1,0:T(8,128)(2,1)S(1)} %get-tuple-element.19), channel_id=1, replica_groups=mesh['dp'=8,'bn'=4] {'dp','bn'}, dimensions={0} | all-to-all | bytes 393216 | tf_op jit(solution)/shard_map/all_to_all | solution.py:394
  78.9 0.3 query_grad.1
  79.3 0.7 collective-permute-start
  79.9 1.5 %collective-permute-done = f32[1024,128]{1,0:T(8,128)S(1)} collective-permute-done((f32[1024,128]{1,0:T(8,128)S(1)}, f32[1024,128]{1,0:T(8,128)S(1)}, u32[]{:S(2)}, u32[]{:S(2)}) %collective-permute-start) | collective-permute-done | bytes 524320 | tf_op jit(solution)/shard_map/ppermute | solution.py:524
  81.5 0.1 broadcast_select_fusion.1
  81.5 1.0 %pad_maximum_fusion = f32[2048,128]{1,0:T(8,128)} fusion(f32[1024,128]{1,0:T(8,128)S(1)} %get-tuple-element.21, f32[1024,128]{1,0:T(8,128)S(1)} %get-tuple-element.20), kind=kLoop, calls=%fused_computation | loop fusion | flops 262144 | bytes 2097152 | tf_op jit(solution)/shard_map/concatenate | solution.py:526
Async XLA Ops:
  0.6 28.1 %copy-start.3 = (bf16[8,2048]{1,0:T(8,128)(2,1)S(1)}, bf16[8,2048]{1,0:T(8,128)(2,1)}, u32[]{:S(2)}) copy-start(bf16[8,2048]{1,0:T(8,128)(2,1)} %query_feats.5) | copy-start | bytes 98308
  0.6 28.1 %copy-start.8 = (f32[512]{0:T(512)S(1)}, f32[512]{0:T(512)}, u32[]{:S(2)}) copy-start(f32[512]{0:T(512)} %param.23) | copy-start | bytes 6148
  0.7 28.1 %copy-start.9 = (f32[512]{0:T(512)S(1)}, f32[512]{0:T(512)}, u32[]{:S(2)}) copy-start(f32[512]{0:T(512)} %param.24) | copy-start | bytes 6148
  0.7 28.1 %copy-start.1 = (bf16[9,512,512]{2,1,0:T(8,128)(2,1)S(1)}, bf16[9,512,512]{2,1,0:T(8,128)(2,1)}, u32[]{:S(2)}) copy-start(bf16[9,512,512]{2,1,0:T(8,128)(2,1)} %weights.5) | copy-start | bytes 14155780
  11.0 34.8 %copy-start = (bf16[512,2048]{1,0:T(8,128)(2,1)S(1)}, bf16[512,2048]{1,0:T(8,128)(2,1)}, u32[]{:S(2)}) copy-start(bf16[512,2048]{1,0:T(8,128)(2,1)} %weights.7) | copy-start | bytes 6291460
  11.0 34.8 %copy-start.10 = (f32[512]{0:T(512)S(1)}, f32[512]{0:T(512)}, u32[]{:S(2)}) copy-start(f32[512]{0:T(512)} %param.25) | copy-start | bytes 6148
  11.0 34.8 %copy-start.11 = (f32[512]{0:T(512)S(1)}, f32[512]{0:T(512)}, u32[]{:S(2)}) copy-start(f32[512]{0:T(512)} %param.26) | copy-start | bytes 6148
  33.0 29.7 %copy-start.2 = (bf16[16384,128]{1,0:T(8,128)(2,1)S(1)}, bf16[16384,128]{1,0:T(8,128)(2,1)}, u32[]{:S(2)}) copy-start(bf16[16384,128]{1,0:T(8,128)(2,1)} %queue.1) | copy-start | bytes 12582916
  33.0 29.7 %copy-start.4 = (bf16[2048,128]{1,0:T(8,128)(2,1)S(1)}, bf16[2048,128]{1,0:T(8,128)(2,1)}, u32[]{:S(2)}) copy-start(bf16[2048,128]{1,0:T(8,128)(2,1)} %w_key.1) | copy-start | bytes 1572868
  33.0 29.6 %copy-start.5 = (bf16[2048,128]{1,0:T(8,128)(2,1)S(1)}, bf16[2048,128]{1,0:T(8,128)(2,1)}, u32[]{:S(2)}) copy-start(bf16[2048,128]{1,0:T(8,128)(2,1)} %w_query.1) | copy-start | bytes 1572868
  33.0 29.6 %copy-start.6 = (f32[2048]{0:T(1024)S(1)}, f32[2048]{0:T(1024)}, u32[]{:S(2)}) copy-start(f32[2048]{0:T(1024)} %param.27) | copy-start | bytes 24580
  33.0 29.6 %copy-start.7 = (f32[2048]{0:T(1024)S(1)}, f32[2048]{0:T(1024)}, u32[]{:S(2)}) copy-start(f32[2048]{0:T(1024)} %param.28) | copy-start | bytes 24580
  79.3 2.2 %collective-permute-start = (f32[1024,128]{1,0:T(8,128)S(1)}, f32[1024,128]{1,0:T(8,128)S(1)}, u32[]{:S(2)}, u32[]{:S(2)}) collective-permute-start(f32[1024,128]{1,0:T(8,128)S(1)} %query_grad.1), channel_id=1, source_target_pairs={{0,1},{1,0},{2,3},{3,2},{4,5},{5,4},{6,7},{7,6},{8,9},{9,8},{10,11... | collective-permute-start | bytes 1572872 | tf_op jit(solution)/shard_map/ppermute | solution.py:524

commit v5 on v4

--- a/solution.py
+++ b/solution.py
@@ -15,7 +15,6 @@
 EPSILON = 1e-05
 MIB = 1 << 20
 MOMENT_ROWS = 16
-QUERY_ROWS = 16
 
 VMEM = pl.BlockSpec(memory_space=pltpu.VMEM)
 ANY = pl.BlockSpec(memory_space=pl.ANY)
@@ -35,18 +34,20 @@
     )
 
 
-def write_queries(message, query_feats, piece):
+def write_queries(message, query_feats, units):
     half = query_feats.shape[1] // 2
-    parts = []
-    for side in range(2):
-        at = side * half + piece * 2 * LANES
-        parts.append(
+    pair = jnp.stack(
+        [
             jnp.concatenate(
-                [query_feats[:, at : at + LANES], query_feats[:, at + LANES : at + 2 * LANES]],
+                [
+                    query_feats[:, side * half + u * LANES : side * half + (u + 1) * LANES]
+                    for u in units
+                ],
                 axis=0,
             )
-        )
-    pair = jnp.stack(parts)
+            for side in range(2)
+        ]
+    )
     devices, length, _ = message.shape
     every = jnp.broadcast_to(pair[None], (devices // 2,) + pair.shape)
     message[:, length - pair.shape[1] :, :] = every.reshape((devices,) + pair.shape[1:])
@@ -96,6 +97,7 @@
 
 def time_conv_kernel(
     cuts,
+    units,
     starts_hbm,
     shuffle_hbm,
     feats,
@@ -146,6 +148,7 @@
     blank = jnp.zeros((clips, 1) + frames.shape[2:], jnp.bfloat16)
     frames[:, 0:1] = blank
     frames[:, FRAMES + 1 : FRAMES + 2] = blank
+    total, squares = [], []
     for k in range(pieces):
         depth = cuts[k + 1] - cuts[k]
         copy_taps(k).wait()
@@ -165,15 +168,12 @@
         )
         for j in range(inner // LANES):
             piece = product[:, j * LANES : (j + 1) * LANES]
-            if k == 0:
-                first[j] = piece
-            else:
-                first[j] += piece
-    total, squares = [], []
-    for j in range(inner // LANES):
-        values = first[j]
-        total.append(jnp.sum(values, axis=0, keepdims=True))
-        squares.append(jnp.sum(values * values, axis=0, keepdims=True))
+            if k > 0:
+                piece = piece + first[j, :rows]
+            first[j, :rows] = piece
+            if k == pieces - 1:
+                total.append(jnp.sum(piece, axis=0, keepdims=True))
+                squares.append(jnp.sum(piece * piece, axis=0, keepdims=True))
     mean, var = mean_and_var(
         jnp.concatenate(total, axis=1), jnp.concatenate(squares, axis=1), rows
     )
@@ -181,15 +181,15 @@
     group = shuffle[0, lax.axis_index("dp")].astype(jnp.float32)
     write_moments(message, mean, var, jnp.full((1, LANES), group, jnp.float32))
     copy_queries.wait()
-    write_queries(message, query_feats, 0)
+    write_queries(message, query_feats, units)
 
 
 def space_conv_kernel(
-    own, got, gain, shift, first, weights, query_feats, second, message, act, taken
+    units, own, got, gain, shift, first, weights, query_feats, second, message, act, taken
 ):
     inner = weights.shape[1]
     part = inner // LANES
-    rows = first.shape[1] // SPOTS
+    rows = act.shape[2]
     number = group_row(own, part)
     scale, bias = group_scale_and_bias(got, number, gain, shift)
     for r in range(SIDE):
@@ -224,15 +224,16 @@
             squares = squares + jnp.sum(values * values, axis=0, keepdims=True)
     mean, var = mean_and_var(total, squares, rows * SPOTS)
     write_moments(message, mean, var, number)
-    write_queries(message, query_feats, 1)
-
-
-def expand_kernel(own, got, gain, shift, second, weights, query_feats, third, message, act):
+    write_queries(message, query_feats, units)
+
+
+def expand_kernel(
+    units, own, got, gain, shift, second, weights, query_feats, third, message, act):
     inner, channels = weights.shape
     rows = act.shape[0]
     part = inner // LANES
     scale, bias = group_scale_and_bias(got, group_row(own, part), gain, shift)
-    pitch = second.shape[1] // SPOTS
+    pitch = second.shape[1] // (SPOTS + 1)
     total = jnp.zeros((SPOTS, inner), jnp.float32)
     for i in range(rows // SPOTS):
         values = jnp.concatenate(
@@ -260,10 +261,11 @@
     message[:, : block.shape[0], :] = jnp.broadcast_to(
         block[None], (message.shape[0],) + block.shape
     )
-    write_queries(message, query_feats, 2)
+    write_queries(message, query_feats, units)
 
 
 def keys_kernel(
+    columns,
     own_numbers,
     numbers,
     got,
@@ -306,23 +308,21 @@
     inner, channels = weights.shape
     part, wide = inner // LANES, channels // LANES
     same = members(numbers, group_row(own_numbers, part), part)
-    act_mean = jnp.concatenate(
-        [
-            jnp.concatenate([got[:, h * part + j, :] for j in range(part)], axis=1)
-            for h in range(2)
-        ],
-        axis=0,
-    )
-    parts = jnp.dot(act_mean, weights[...], preferred_element_type=jnp.float32)
-    devices = got.shape[0]
-    block_mean = parts[:devices] + parts[devices:]
-    chosen = same[:, 0, 0:1]
-    blocks = jnp.sum(same, axis=0)
-    mean = jnp.sum(block_mean * chosen, axis=0, keepdims=True) / blocks[:, 0:1]
+    picked = got[:, : 2 * part, :].astype(jnp.float32) * same
+    picked = jnp.sum(picked.reshape((-1, columns) + picked.shape[1:]), axis=0)
+    picked = picked[:, :part] + picked[:, part:]
+    high, low = two_halves(jnp.concatenate([picked[:, j, :] for j in range(part)], axis=1))
+    parts = jnp.dot(
+        jnp.concatenate([high, low], axis=0).astype(jnp.bfloat16),
+        weights[...],
+        preferred_element_type=jnp.float32,
+    )
+    block_mean = parts[:columns] + parts[columns:]
+    mean = jnp.sum(block_mean, axis=0, keepdims=True) / columns
     apart = block_mean - mean
-    between = jnp.sum(apart * apart * chosen, axis=0, keepdims=True) / blocks[:, 0:1]
+    between = jnp.sum(apart * apart, axis=0, keepdims=True) / columns
     block_var = got[:, 2 * part : 2 * part + wide, :].astype(jnp.float32)
-    within = as_row(jnp.sum(block_var * same, axis=0) / blocks)
+    within = as_row(jnp.sum(block_var * same, axis=0) / columns)
     scale = gain[...] * lax.rsqrt(within + between + EPSILON)
     bias = shift[...] - mean * scale
 
@@ -372,22 +372,36 @@
     grad = (pulled / partition + (positive / partition - 1.0) * own) / SHARPNESS_DIVISOR
     radial = jnp.sum(direction * grad, axis=-1, keepdims=True)
     grad = ((grad - radial * direction) / length).astype(jnp.bfloat16)
-    message[:, :clips, :] = jnp.broadcast_to(grad[None], (message.shape[0],) + grad.shape)
-    write_queries(message, query_feats, 3)
-
-
-def gradient_kernel(one, two, three, four, out):
-    devices, _, width = four.shape
-    clips = QUERY_ROWS // 2
-    grads = four[:, :clips, :].reshape(devices * clips, width)
-    for i, message in enumerate((one, two, three, four)):
-        for j in range(2):
-            at = message.shape[1] - QUERY_ROWS + j * clips
-            queries = message[:, at : at + clips, :].reshape(devices * clips, LANES)
-            start = (2 * i + j) * LANES
-            out[start : start + LANES] = lax.dot_general(
-                queries, grads, (((0,), (0,)), ((), ())), preferred_element_type=jnp.float32
-            )
+    message[...] = jnp.broadcast_to(grad[None], message.shape)
+
+
+def gradient_kernel(shares, grads, *rest):
+    mine, others, (out_hbm, out, out_sem) = rest[:3], rest[3:6], rest[6:]
+    devices, clips, width = grads.shape
+    right = grads[...].reshape(devices * clips, width)
+    half = out.shape[1]
+    odd = lax.axis_index("bn") % 2
+
+    def give(i):
+        start = pl.multiple_of((odd ^ i) * half, half)
+        return pltpu.make_async_copy(out.at[i], out_hbm.at[pl.ds(start, half)], out_sem.at[i])
+
+    for i, messages in enumerate((others, mine)):
+        i = 1 - i
+        for units, message in zip(shares, messages):
+            for j, u in enumerate(units):
+                at = message.shape[1] - (len(units) - j) * clips
+                queries = message[:, at : at + clips, :].reshape(devices * clips, LANES)
+                out[i, u * LANES : (u + 1) * LANES] = lax.dot_general(
+                    queries, right, (((0,), (0,)), ((), ())), preferred_element_type=jnp.float32
+                )
+        give(i).start()
+    for i in range(2):
+        give(i).wait()
+
+
+def from_neighbour(message):
+    return lax.ppermute(message, "bn", [(i, i ^ 1) for i in range(lax.axis_size("bn"))])
 
 
 def exchange(message):
@@ -417,18 +431,24 @@
     inner, emb = conv_space.shape[1], queue.shape[1]
     part, wide = inner // LANES, channels // LANES
     rows = clips * FRAMES * spots
-    short = jax.ShapeDtypeStruct((devices, MOMENT_ROWS + QUERY_ROWS, LANES), jnp.bfloat16)
+    count = channels // 2 // LANES
+    limits = (0, 3 * count // 8, 6 * count // 8, count)
+    shares = [tuple(range(a, b)) for a, b in zip(limits, limits[1:])]
+
+    def moments_message(share):
+        return jax.ShapeDtypeStruct((devices, MOMENT_ROWS + clips * len(share), LANES), jnp.bfloat16)
+
     row = lambda vector: vector.reshape(1, -1)
 
     cuts = (0, channels // 8, 3 * channels // 8, channels)
     pieces = len(cuts) - 1
     padded = (clips, FRAMES + 2, spots, channels)
     first, frames, sent_one = pl.pallas_call(
-        functools.partial(time_conv_kernel, cuts),
+        functools.partial(time_conv_kernel, cuts, shares[0]),
         out_shape=(
-            jax.ShapeDtypeStruct((part, rows, LANES), jnp.float32),
+            jax.ShapeDtypeStruct((part, rows + spots, LANES), jnp.float32),
             jax.ShapeDtypeStruct(padded, jnp.bfloat16),
-            short,
+            moments_message(shares[0]),
         ),
         in_specs=[ANY] * 5,
         out_specs=(VMEM,) * 3,
@@ -451,12 +471,16 @@
         in_hbm(query_feats),
     )
     got_one = exchange(sent_one)
+    other_one = from_neighbour(got_one)
 
     grid_rows = rows // spots
     pitch = grid_rows + 8
     second, sent_two = pl.pallas_call(
-        space_conv_kernel,
-        out_shape=(jax.ShapeDtypeStruct((part, SPOTS, pitch, LANES), jnp.float32), short),
+        functools.partial(space_conv_kernel, shares[1]),
+        out_shape=(
+            jax.ShapeDtypeStruct((part, SPOTS + 1, pitch, LANES), jnp.float32),
+            moments_message(shares[1]),
+        ),
         in_specs=[VMEM] * 7,
         out_specs=(VMEM, VMEM),
         scratch_shapes=[
@@ -466,14 +490,18 @@
         compiler_params=pltpu.CompilerParams(vmem_limit_bytes=10 * MIB),
         name="space_conv",
     )(sent_one, got_one, row(gain_one), row(shift_one), first, conv_space, query_feats)
+    sent_two, other_one = lax.optimization_barrier((sent_two, other_one))
     got_two = exchange(sent_two)
-    second = second.reshape(part, SPOTS * pitch, LANES)
+    other_two = from_neighbour(got_two)
+    second = second.reshape(part, (SPOTS + 1) * pitch, LANES)
 
     third, sent = pl.pallas_call(
-        expand_kernel,
+        functools.partial(expand_kernel, shares[2]),
         out_shape=(
             jax.ShapeDtypeStruct((wide, rows, LANES), jnp.float32),
-            jax.ShapeDtypeStruct((devices, 2 * part + wide + QUERY_ROWS, LANES), jnp.bfloat16),
+            jax.ShapeDtypeStruct(
+                (devices, 2 * part + wide + clips * len(shares[2]), LANES), jnp.bfloat16
+            ),
         ),
         in_specs=[VMEM] * 7,
         out_specs=(VMEM, VMEM),
@@ -481,13 +509,15 @@
         compiler_params=pltpu.CompilerParams(vmem_limit_bytes=8 * MIB),
         name="expand",
     )(sent_two, got_two, row(gain_two), row(shift_two), second, conv_expand, query_feats)
+    sent, other_two = lax.optimization_barrier((sent, other_two))
     got_three = exchange(sent)
+    other_three = from_neighbour(got_three)
 
     own_keys, sent = pl.pallas_call(
-        keys_kernel,
+        functools.partial(keys_kernel, lax.axis_size("bn")),
         out_shape=(
             jax.ShapeDtypeStruct((clips, emb), jnp.bfloat16),
-            jax.ShapeDtypeStruct((devices, clips + QUERY_ROWS, emb), jnp.bfloat16),
+            jax.ShapeDtypeStruct((devices, clips, emb), jnp.bfloat16),
         ),
         in_specs=[VMEM] * 12,
         out_specs=(VMEM, VMEM),
@@ -511,21 +541,19 @@
         w_query,
         queue,
     )
-    got_four = exchange(sent)
-    own_half = pl.pallas_call(
-        gradient_kernel,
-        out_shape=jax.ShapeDtypeStruct((channels // 2, emb), jnp.float32),
-        in_specs=[VMEM] * 4,
-        out_specs=VMEM,
-        compiler_params=pltpu.CompilerParams(vmem_limit_bytes=6 * MIB),
+    sent, other_three = lax.optimization_barrier((sent, other_three))
+    query_grad = pl.pallas_call(
+        functools.partial(gradient_kernel, shares),
+        out_shape=jax.ShapeDtypeStruct((channels, emb), jnp.float32),
+        in_specs=[VMEM] * 7,
+        out_specs=ANY,
+        scratch_shapes=[
+            pltpu.VMEM((2, channels // 2, emb), jnp.float32),
+            pltpu.SemaphoreType.DMA((2,)),
+        ],
+        compiler_params=pltpu.CompilerParams(vmem_limit_bytes=8 * MIB),
         name="query_grad",
-    )(got_one, got_two, got_three, got_four)
-    members_bn = lax.axis_size("bn")
-    other_half = lax.ppermute(own_half, "bn", [(i, i ^ 1) for i in range(members_bn)])
-    odd = lax.axis_index("bn") % 2 == 1
-    query_grad = jnp.concatenate(
-        [jnp.where(odd, other_half, own_half), jnp.where(odd, own_half, other_half)], axis=0
-    )
+    )(exchange(sent), got_one, got_two, got_three, other_one, other_two, other_three)
     return (own_keys, query_grad)
 
 

time: 82.8 us -> 82.2 us (level)
  blocking collectives: 55.8 us -> 57.4 us
  waiting for transfers between devices: 1.54 us -> 0.01 us
  other arithmetic: 1.11 us -> 0 us
  Pallas kernels: 22.6 us -> 23.5 us
    all_to_all x4, blocking collectives: 55.8 us -> 57.4 us  [exchange(): return lax.all_to_all(message, ('dp', 'bn'), 0, 0)]
    ppermute x1 -> x3, waiting for transfers between devices: 1.54 us -> 0.01 us  [from_neighbour(): lax.ppermute(message, 'bn', [(i, i ^ 1) for i in range(lax.axis_size('bn'...]
    concatenate x1 -> x0, other arithmetic: 1.04 us -> none  [local(): jnp.concatenate([jnp.where(odd, other_half, own_half), jnp.where(odd, own...]
    pallas_call x5, Pallas kernels: 22.6 us -> 23.5 us  [the longest x1 10.3 us: local(): pl.pallas_call(functools.partial(time_conv_kernel, cuts, shares[0]), out_...]
  transfers between devices with their start and end apart: 1 -> 3, of which waited for: 1 -> 0; matrix products, arithmetic and copies ran while one was open for 0% -> 0% of each run, Pallas kernels for 0% -> 14%
where the time goes in v5:
time: 82.2 us; the launch traced here: 82 us
  blocking collectives  57.4 us (70%)
  Pallas kernels  23.5 us (29%)
  between operations  0.99 us (1%)
    all_to_all x4, blocking collectives, exchange(): return lax.all_to_all(message, ('dp', 'bn'), 0, 0)  57.4 us
    pallas_call x1, Pallas kernels, local(): pl.pallas_call(functools.partial(time_conv_kernel, cuts, shares[0]), out_...  10.3 us
    pallas_call x1, Pallas kernels, local(): pl.pallas_call(functools.partial(keys_kernel, lax.axis_size('bn')), out_s...  5.07 us
    pallas_call x1, Pallas kernels, local(): pl.pallas_call(functools.partial(space_conv_kernel, shares[1]), out_shape...  4.22 us
    pallas_call x1, Pallas kernels, local(): pl.pallas_call(functools.partial(expand_kernel, shares[2]), out_shape=(ja...  2.58 us
  transfers between devices with their start and end apart: 3, of which 0 were waited for; matrix products, arithmetic and copies ran while one was open for 0% of the time, Pallas kernels for 14%

profile of v5, /device:TPU:0, one launch (start us, length us, event | category | flops | bytes accessed | tf_op | source)
XLA Modules:
  0.0 82.0 jit_solution(16400730948043401320)
XLA Ops:
  0.6 0.0 copy-start.3
  0.6 0.0 copy-start.8
  0.7 0.0 copy-start.9
  0.7 0.0 copy-start.1
  0.7 10.3 %time_conv.1 = (f32[4,1040,128]{2,1,0:T(8,128)S(1)}, bf16[8,10,16,2048]{3,2,1,0:T(8,128)(2,1)S(1)}, bf16[32,40,128]{2,1,0:T(8,128)(2,1)S(1)}) custom-call(s32[8]{0:T(128)} %starts_hbm.1, s32[1,8]{1,0:T(1,128)} %shuffle_hbm.1, bf16[8,12,16,2048]{3,2,1,0:T(8,128)(2,1)} %feats.1, bf16[3,2048,512]{2,1,0:T(8,128)(2,1)} %weights.4, bf16[8,2048]{1,0:T(8,128)(2,1)} %query_feats.5), custom_call_target="tpu_custom_call" | custom-call | tf_op jit(solution)/shard_map/time_conv/pallas_call | solution.py:446
  11.0 0.0 copy-start
  11.0 0.0 copy-start.10
  11.0 0.0 copy-start.11
  11.1 19.1 %all_to_all.20.got.numbers.rest_0_ = bf16[32,40,128]{2,1,0:T(8,128)(2,1)S(1)} all-to-all(bf16[32,40,128]{2,1,0:T(8,128)(2,1)S(1)} %get-tuple-element.17.own.own_numbers), channel_id=1, replica_groups=mesh['dp'=8,'bn'=4] {'dp','bn'}, dimensions={0} | all-to-all | bytes 655360 | tf_op jit(solution)/shard_map/all_to_all | solution.py:408
  30.1 0.0 collective-permute-start
  30.1 0.0 copy-done.3
  30.1 0.0 copy-done.8
  30.2 0.0 copy-done.9
  30.2 0.0 copy-done.1
  30.2 4.2 %space_conv.1 = (f32[4,17,72,128]{3,2,1,0:T(8,128)S(1)}, bf16[32,40,128]{2,1,0:T(8,128)(2,1)S(1)}) custom-call(bf16[32,40,128]{2,1,0:T(8,128)(2,1)S(1)} %get-tuple-element.17.own.own_numbers, bf16[32,40,128]{2,1,0:T(8,128)(2,1)S(1)} %all_to_all.20.got.numbers.rest_0_, f32[1,512]{1,0:T(1,128)S(1)} %bitcast.10, f32[1,512]{1,0:T(1,128)S(1)} %bitcast.11, ...), custom_call_target="tpu_custom_call" | custom-call | tf_op jit(solution)/shard_map/space_conv/pallas_call | solution.py:478
  34.4 0.0 copy-start.2
  34.4 0.0 copy-start.4
  34.4 0.0 copy-start.5
  34.4 0.0 copy-start.6
  34.4 0.0 copy-start.7
  34.5 0.0 collective-permute-done.rest_3_
  34.5 14.3 %all_to_all.21.got.rest_1_ = bf16[32,40,128]{2,1,0:T(8,128)(2,1)S(1)} all-to-all(bf16[32,40,128]{2,1,0:T(8,128)(2,1)S(1)} %get-tuple-element.20.own), channel_id=1, replica_groups=mesh['dp'=8,'bn'=4] {'dp','bn'}, dimensions={0} | all-to-all | bytes 655360 | tf_op jit(solution)/shard_map/all_to_all | solution.py:408
  48.8 0.0 collective-permute-start.1
  48.8 0.0 copy-done
  48.8 0.0 copy-done.10
  48.8 0.0 copy-done.11
  48.8 2.6 %expand.1 = (f32[16,1024,128]{2,1,0:T(8,128)S(1)}, bf16[32,40,128]{2,1,0:T(8,128)(2,1)S(1)}) custom-call(bf16[32,40,128]{2,1,0:T(8,128)(2,1)S(1)} %get-tuple-element.20.own, bf16[32,40,128]{2,1,0:T(8,128)(2,1)S(1)} %all_to_all.21.got.rest_1_, f32[1,512]{1,0:T(1,128)S(1)} %bitcast.12, f32[1,512]{1,0:T(1,128)S(1)} %bitcast.13, f32[4,1224,128]{2,1,0:T(8,128)S(1)} %bitcast.7, ...), custom_call_target="tpu_custom_call" | custom-call | tf_op jit(solution)/shard_map/expand/pallas_call | solution.py:498
  51.4 0.0 collective-permute-done.1.rest_4_
  51.4 14.3 %all_to_all.22.got.rest_2_ = bf16[32,40,128]{2,1,0:T(8,128)(2,1)S(1)} all-to-all(bf16[32,40,128]{2,1,0:T(8,128)(2,1)S(1)} %get-tuple-element.23), channel_id=1, replica_groups=mesh['dp'=8,'bn'=4] {'dp','bn'}, dimensions={0} | all-to-all | bytes 655360 | tf_op jit(solution)/shard_map/all_to_all | solution.py:408
  65.7 0.0 collective-permute-start.2
  65.7 0.0 copy-done.2
  65.7 0.0 copy-done.4
  65.7 0.0 copy-done.5
  65.7 0.0 copy-done.6
  65.7 0.0 copy-done.7
  65.8 5.1 %keys.1 = (bf16[8,128]{1,0:T(8,128)(2,1)}, bf16[32,8,128]{2,1,0:T(8,128)(2,1)S(1)}) custom-call(bf16[32,40,128]{2,1,0:T(8,128)(2,1)S(1)} %get-tuple-element.17.own.own_numbers, bf16[32,40,128]{2,1,0:T(8,128)(2,1)S(1)} %all_to_all.20.got.numbers.rest_0_, bf16[32,40,128]{2,1,0:T(8,128)(2,1)S(1)} %all_to_all.22.got.rest_2_, f32[1,2048]{1,0:T(1,128)S(1)} %bitcast.8, ...), custom_call_target="tpu_custom_call" | custom-call | tf_op jit(solution)/shard_map/keys/pallas_call | solution.py:516
  70.8 0.0 collective-permute-done.2.rest_5_
  70.8 9.7 %all_to_all.23.grads = bf16[32,8,128]{2,1,0:T(8,128)(2,1)S(1)} all-to-all(bf16[32,8,128]{2,1,0:T(8,128)(2,1)S(1)} %get-tuple-element.28), channel_id=1, replica_groups=mesh['dp'=8,'bn'=4] {'dp','bn'}, dimensions={0} | all-to-all | bytes 131072 | tf_op jit(solution)/shard_map/all_to_all | solution.py:408
  80.5 1.3 %query_grad.1 = f32[2048,128]{1,0:T(8,128)} custom-call(bf16[32,8,128]{2,1,0:T(8,128)(2,1)S(1)} %all_to_all.23.grads, bf16[32,40,128]{2,1,0:T(8,128)(2,1)S(1)} %all_to_all.20.got.numbers.rest_0_, bf16[32,40,128]{2,1,0:T(8,128)(2,1)S(1)} %all_to_all.21.got.rest_1_, bf16[32,40,128]{2,1,0:T(8,128)(2,1)S(1)} %all_to_all.22.got.rest_2_, ...), custom_call_target="tpu_custom_call" | custom-call | tf_op jit(solution)/shard_map/query_grad/pallas_call | solution.py:545
Async XLA Ops:
  0.6 29.5 %copy-start.3 = (bf16[8,2048]{1,0:T(8,128)(2,1)S(1)}, bf16[8,2048]{1,0:T(8,128)(2,1)}, u32[]{:S(2)}) copy-start(bf16[8,2048]{1,0:T(8,128)(2,1)} %query_feats.5) | copy-start | bytes 98308
  0.6 29.5 %copy-start.8 = (f32[512]{0:T(512)S(1)}, f32[512]{0:T(512)}, u32[]{:S(2)}) copy-start(f32[512]{0:T(512)} %param.23) | copy-start | bytes 6148
  0.7 29.5 %copy-start.9 = (f32[512]{0:T(512)S(1)}, f32[512]{0:T(512)}, u32[]{:S(2)}) copy-start(f32[512]{0:T(512)} %param.24) | copy-start | bytes 6148
  0.7 29.5 %copy-start.1 = (bf16[9,512,512]{2,1,0:T(8,128)(2,1)S(1)}, bf16[9,512,512]{2,1,0:T(8,128)(2,1)}, u32[]{:S(2)}) copy-start(bf16[9,512,512]{2,1,0:T(8,128)(2,1)} %weights.5) | copy-start | bytes 14155780
  11.0 37.8 %copy-start = (bf16[512,2048]{1,0:T(8,128)(2,1)S(1)}, bf16[512,2048]{1,0:T(8,128)(2,1)}, u32[]{:S(2)}) copy-start(bf16[512,2048]{1,0:T(8,128)(2,1)} %weights.7) | copy-start | bytes 6291460
  11.0 37.8 %copy-start.10 = (f32[512]{0:T(512)S(1)}, f32[512]{0:T(512)}, u32[]{:S(2)}) copy-start(f32[512]{0:T(512)} %param.25) | copy-start | bytes 6148
  11.0 37.7 %copy-start.11 = (f32[512]{0:T(512)S(1)}, f32[512]{0:T(512)}, u32[]{:S(2)}) copy-start(f32[512]{0:T(512)} %param.26) | copy-start | bytes 6148
  30.1 4.3 %collective-permute-start = (bf16[32,40,128]{2,1,0:T(8,128)(2,1)S(1)}, bf16[32,40,128]{2,1,0:T(8,128)(2,1)S(1)}, u32[]{:S(2)}, u32[]{:S(2)}) collective-permute-start(bf16[32,40,128]{2,1,0:T(8,128)(2,1)S(1)} %all_to_all.20.got.numbers.rest_0_), channel_id=1, source_target_pairs={{0,1},{1,0},{2,3},{3,2},{4,5},{5,4},{6,7},{7,6},{8,9},{9,8},{10,11... | collective-permute-start | bytes 983048 | tf_op jit(solution)/shard_map/ppermute | solution.py:404
  34.4 31.3 %copy-start.2 = (bf16[16384,128]{1,0:T(8,128)(2,1)S(1)}, bf16[16384,128]{1,0:T(8,128)(2,1)}, u32[]{:S(2)}) copy-start(bf16[16384,128]{1,0:T(8,128)(2,1)} %queue.1) | copy-start | bytes 12582916
  34.4 31.3 %copy-start.4 = (bf16[2048,128]{1,0:T(8,128)(2,1)S(1)}, bf16[2048,128]{1,0:T(8,128)(2,1)}, u32[]{:S(2)}) copy-start(bf16[2048,128]{1,0:T(8,128)(2,1)} %w_key.1) | copy-start | bytes 1572868
  34.4 31.3 %copy-start.5 = (bf16[2048,128]{1,0:T(8,128)(2,1)S(1)}, bf16[2048,128]{1,0:T(8,128)(2,1)}, u32[]{:S(2)}) copy-start(bf16[2048,128]{1,0:T(8,128)(2,1)} %w_query.1) | copy-start | bytes 1572868
  34.4 31.3 %copy-start.6 = (f32[2048]{0:T(1024)S(1)}, f32[2048]{0:T(1024)}, u32[]{:S(2)}) copy-start(f32[2048]{0:T(1024)} %param.27) | copy-start | bytes 24580
  34.4 31.3 %copy-start.7 = (f32[2048]{0:T(1024)S(1)}, f32[2048]{0:T(1024)}, u32[]{:S(2)}) copy-start(f32[2048]{0:T(1024)} %param.28) | copy-start | bytes 24580
  48.8 2.6 %collective-permute-start.1 = (bf16[32,40,128]{2,1,0:T(8,128)(2,1)S(1)}, bf16[32,40,128]{2,1,0:T(8,128)(2,1)S(1)}, u32[]{:S(2)}, u32[]{:S(2)}) collective-permute-start(bf16[32,40,128]{2,1,0:T(8,128)(2,1)S(1)} %all_to_all.21.got.rest_1_), channel_id=1, source_target_pairs={{0,1},{1,0},{2,3},{3,2},{4,5},{5,4},{6,7},{7,6},{8,9},{9,8},{10,11... | collective-permute-start | bytes 983048 | tf_op jit(solution)/shard_map/ppermute | solution.py:404
  65.7 5.1 %collective-permute-start.2 = (bf16[32,40,128]{2,1,0:T(8,128)(2,1)S(1)}, bf16[32,40,128]{2,1,0:T(8,128)(2,1)S(1)}, u32[]{:S(2)}, u32[]{:S(2)}) collective-permute-start(bf16[32,40,128]{2,1,0:T(8,128)(2,1)S(1)} %all_to_all.22.got.rest_2_), channel_id=1, source_target_pairs={{0,1},{1,0},{2,3},{3,2},{4,5},{5,4},{6,7},{7,6},{8,9},{9,8},{10,11... | collective-permute-start | bytes 983048 | tf_op jit(solution)/shard_map/ppermute | solution.py:404

commit v6 on v5

--- a/solution.py
+++ b/solution.py
@@ -296,7 +296,7 @@
     step = queue.shape[0] // clips
 
     def queue_products(i):
-        entries = queue[pl.ds(i * step, step), :]
+        entries = queue[i * step : (i + 1) * step, :]
         return lax.dot_general(
             both,
             jnp.concatenate([entries, entries * entries], axis=1),
@@ -326,39 +326,33 @@
     scale = gain[...] * lax.rsqrt(within + between + EPSILON)
     bias = shift[...] - mean * scale
 
-    def one_step(n, carry):
-        negatives, pulled = carry
-        inverse = lax.rsqrt(products[clips:] + 1e-06)
-        weight = jnp.exp(products[:clips] * inverse / SHARPNESS_DIVISOR)
+    negatives = jnp.zeros((clips, 1), jnp.float32)
+    pulled = jnp.zeros((clips, emb), jnp.float32)
+    length_of_clip = FRAMES * SPOTS
+    for n in range(clips):
+        current = products[...]
+        if n + 1 < clips:
+            products[...] = queue_products(n + 1)
+        inverse = lax.rsqrt(current[clips:] + 1e-06)
+        weight = jnp.exp(current[:clips] * inverse / SHARPNESS_DIVISOR)
         negatives = negatives + jnp.sum(weight, axis=-1, keepdims=True)
         pulled = pulled + jnp.dot(
             (weight * inverse).astype(jnp.bfloat16),
-            queue[pl.ds(n * step, step), :],
+            queue[n * step : (n + 1) * step, :],
             preferred_element_type=jnp.float32,
         )
-        products[...] = queue_products(jnp.minimum(n + 1, clips - 1))
-        total = jnp.zeros((SPOTS, channels), jnp.float32)
-        for t in range(FRAMES):
-            values = jnp.concatenate(
-                [
-                    third[j, pl.ds((n * FRAMES + t) * SPOTS, SPOTS), :]
-                    for j in range(wide)
-                ],
-                axis=1,
+        for j in range(wide):
+            lanes = slice(j * LANES, (j + 1) * LANES)
+            chosen = frames[n, 1 : FRAMES + 1, :, lanes].reshape(length_of_clip, LANES)
+            merged = jnp.maximum(
+                third[j, n * length_of_clip : (n + 1) * length_of_clip, :] * scale[:, lanes]
+                + bias[:, lanes]
+                + chosen.astype(jnp.float32),
+                0.0,
             )
-            total = total + jnp.maximum(
-                values * scale + bias + frames[n, t + 1].astype(jnp.float32), 0.0
+            pooled[n : n + 1, lanes] = (
+                jnp.sum(merged, axis=0, keepdims=True) / length_of_clip
             )
-        pooled[pl.ds(n, 1), :] = jnp.sum(total, axis=0, keepdims=True) / (FRAMES * SPOTS)
-        return negatives, pulled
-
-    negatives, pulled = lax.fori_loop(
-        0,
-        clips,
-        one_step,
-        (jnp.zeros((clips, 1), jnp.float32), jnp.zeros((clips, emb), jnp.float32)),
-        unroll=clips,
-    )
     projected = jnp.dot(
         pooled[...].astype(jnp.bfloat16), w_key[...], preferred_element_type=jnp.float32
     )

time: 82.2 us -> 81.3 us (0.989)
  Pallas kernels: 23.5 us -> 22.6 us
    pallas_call x1, Pallas kernels: 5.07 us -> 4.17 us  [local(): pl.pallas_call(functools.partial(keys_kernel, lax.axis_size('bn')), out_s...]
where the time goes in v6:
time: 81.3 us; the launch traced here: 81.1 us
  blocking collectives  57.4 us (71%)
  Pallas kernels  22.6 us (28%)
  between operations  0.99 us (1%)
    all_to_all x4, blocking collectives, exchange(): return lax.all_to_all(message, ('dp', 'bn'), 0, 0)  57.4 us
    pallas_call x1, Pallas kernels, local(): pl.pallas_call(functools.partial(time_conv_kernel, cuts, shares[0]), out_...  10.3 us
    pallas_call x1, Pallas kernels, local(): pl.pallas_call(functools.partial(space_conv_kernel, shares[1]), out_shape...  4.22 us
    pallas_call x1, Pallas kernels, local(): pl.pallas_call(functools.partial(keys_kernel, lax.axis_size('bn')), out_s...  4.17 us
    pallas_call x1, Pallas kernels, local(): pl.pallas_call(functools.partial(expand_kernel, shares[2]), out_shape=(ja...  2.58 us
  transfers between devices with their start and end apart: 3, of which 0 were waited for; matrix products, arithmetic and copies ran while one was open for 0% of the time, Pallas kernels for 14%

profile of v6, /device:TPU:0, one launch (start us, length us, event | category | flops | bytes accessed | tf_op | source)
XLA Modules:
  0.0 81.1 jit_solution(3804470462302795950)
XLA Ops:
  0.6 0.0 copy-start.3
  0.6 0.0 copy-start.8
  0.7 0.0 copy-start.9
  0.7 0.0 copy-start.1
  0.7 10.3 %time_conv.1 = (f32[4,1040,128]{2,1,0:T(8,128)S(1)}, bf16[8,10,16,2048]{3,2,1,0:T(8,128)(2,1)S(1)}, bf16[32,40,128]{2,1,0:T(8,128)(2,1)S(1)}) custom-call(s32[8]{0:T(128)} %starts_hbm.1, s32[1,8]{1,0:T(1,128)} %shuffle_hbm.1, bf16[8,12,16,2048]{3,2,1,0:T(8,128)(2,1)} %feats.1, bf16[3,2048,512]{2,1,0:T(8,128)(2,1)} %weights.4, bf16[8,2048]{1,0:T(8,128)(2,1)} %query_feats.5), custom_call_target="tpu_custom_call" | custom-call | tf_op jit(solution)/shard_map/time_conv/pallas_call | solution.py:440
  11.0 0.0 copy-start
  11.0 0.0 copy-start.10
  11.0 0.0 copy-start.11
  11.1 19.1 %all_to_all.20.got.numbers.rest_0_ = bf16[32,40,128]{2,1,0:T(8,128)(2,1)S(1)} all-to-all(bf16[32,40,128]{2,1,0:T(8,128)(2,1)S(1)} %get-tuple-element.17.own.own_numbers), channel_id=1, replica_groups=mesh['dp'=8,'bn'=4] {'dp','bn'}, dimensions={0} | all-to-all | bytes 655360 | tf_op jit(solution)/shard_map/all_to_all | solution.py:402
  30.1 0.0 collective-permute-start
  30.1 0.0 copy-done.3
  30.1 0.0 copy-done.8
  30.2 0.0 copy-done.9
  30.2 0.0 copy-done.1
  30.2 4.2 %space_conv.1 = (f32[4,17,72,128]{3,2,1,0:T(8,128)S(1)}, bf16[32,40,128]{2,1,0:T(8,128)(2,1)S(1)}) custom-call(bf16[32,40,128]{2,1,0:T(8,128)(2,1)S(1)} %get-tuple-element.17.own.own_numbers, bf16[32,40,128]{2,1,0:T(8,128)(2,1)S(1)} %all_to_all.20.got.numbers.rest_0_, f32[1,512]{1,0:T(1,128)S(1)} %bitcast.10, f32[1,512]{1,0:T(1,128)S(1)} %bitcast.11, ...), custom_call_target="tpu_custom_call" | custom-call | tf_op jit(solution)/shard_map/space_conv/pallas_call | solution.py:472
  34.4 0.0 copy-start.2
  34.4 0.0 copy-start.4
  34.4 0.0 copy-start.5
  34.4 0.0 copy-start.6
  34.4 0.0 copy-start.7
  34.5 0.0 collective-permute-done.rest_3_
  34.5 14.3 %all_to_all.21.got.rest_1_ = bf16[32,40,128]{2,1,0:T(8,128)(2,1)S(1)} all-to-all(bf16[32,40,128]{2,1,0:T(8,128)(2,1)S(1)} %get-tuple-element.20.own), channel_id=1, replica_groups=mesh['dp'=8,'bn'=4] {'dp','bn'}, dimensions={0} | all-to-all | bytes 655360 | tf_op jit(solution)/shard_map/all_to_all | solution.py:402
  48.8 0.0 collective-permute-start.1
  48.8 0.0 copy-done
  48.8 0.0 copy-done.10
  48.8 0.0 copy-done.11
  48.8 2.6 %expand.1 = (f32[16,1024,128]{2,1,0:T(8,128)S(1)}, bf16[32,40,128]{2,1,0:T(8,128)(2,1)S(1)}) custom-call(bf16[32,40,128]{2,1,0:T(8,128)(2,1)S(1)} %get-tuple-element.20.own, bf16[32,40,128]{2,1,0:T(8,128)(2,1)S(1)} %all_to_all.21.got.rest_1_, f32[1,512]{1,0:T(1,128)S(1)} %bitcast.12, f32[1,512]{1,0:T(1,128)S(1)} %bitcast.13, f32[4,1224,128]{2,1,0:T(8,128)S(1)} %bitcast.7, ...), custom_call_target="tpu_custom_call" | custom-call | tf_op jit(solution)/shard_map/expand/pallas_call | solution.py:492
  51.4 0.0 collective-permute-done.1.rest_4_
  51.4 14.3 %all_to_all.22.got.rest_2_ = bf16[32,40,128]{2,1,0:T(8,128)(2,1)S(1)} all-to-all(bf16[32,40,128]{2,1,0:T(8,128)(2,1)S(1)} %get-tuple-element.23), channel_id=1, replica_groups=mesh['dp'=8,'bn'=4] {'dp','bn'}, dimensions={0} | all-to-all | bytes 655360 | tf_op jit(solution)/shard_map/all_to_all | solution.py:402
  65.7 0.0 collective-permute-start.2
  65.7 0.0 copy-done.2
  65.7 0.0 copy-done.4
  65.7 0.0 copy-done.5
  65.7 0.0 copy-done.6
  65.7 0.0 copy-done.7
  65.8 4.2 %keys.1 = (bf16[8,128]{1,0:T(8,128)(2,1)}, bf16[32,8,128]{2,1,0:T(8,128)(2,1)S(1)}) custom-call(bf16[32,40,128]{2,1,0:T(8,128)(2,1)S(1)} %get-tuple-element.17.own.own_numbers, bf16[32,40,128]{2,1,0:T(8,128)(2,1)S(1)} %all_to_all.20.got.numbers.rest_0_, bf16[32,40,128]{2,1,0:T(8,128)(2,1)S(1)} %all_to_all.22.got.rest_2_, f32[1,2048]{1,0:T(1,128)S(1)} %bitcast.8, ...), custom_call_target="tpu_custom_call" | custom-call | tf_op jit(solution)/shard_map/keys/pallas_call | solution.py:510
  69.9 0.0 collective-permute-done.2.rest_5_
  69.9 9.7 %all_to_all.23.grads = bf16[32,8,128]{2,1,0:T(8,128)(2,1)S(1)} all-to-all(bf16[32,8,128]{2,1,0:T(8,128)(2,1)S(1)} %get-tuple-element.28), channel_id=1, replica_groups=mesh['dp'=8,'bn'=4] {'dp','bn'}, dimensions={0} | all-to-all | bytes 131072 | tf_op jit(solution)/shard_map/all_to_all | solution.py:402
  79.7 1.3 %query_grad.1 = f32[2048,128]{1,0:T(8,128)} custom-call(bf16[32,8,128]{2,1,0:T(8,128)(2,1)S(1)} %all_to_all.23.grads, bf16[32,40,128]{2,1,0:T(8,128)(2,1)S(1)} %all_to_all.20.got.numbers.rest_0_, bf16[32,40,128]{2,1,0:T(8,128)(2,1)S(1)} %all_to_all.21.got.rest_1_, bf16[32,40,128]{2,1,0:T(8,128)(2,1)S(1)} %all_to_all.22.got.rest_2_, ...), custom_call_target="tpu_custom_call" | custom-call | tf_op jit(solution)/shard_map/query_grad/pallas_call | solution.py:539
Async XLA Ops:
  0.6 29.5 %copy-start.3 = (bf16[8,2048]{1,0:T(8,128)(2,1)S(1)}, bf16[8,2048]{1,0:T(8,128)(2,1)}, u32[]{:S(2)}) copy-start(bf16[8,2048]{1,0:T(8,128)(2,1)} %query_feats.5) | copy-start | bytes 98308
  0.6 29.5 %copy-start.8 = (f32[512]{0:T(512)S(1)}, f32[512]{0:T(512)}, u32[]{:S(2)}) copy-start(f32[512]{0:T(512)} %param.23) | copy-start | bytes 6148
  0.7 29.5 %copy-start.9 = (f32[512]{0:T(512)S(1)}, f32[512]{0:T(512)}, u32[]{:S(2)}) copy-start(f32[512]{0:T(512)} %param.24) | copy-start | bytes 6148
  0.7 29.5 %copy-start.1 = (bf16[9,512,512]{2,1,0:T(8,128)(2,1)S(1)}, bf16[9,512,512]{2,1,0:T(8,128)(2,1)}, u32[]{:S(2)}) copy-start(bf16[9,512,512]{2,1,0:T(8,128)(2,1)} %weights.5) | copy-start | bytes 14155780
  11.0 37.8 %copy-start = (bf16[512,2048]{1,0:T(8,128)(2,1)S(1)}, bf16[512,2048]{1,0:T(8,128)(2,1)}, u32[]{:S(2)}) copy-start(bf16[512,2048]{1,0:T(8,128)(2,1)} %weights.7) | copy-start | bytes 6291460
  11.0 37.8 %copy-start.10 = (f32[512]{0:T(512)S(1)}, f32[512]{0:T(512)}, u32[]{:S(2)}) copy-start(f32[512]{0:T(512)} %param.25) | copy-start | bytes 6148
  11.0 37.7 %copy-start.11 = (f32[512]{0:T(512)S(1)}, f32[512]{0:T(512)}, u32[]{:S(2)}) copy-start(f32[512]{0:T(512)} %param.26) | copy-start | bytes 6148
  30.1 4.3 %collective-permute-start = (bf16[32,40,128]{2,1,0:T(8,128)(2,1)S(1)}, bf16[32,40,128]{2,1,0:T(8,128)(2,1)S(1)}, u32[]{:S(2)}, u32[]{:S(2)}) collective-permute-start(bf16[32,40,128]{2,1,0:T(8,128)(2,1)S(1)} %all_to_all.20.got.numbers.rest_0_), channel_id=1, source_target_pairs={{0,1},{1,0},{2,3},{3,2},{4,5},{5,4},{6,7},{7,6},{8,9},{9,8},{10,11... | collective-permute-start | bytes 983048 | tf_op jit(solution)/shard_map/ppermute | solution.py:398
  34.4 31.3 %copy-start.2 = (bf16[16384,128]{1,0:T(8,128)(2,1)S(1)}, bf16[16384,128]{1,0:T(8,128)(2,1)}, u32[]{:S(2)}) copy-start(bf16[16384,128]{1,0:T(8,128)(2,1)} %queue.1) | copy-start | bytes 12582916
  34.4 31.3 %copy-start.4 = (bf16[2048,128]{1,0:T(8,128)(2,1)S(1)}, bf16[2048,128]{1,0:T(8,128)(2,1)}, u32[]{:S(2)}) copy-start(bf16[2048,128]{1,0:T(8,128)(2,1)} %w_key.1) | copy-start | bytes 1572868
  34.4 31.3 %copy-start.5 = (bf16[2048,128]{1,0:T(8,128)(2,1)S(1)}, bf16[2048,128]{1,0:T(8,128)(2,1)}, u32[]{:S(2)}) copy-start(bf16[2048,128]{1,0:T(8,128)(2,1)} %w_query.1) | copy-start | bytes 1572868
  34.4 31.3 %copy-start.6 = (f32[2048]{0:T(1024)S(1)}, f32[2048]{0:T(1024)}, u32[]{:S(2)}) copy-start(f32[2048]{0:T(1024)} %param.27) | copy-start | bytes 24580
  34.4 31.3 %copy-start.7 = (f32[2048]{0:T(1024)S(1)}, f32[2048]{0:T(1024)}, u32[]{:S(2)}) copy-start(f32[2048]{0:T(1024)} %param.28) | copy-start | bytes 24580
  48.8 2.6 %collective-permute-start.1 = (bf16[32,40,128]{2,1,0:T(8,128)(2,1)S(1)}, bf16[32,40,128]{2,1,0:T(8,128)(2,1)S(1)}, u32[]{:S(2)}, u32[]{:S(2)}) collective-permute-start(bf16[32,40,128]{2,1,0:T(8,128)(2,1)S(1)} %all_to_all.21.got.rest_1_), channel_id=1, source_target_pairs={{0,1},{1,0},{2,3},{3,2},{4,5},{5,4},{6,7},{7,6},{8,9},{9,8},{10,11... | collective-permute-start | bytes 983048 | tf_op jit(solution)/shard_map/ppermute | solution.py:398
  65.7 4.2 %collective-permute-start.2 = (bf16[32,40,128]{2,1,0:T(8,128)(2,1)S(1)}, bf16[32,40,128]{2,1,0:T(8,128)(2,1)S(1)}, u32[]{:S(2)}, u32[]{:S(2)}) collective-permute-start(bf16[32,40,128]{2,1,0:T(8,128)(2,1)S(1)} %all_to_all.22.got.rest_2_), channel_id=1, source_target_pairs={{0,1},{1,0},{2,3},{3,2},{4,5},{5,4},{6,7},{7,6},{8,9},{9,8},{10,11... | collective-permute-start | bytes 983048 | tf_op jit(solution)/shard_map/ppermute | solution.py:398

commit v7 on v6

--- a/solution.py
+++ b/solution.py
@@ -199,7 +199,8 @@
                 axis=1,
             )
             act[r, c] = jnp.maximum(values * scale + bias, 0.0).astype(jnp.bfloat16)
-    for k in (4, 0, 1, 2, 3, 5, 6, 7, 8):
+    taken[0:1] = jnp.zeros((1,) + taken.shape[1:], jnp.float32)
+    for k in (1, 0, 2, 3, 5, 6, 7, 8, 4):
         down, right = k // 3 - 1, k % 3 - 1
         r0, r1 = max(0, -down), min(SIDE, SIDE - down)
         c0, c1 = max(0, -right), min(SIDE, SIDE - right)
@@ -209,15 +210,15 @@
             weights[k],
             preferred_element_type=jnp.float32,
         ).reshape(r1 - r0, c1 - c0, rows, inner)
-        if k == 4:
-            taken[...] = product
-        else:
+        if k == 1:
+            taken[r0:r1, c0:c1] = product
+        elif k != 4:
             taken[r0:r1, c0:c1] += product
     total = jnp.zeros((1, inner), jnp.float32)
     squares = jnp.zeros((1, inner), jnp.float32)
     for r in range(SIDE):
         for c in range(SIDE):
-            values = taken[r, c]
+            values = taken[r, c] + product[r, c]
             for j in range(part):
                 second[j, r * SIDE + c, 0:rows] = values[:, j * LANES : (j + 1) * LANES]
             total = total + jnp.sum(values, axis=0, keepdims=True)

time: 81.3 us -> 81.2 us (level)
  transfers between devices with their start and end apart: 3 -> 3, of which waited for: 0 -> 0; matrix products, arithmetic and copies ran while one was open for 0% -> 0% of each run, Pallas kernels for 14% -> 13%
where the time goes in v7:
time: 81.2 us; the launch traced here: 81 us
  blocking collectives  57.5 us (71%)
  Pallas kernels  22.5 us (28%)
  between operations  0.99 us (1%)
    all_to_all x4, blocking collectives, exchange(): return lax.all_to_all(message, ('dp', 'bn'), 0, 0)  57.5 us
    pallas_call x1, Pallas kernels, local(): pl.pallas_call(functools.partial(time_conv_kernel, cuts, shares[0]), out_...  10.3 us
    pallas_call x1, Pallas kernels, local(): pl.pallas_call(functools.partial(keys_kernel, lax.axis_size('bn')), out_s...  4.17 us
    pallas_call x1, Pallas kernels, local(): pl.pallas_call(functools.partial(space_conv_kernel, shares[1]), out_shape...  4.08 us
    pallas_call x1, Pallas kernels, local(): pl.pallas_call(functools.partial(expand_kernel, shares[2]), out_shape=(ja...  2.58 us
  transfers between devices with their start and end apart: 3, of which 0 were waited for; matrix products, arithmetic and copies ran while one was open for 0% of the time, Pallas kernels for 13%

profile of v7, /device:TPU:0, one launch (start us, length us, event | category | flops | bytes accessed | tf_op | source)
XLA Modules:
  0.0 81.0 jit_solution(4802824131407103851)
XLA Ops:
  0.6 0.0 copy-start.3
  0.6 0.0 copy-start.8
  0.7 0.0 copy-start.9
  0.7 0.0 copy-start.1
  0.7 10.3 %time_conv.1 = (f32[4,1040,128]{2,1,0:T(8,128)S(1)}, bf16[8,10,16,2048]{3,2,1,0:T(8,128)(2,1)S(1)}, bf16[32,40,128]{2,1,0:T(8,128)(2,1)S(1)}) custom-call(s32[8]{0:T(128)} %starts_hbm.1, s32[1,8]{1,0:T(1,128)} %shuffle_hbm.1, bf16[8,12,16,2048]{3,2,1,0:T(8,128)(2,1)} %feats.1, bf16[3,2048,512]{2,1,0:T(8,128)(2,1)} %weights.4, bf16[8,2048]{1,0:T(8,128)(2,1)} %query_feats.5), custom_call_target="tpu_custom_call" | custom-call | tf_op jit(solution)/shard_map/time_conv/pallas_call | solution.py:441
  11.0 0.0 copy-start
  11.0 0.0 copy-start.10
  11.0 0.0 copy-start.11
  11.1 19.1 %all_to_all.20.got.numbers.rest_0_ = bf16[32,40,128]{2,1,0:T(8,128)(2,1)S(1)} all-to-all(bf16[32,40,128]{2,1,0:T(8,128)(2,1)S(1)} %get-tuple-element.17.own.own_numbers), channel_id=1, replica_groups=mesh['dp'=8,'bn'=4] {'dp','bn'}, dimensions={0} | all-to-all | bytes 655360 | tf_op jit(solution)/shard_map/all_to_all | solution.py:403
  30.1 0.0 collective-permute-start
  30.1 0.0 copy-done.3
  30.1 0.0 copy-done.8
  30.2 0.0 copy-done.9
  30.2 0.0 copy-done.1
  30.2 4.1 %space_conv.1 = (f32[4,17,72,128]{3,2,1,0:T(8,128)S(1)}, bf16[32,40,128]{2,1,0:T(8,128)(2,1)S(1)}) custom-call(bf16[32,40,128]{2,1,0:T(8,128)(2,1)S(1)} %get-tuple-element.17.own.own_numbers, bf16[32,40,128]{2,1,0:T(8,128)(2,1)S(1)} %all_to_all.20.got.numbers.rest_0_, f32[1,512]{1,0:T(1,128)S(1)} %bitcast.10, f32[1,512]{1,0:T(1,128)S(1)} %bitcast.11, ...), custom_call_target="tpu_custom_call" | custom-call | tf_op jit(solution)/shard_map/space_conv/pallas_call | solution.py:473
  34.3 0.0 copy-start.2
  34.3 0.0 copy-start.4
  34.3 0.0 copy-start.5
  34.3 0.0 copy-start.6
  34.3 0.0 copy-start.7
  34.3 0.0 collective-permute-done.rest_3_
  34.3 14.3 %all_to_all.21.got.rest_1_ = bf16[32,40,128]{2,1,0:T(8,128)(2,1)S(1)} all-to-all(bf16[32,40,128]{2,1,0:T(8,128)(2,1)S(1)} %get-tuple-element.20.own), channel_id=1, replica_groups=mesh['dp'=8,'bn'=4] {'dp','bn'}, dimensions={0} | all-to-all | bytes 655360 | tf_op jit(solution)/shard_map/all_to_all | solution.py:403
  48.7 0.0 collective-permute-start.1
  48.7 0.0 copy-done
  48.7 0.0 copy-done.10
  48.7 0.0 copy-done.11
  48.7 2.6 %expand.1 = (f32[16,1024,128]{2,1,0:T(8,128)S(1)}, bf16[32,40,128]{2,1,0:T(8,128)(2,1)S(1)}) custom-call(bf16[32,40,128]{2,1,0:T(8,128)(2,1)S(1)} %get-tuple-element.20.own, bf16[32,40,128]{2,1,0:T(8,128)(2,1)S(1)} %all_to_all.21.got.rest_1_, f32[1,512]{1,0:T(1,128)S(1)} %bitcast.12, f32[1,512]{1,0:T(1,128)S(1)} %bitcast.13, f32[4,1224,128]{2,1,0:T(8,128)S(1)} %bitcast.7, ...), custom_call_target="tpu_custom_call" | custom-call | tf_op jit(solution)/shard_map/expand/pallas_call | solution.py:493
  51.3 0.0 collective-permute-done.1.rest_4_
  51.3 14.3 %all_to_all.22.got.rest_2_ = bf16[32,40,128]{2,1,0:T(8,128)(2,1)S(1)} all-to-all(bf16[32,40,128]{2,1,0:T(8,128)(2,1)S(1)} %get-tuple-element.23), channel_id=1, replica_groups=mesh['dp'=8,'bn'=4] {'dp','bn'}, dimensions={0} | all-to-all | bytes 655360 | tf_op jit(solution)/shard_map/all_to_all | solution.py:403
  65.6 0.0 collective-permute-start.2
  65.6 0.0 copy-done.2
  65.6 0.0 copy-done.4
  65.6 0.0 copy-done.5
  65.6 0.0 copy-done.6
  65.6 0.0 copy-done.7
  65.6 4.2 %keys.1 = (bf16[8,128]{1,0:T(8,128)(2,1)}, bf16[32,8,128]{2,1,0:T(8,128)(2,1)S(1)}) custom-call(bf16[32,40,128]{2,1,0:T(8,128)(2,1)S(1)} %get-tuple-element.17.own.own_numbers, bf16[32,40,128]{2,1,0:T(8,128)(2,1)S(1)} %all_to_all.20.got.numbers.rest_0_, bf16[32,40,128]{2,1,0:T(8,128)(2,1)S(1)} %all_to_all.22.got.rest_2_, f32[1,2048]{1,0:T(1,128)S(1)} %bitcast.8, ...), custom_call_target="tpu_custom_call" | custom-call | tf_op jit(solution)/shard_map/keys/pallas_call | solution.py:511
  69.8 0.0 collective-permute-done.2.rest_5_
  69.8 9.7 %all_to_all.23.grads = bf16[32,8,128]{2,1,0:T(8,128)(2,1)S(1)} all-to-all(bf16[32,8,128]{2,1,0:T(8,128)(2,1)S(1)} %get-tuple-element.28), channel_id=1, replica_groups=mesh['dp'=8,'bn'=4] {'dp','bn'}, dimensions={0} | all-to-all | bytes 131072 | tf_op jit(solution)/shard_map/all_to_all | solution.py:403
  79.5 1.3 %query_grad.1 = f32[2048,128]{1,0:T(8,128)} custom-call(bf16[32,8,128]{2,1,0:T(8,128)(2,1)S(1)} %all_to_all.23.grads, bf16[32,40,128]{2,1,0:T(8,128)(2,1)S(1)} %all_to_all.20.got.numbers.rest_0_, bf16[32,40,128]{2,1,0:T(8,128)(2,1)S(1)} %all_to_all.21.got.rest_1_, bf16[32,40,128]{2,1,0:T(8,128)(2,1)S(1)} %all_to_all.22.got.rest_2_, ...), custom_call_target="tpu_custom_call" | custom-call | tf_op jit(solution)/shard_map/query_grad/pallas_call | solution.py:540
Async XLA Ops:
  0.6 29.5 %copy-start.3 = (bf16[8,2048]{1,0:T(8,128)(2,1)S(1)}, bf16[8,2048]{1,0:T(8,128)(2,1)}, u32[]{:S(2)}) copy-start(bf16[8,2048]{1,0:T(8,128)(2,1)} %query_feats.5) | copy-start | bytes 98308
  0.6 29.5 %copy-start.8 = (f32[512]{0:T(512)S(1)}, f32[512]{0:T(512)}, u32[]{:S(2)}) copy-start(f32[512]{0:T(512)} %param.23) | copy-start | bytes 6148
  0.7 29.5 %copy-start.9 = (f32[512]{0:T(512)S(1)}, f32[512]{0:T(512)}, u32[]{:S(2)}) copy-start(f32[512]{0:T(512)} %param.24) | copy-start | bytes 6148
  0.7 29.5 %copy-start.1 = (bf16[9,512,512]{2,1,0:T(8,128)(2,1)S(1)}, bf16[9,512,512]{2,1,0:T(8,128)(2,1)}, u32[]{:S(2)}) copy-start(bf16[9,512,512]{2,1,0:T(8,128)(2,1)} %weights.5) | copy-start | bytes 14155780
  11.0 37.6 %copy-start = (bf16[512,2048]{1,0:T(8,128)(2,1)S(1)}, bf16[512,2048]{1,0:T(8,128)(2,1)}, u32[]{:S(2)}) copy-start(bf16[512,2048]{1,0:T(8,128)(2,1)} %weights.7) | copy-start | bytes 6291460
  11.0 37.6 %copy-start.10 = (f32[512]{0:T(512)S(1)}, f32[512]{0:T(512)}, u32[]{:S(2)}) copy-start(f32[512]{0:T(512)} %param.25) | copy-start | bytes 6148
  11.0 37.6 %copy-start.11 = (f32[512]{0:T(512)S(1)}, f32[512]{0:T(512)}, u32[]{:S(2)}) copy-start(f32[512]{0:T(512)} %param.26) | copy-start | bytes 6148
  30.1 4.2 %collective-permute-start = (bf16[32,40,128]{2,1,0:T(8,128)(2,1)S(1)}, bf16[32,40,128]{2,1,0:T(8,128)(2,1)S(1)}, u32[]{:S(2)}, u32[]{:S(2)}) collective-permute-start(bf16[32,40,128]{2,1,0:T(8,128)(2,1)S(1)} %all_to_all.20.got.numbers.rest_0_), channel_id=1, source_target_pairs={{0,1},{1,0},{2,3},{3,2},{4,5},{5,4},{6,7},{7,6},{8,9},{9,8},{10,11... | collective-permute-start | bytes 983048 | tf_op jit(solution)/shard_map/ppermute | solution.py:399
  34.3 31.3 %copy-start.2 = (bf16[16384,128]{1,0:T(8,128)(2,1)S(1)}, bf16[16384,128]{1,0:T(8,128)(2,1)}, u32[]{:S(2)}) copy-start(bf16[16384,128]{1,0:T(8,128)(2,1)} %queue.1) | copy-start | bytes 12582916
  34.3 31.3 %copy-start.4 = (bf16[2048,128]{1,0:T(8,128)(2,1)S(1)}, bf16[2048,128]{1,0:T(8,128)(2,1)}, u32[]{:S(2)}) copy-start(bf16[2048,128]{1,0:T(8,128)(2,1)} %w_key.1) | copy-start | bytes 1572868
  34.3 31.3 %copy-start.5 = (bf16[2048,128]{1,0:T(8,128)(2,1)S(1)}, bf16[2048,128]{1,0:T(8,128)(2,1)}, u32[]{:S(2)}) copy-start(bf16[2048,128]{1,0:T(8,128)(2,1)} %w_query.1) | copy-start | bytes 1572868
  34.3 31.3 %copy-start.6 = (f32[2048]{0:T(1024)S(1)}, f32[2048]{0:T(1024)}, u32[]{:S(2)}) copy-start(f32[2048]{0:T(1024)} %param.27) | copy-start | bytes 24580
  34.3 31.3 %copy-start.7 = (f32[2048]{0:T(1024)S(1)}, f32[2048]{0:T(1024)}, u32[]{:S(2)}) copy-start(f32[2048]{0:T(1024)} %param.28) | copy-start | bytes 24580
  48.7 2.6 %collective-permute-start.1 = (bf16[32,40,128]{2,1,0:T(8,128)(2,1)S(1)}, bf16[32,40,128]{2,1,0:T(8,128)(2,1)S(1)}, u32[]{:S(2)}, u32[]{:S(2)}) collective-permute-start(bf16[32,40,128]{2,1,0:T(8,128)(2,1)S(1)} %all_to_all.21.got.rest_1_), channel_id=1, source_target_pairs={{0,1},{1,0},{2,3},{3,2},{4,5},{5,4},{6,7},{7,6},{8,9},{9,8},{10,11... | collective-permute-start | bytes 983048 | tf_op jit(solution)/shard_map/ppermute | solution.py:399
  65.6 4.2 %collective-permute-start.2 = (bf16[32,40,128]{2,1,0:T(8,128)(2,1)S(1)}, bf16[32,40,128]{2,1,0:T(8,128)(2,1)S(1)}, u32[]{:S(2)}, u32[]{:S(2)}) collective-permute-start(bf16[32,40,128]{2,1,0:T(8,128)(2,1)S(1)} %all_to_all.22.got.rest_2_), channel_id=1, source_target_pairs={{0,1},{1,0},{2,3},{3,2},{4,5},{5,4},{6,7},{7,6},{8,9},{9,8},{10,11... | collective-permute-start | bytes 983048 | tf_op jit(solution)/shard_map/ppermute | solution.py:399
